TPU v7x, 256 devices: a whole 4x4x8 slice. The times are simulated.
256 devices in a mesh: segment: 8 (over x, core), slab: 32 (over y, z).
Axes of the slice: x: 4, y: 4, z: 8, core: 2. Of those that a mesh axis runs over, the one named last changes fastest.
Arguments:
- fwd_input: bfloat16 [8, 192, 64, 128], P('segment', None, 'slab'), may hold values from -90 to 90
- fwd_skip: bfloat16 [8, 192, 64, 128], P('segment', None, 'slab'), may hold values from -6 to 6
- bwd_input: bfloat16 [8, 192, 64, 128], P('segment', None, 'slab'), may hold values from -90 to 90
- bwd_skip: bfloat16 [8, 192, 64, 128], P('segment', None, 'slab'), may hold values from -6 to 6
- out_cot: bfloat16 [8, 192, 64, 128], P('segment', None, 'slab'), may hold values from -6 to 6
- skip_cot: bfloat16 [8, 192, 64, 128], P('segment', None, 'slab'), may hold values from -6 to 6
- kernel: bfloat16 [8, 192, 5184], P('segment'), may hold values from -0.078125 to 0.078125
- norm_gain: float32 [8, 192], P('segment'), may hold values from 0.1 to 1.9
- norm_shift: float32 [8, 192], P('segment'), may hold values from -0.5 to 0.5
- head_weight: bfloat16 [192, 105], replicated, may hold values from -2.8867513 to 2.8867513
- labels: int32 [64, 128], P('slab'), may hold values from 0 to 104
Outputs:
- next_input: bfloat16 [8, 192, 64, 128], P('segment', None, 'slab')
- next_cot: bfloat16 [8, 192, 64, 128], P('segment', None, 'slab')
- skip_store: bfloat16 [8, 192, 64, 128], P('segment', None, 'slab')
- kernel_grad: float32 [8, 192, 5184], P('segment', 'slab')
- gain_grad: float32 [8, 192], P('segment')
- shift_grad: float32 [8, 192], P('segment')
All inputs are finite; a program needn't handle non-finite values.
Results may differ from a plain program's by a relative error of at most 0.038.
Values may be sent and summed in bfloat16 or wider, within the bound.
No kernel may reach another device: no remote copies, remote signals or barrier semaphores. Data moves between devices by JAX's collectives and lax.ppermute only.
A program may use at most 64 MiB of HBM per device.

v0:
```python
import jax
import jax.numpy as jnp
from jax import lax
from jax.sharding import PartitionSpec as P

ROWS = 8
COLS = 16


epsilon = 1e-05
leak_slope = 0.01


def padded_2(block, sides, width):
    for axis, dim in sides:
        count = lax.axis_size(axis)
        forward = [(i, i + 1) for i in range(count - 1)]
        backward = [(target, source) for source, target in forward]
        low = lax.ppermute(
            lax.slice_in_dim(block, block.shape[dim] - width, None, axis=dim), axis, forward
        )
        high = lax.ppermute(lax.slice_in_dim(block, 0, width, axis=dim), axis, backward)
        block = jnp.concatenate([low, block, high], axis=dim)
    return block


def from_behind(block, axis, distance):
    devices = range(lax.axis_size(axis))
    route = [((i - distance) % len(devices), i) for i in devices]
    return lax.ppermute(block, axis, route)


def depth_rim(values):
    grid = values.reshape(values.shape[0], values.shape[1], ROWS, COLS)
    extended = padded_2(grid, (("slab", 1),), 1)
    return jnp.pad(extended, ((0, 0), (0, 0), (1, 1), (1, 1)))


def tap_views(padded, planes, mirror):
    tap_list = []
    for plane_off in range(3):
        for row_off in range(3):
            for col_off in range(3):
                if mirror:
                    offsets = (2 - plane_off, 2 - row_off, 2 - col_off)
                else:
                    offsets = (plane_off, row_off, col_off)
                window = padded[
                    :,
                    offsets[0] : offsets[0] + planes,
                    offsets[1] : offsets[1] + ROWS,
                    offsets[2] : offsets[2] + COLS,
                ]
                tap_list.append(window.reshape(padded.shape[0], planes * ROWS * COLS))
    return tap_list


def convolve(tap_list, kernel_mat):
    channels = kernel_mat.shape[0]
    summed = jnp.zeros((channels, tap_list[0].shape[1]), jnp.float32)
    for tap_index in range(27):
        weight = kernel_mat[:, tap_index * channels : (tap_index + 1) * channels]
        summed = summed + lax.dot_general(
            weight,
            tap_list[tap_index],
            (((0,), (0,)), ((), ())),
            preferred_element_type=jnp.float32,
        )
    return summed


def convolve_back(tap_list, kernel_mat):
    channels = kernel_mat.shape[0]
    summed = jnp.zeros((channels, tap_list[0].shape[1]), jnp.float32)
    for tap_index in range(27):
        weight = kernel_mat[:, tap_index * channels : (tap_index + 1) * channels]
        summed = summed + jnp.dot(weight, tap_list[tap_index], preferred_element_type=jnp.float32)
    return summed


def kernel_rows(tap_list, grad_z):
    blocks = []
    for tap_index in range(27):
        part_rows = tap_list[tap_index]
        blocks.append(
            lax.dot_general(
                part_rows, grad_z, (((1,), (1,)), ((), ())), preferred_element_type=jnp.float32
            )
        )
    return jnp.concatenate(blocks, axis=1)


def norm_stats(conv_out, total_cells):
    first_sum = lax.psum(jnp.sum(conv_out, axis=1), "slab")
    center = first_sum / total_cells
    square_sum = lax.psum(jnp.sum(jnp.square(conv_out - center[:, None]), axis=1), "slab")
    spread = square_sum / total_cells
    return (center, spread)


def section_forward(joined, kernel_mat, gain_vec, shift_vec, total_cells):
    tap_list = tap_views(depth_rim(joined), joined.shape[1], False)
    conv_out = convolve(tap_list, kernel_mat)
    center, spread = norm_stats(conv_out, total_cells)
    inv_std = lax.rsqrt(spread + epsilon)
    normed = (conv_out - center[:, None]) * inv_std[:, None]
    scaled = normed * gain_vec[:, None] + shift_vec[:, None]
    activated = jnp.where(scaled > 0, scaled, leak_slope * scaled)
    output = (joined.reshape(conv_out.shape).astype(jnp.float32) + activated).astype(jnp.bfloat16)
    return (output, tap_list, normed, scaled, inv_std)


def per_device(
    fwd_input,
    fwd_skip,
    bwd_input,
    bwd_skip,
    out_cot,
    skip_cot,
    kernel,
    norm_gain,
    norm_shift,
    head_weight,
    labels,
):
    segments = lax.axis_size("segment")
    slabs = lax.axis_size("slab")
    segment_id = lax.axis_index("segment")
    is_decoder = segment_id * 2 >= segments
    is_last = segment_id == segments - 1
    channels = kernel.shape[1]
    planes = fwd_input.shape[2]
    total_cells = float(planes * slabs * ROWS * COLS)
    kernel_mat = kernel[0]
    gain_vec = norm_gain[0]
    shift_vec = norm_shift[0]
    joined_fwd = jnp.where(
        is_decoder,
        (fwd_input[0].astype(jnp.float32) + fwd_skip[0].astype(jnp.float32)).astype(jnp.bfloat16),
        fwd_input[0],
    )
    joined_bwd = jnp.where(
        is_decoder,
        (bwd_input[0].astype(jnp.float32) + bwd_skip[0].astype(jnp.float32)).astype(jnp.bfloat16),
        bwd_input[0],
    )
    fwd_out = section_forward(joined_fwd, kernel_mat, gain_vec, shift_vec, total_cells)[0]
    bwd_out, tap_list, normed, scaled, inv_std = section_forward(
        joined_bwd, kernel_mat, gain_vec, shift_vec, total_cells
    )
    logits = lax.dot_general(
        head_weight, bwd_out, (((0,), (0,)), ((), ())), preferred_element_type=jnp.float32
    )
    class_prob = jax.nn.softmax(logits, axis=0)
    one_hot = (
        jnp.arange(head_weight.shape[1], dtype=jnp.int32)[:, None] == labels.reshape(1, -1)
    ).astype(jnp.float32)
    head_delta = (class_prob - one_hot).astype(jnp.bfloat16)
    head_cot = jnp.dot(head_weight, head_delta, preferred_element_type=jnp.float32)
    cot_plain = out_cot[0].reshape(channels, -1).astype(jnp.float32)
    skip_plain = skip_cot[0].reshape(channels, -1).astype(jnp.float32)
    upstream = jnp.where(is_last, head_cot, cot_plain) + jnp.where(
        is_decoder, jnp.zeros_like(skip_plain), skip_plain
    )
    grad_act = upstream * jnp.where(scaled > 0, 1.0, leak_slope)
    sum_grad, sum_cross = lax.psum(
        (jnp.sum(grad_act, axis=1), jnp.sum(grad_act * normed, axis=1)), "slab"
    )
    grad_z = (
        gain_vec[:, None]
        * inv_std[:, None]
        * (grad_act - sum_grad[:, None] / total_cells - normed * sum_cross[:, None] / total_cells)
    ).astype(jnp.bfloat16)
    kernel_part = lax.psum_scatter(
        kernel_rows(tap_list, grad_z).astype(jnp.bfloat16), "slab", scatter_dimension=0, tiled=True
    ).astype(jnp.float32)
    back_taps = tap_views(depth_rim(grad_z.reshape(channels, planes, ROWS * COLS)), planes, True)
    grad_joined = (upstream + convolve_back(back_taps, kernel_mat)).astype(jnp.bfloat16)
    next_block = from_behind(fwd_out, "segment", 1)
    prev_block = from_behind(grad_joined, "segment", -1)
    outgoing = jnp.where(is_decoder, grad_joined, fwd_out)
    groups = outgoing.reshape(segments, channels // segments, -1)
    scattered = lax.all_to_all(groups, "segment", split_axis=0, concat_axis=0, tiled=True)
    reversed_groups = scattered[::-1]
    outgoing = lax.all_to_all(
        reversed_groups, "segment", split_axis=0, concat_axis=0, tiled=True
    ).reshape(channels, -1)
    scale_out = total_cells ** (-0.5)
    next_input = next_block.reshape(1, channels, planes, -1)
    next_cot = prev_block.reshape(1, channels, planes, -1)
    skip_store = outgoing.reshape(1, channels, planes, -1)
    return (
        next_input,
        next_cot,
        skip_store,
        (kernel_part * scale_out)[None],
        (sum_cross * scale_out)[None],
        (sum_grad * scale_out)[None],
    )


def solution(mesh):
    in_specs = (
        P("segment", None, "slab", None),
        P("segment", None, "slab", None),
        P("segment", None, "slab", None),
        P("segment", None, "slab", None),
        P("segment", None, "slab", None),
        P("segment", None, "slab", None),
        P("segment", None, None),
        P("segment", None),
        P("segment", None),
        P(),
        P("slab", None),
    )
    out_specs = (
        P("segment", None, "slab", None),
        P("segment", None, "slab", None),
        P("segment", None, "slab", None),
        P("segment", "slab", None),
        P("segment", None),
        P("segment", None),
    )
    return jax.shard_map(
        per_device, mesh=mesh, in_specs=in_specs, out_specs=out_specs, check_vma=False
    )
```

profile of v0, /device:TPU:6, one launch (start us, length us, event | category | flops | bytes accessed | tf_op | source)
XLA Modules:
  0.0 468.4 jit_solution(9786626081574530358)
XLA Ops:
  7.2 0.9 copy_convert_fusion.1
  8.3 0.9 copy_convert_fusion
  9.4 1.0 copy.44
  10.4 1.0 copy.48
  11.5 3.8 collective-permute-start.3
  15.4 1.3 collective-permute-start.4
  16.7 4.5 collective-permute-start
  21.3 1.3 collective-permute-start.1
  23.0 0.8 convert_select_fusion
  23.8 0.8 convert.140
  25.4 2.0 collective-permute-done.1
  28.0 0.9 fusion.164
  29.0 1.6 fusion.163
  30.6 0.9 copy-done.1
  39.3 77.1 %psum.44 = f32[192]{0:T(256)S(1)} all-reduce(f32[192]{0:T(256)S(1)} %get-tuple-element.136), channel_id=1, replica_groups=mesh['segment'=8,'slab'=32] {'slab'}, use_global_device_ids=true, to_apply=%region_5.6 | all-reduce | flops 192 | bytes 1536 | tf_op jit(solution)/shard_map/psum | solution.py:94
  116.4 1.2 fusion.149
  117.6 1.2 fusion.131
  118.8 1.1 convolution_bitcast_fusion.26
  120.0 1.2 convolution_bitcast_fusion.27
  121.2 1.1 convolution_bitcast_fusion.28
  122.3 1.2 convolution_bitcast_fusion.29
  123.8 1.2 convolution_add_fusion.41
  125.0 1.2 convolution_add_fusion.40
  131.9 69.6 %all-reduce.5 = (f32[192]{0:T(256)S(1)}, f32[192]{0:T(256)S(1)}) all-reduce(f32[192]{0:T(256)S(1)} %get-tuple-element.134, f32[192]{0:T(256)S(1)} %multiply_reduce_fusion.1), channel_id=1, replica_groups=mesh['segment'=8,'slab'=32] {'slab'}, use_global_device_ids=true, to_apply=%region_1.2 | all-reduce | flops 384 | bytes 3072 | tf_op jit(solution)/shard_map/psum | solution.py:94
  202.2 2.0 fusion.158
  204.2 71.7 %all-reduce.4 = (f32[192]{0:T(256)S(1)}, f32[192]{0:T(256)S(1)}, f32[192]{0:T(256)S(1)}) all-reduce(f32[192]{0:T(256)S(1)} %multiply_reduce_fusion.2, f32[192]{0:T(256)S(1)} %get-tuple-element.37, f32[192]{0:T(256)S(1)} %get-tuple-element.36), channel_id=1, replica_groups=mesh['segment'=8,'slab'=32] {'slab'}, use_global_device_ids=true, to_apply=%region_3.4 | all-reduce | flops 576 | bytes 4608 | tf_op jit(solution)/shard_map/psum | solution.py:96
  276.4 1.2 multiply_convert_fusion
  277.6 1.8 convolution_convert_fusion
  279.4 1.7 convolution_convert_fusion.1
  281.1 1.7 convolution_convert_fusion.10
  282.9 1.8 convolution_convert_fusion.11
  284.6 1.8 convolution_convert_fusion.12
  286.5 1.8 convolution_convert_fusion.14
  288.3 1.8 convolution_convert_fusion.15
  290.0 1.8 convolution_convert_fusion.16
  291.8 1.7 convolution_convert_fusion.17
  293.6 1.7 convolution_convert_fusion.18
  295.3 0.8 convolution_convert_fusion.19
  296.2 0.9 convolution_convert_fusion.2
  297.0 0.9 convolution_convert_fusion.20
  297.9 0.9 convolution_convert_fusion.3
  298.7 0.8 convolution_convert_fusion.5
  299.6 0.9 convolution_convert_fusion.6
  300.4 0.9 convolution_convert_fusion.7
  301.3 0.9 convolution_convert_fusion.8
  302.2 0.9 convolution_convert_fusion.9
  303.0 0.8 convolution_convert_fusion.21
  303.9 0.9 convolution_convert_fusion.23
  304.7 0.9 convolution_convert_fusion.24
  306.3 0.9 convolution_convert_fusion.4
  307.5 4.6 concatenate.40
  312.1 1.9 collective-permute-start.5
  314.0 1.3 collective-permute-start.6
  315.9 5.1 %collective-permute-done.6 = bf16[192,1,8,16]{0,3,2,1:T(8,128)(2,1)S(1)} collective-permute-done((bf16[192,1,8,16]{0,3,2,1:T(8,128)(2,1)S(1)}, bf16[192,1,8,16]{0,3,2,1:T(8,128)(2,1)S(1)}, u32[]{:S(2)}, u32[]{:S(2)}) %collective-permute-start.6) | collective-permute-done | bytes 49184 | tf_op jit(solution)/shard_map/ppermute | solution.py:22
  327.6 0.9 broadcast_select_fusion
  328.5 4.8 %all-to-all-start = ((bf16[8,24,256]{2,1,0:T(8,128)(2,1)}), bf16[8,24,256]{2,1,0:T(8,128)(2,1)S(1)}, u32[]{:S(2)}, u32[]{:S(2)}) async-start(bf16[8,24,256]{2,1,0:T(8,128)(2,1)} %bitcast.122), calls=%async_computation | async-start | bytes 196608 | tf_op jit(solution)/shard_map/all_to_all | solution.py:183
  334.6 1.6 collective-permute-start.7
  336.2 0.7 all-to-all-done
  337.6 5.4 %all-to-all-start.1 = ((bf16[8,24,256]{2,1,0:T(8,128)(2,1)}), bf16[8,24,256]{2,1,0:T(8,128)(2,1)S(1)}, u32[]{:S(2)}, u32[]{:S(2)}) async-start(bf16[8,24,256]{2,1,0:T(8,128)(2,1)} %rev.3), calls=%async_computation.1 | async-start | bytes 196608 | tf_op jit(solution)/shard_map/all_to_all | solution.py:185
  344.3 0.7 reshape.384
  344.9 1.8 all-to-all-done.1
  347.4 112.4 %all-reduce.8.cloned.1.call-done = bf16[192,5184]{1,0:T(8,128)(2,1)} async-done(((bf16[192,5184]{1,0:T(8,128)(2,1)}), bf16[192,5184]{1,0:T(8,128)(2,1)}) %all-reduce.8.cloned.1.call-update) | async-done | bytes 1990672
  459.8 0.9 multiply_bitcast_fusion
  460.8 0.8 copy.51
  (254 shorter events, 27.6 us)
Async XLA Ops:
  7.2 194.4 %copy-start = (bf16[192,105]{1,0:T(8,128)(2,1)S(1)}, bf16[192,105]{1,0:T(8,128)(2,1)}, u32[]{:S(2)}) copy-start(bf16[192,105]{1,0:T(8,128)(2,1)} %param.20) | copy-start | bytes 120964
  7.2 452.6 %all-reduce.8.cloned.1.call-start = ((), (), s32[]{:S(2)}) async-start(), calls=%async_computation.2 | async-start | bytes 4030464
  8.1 14.7 %copy-start.51 = (bf16[1,192,2,128]{3,2,1,0:T(2,128)(2,1)S(1)}, bf16[1,192,2,128]{3,2,1,0:T(2,128)(2,1)}, u32[]{:S(2)}) copy-start(bf16[1,192,2,128]{3,2,1,0:T(2,128)(2,1)} %param.11) | copy-start | bytes 294916
  8.2 14.7 %copy-start.52 = (bf16[1,192,2,128]{3,2,1,0:T(2,128)(2,1)S(1)}, bf16[1,192,2,128]{3,2,1,0:T(2,128)(2,1)}, u32[]{:S(2)}) copy-start(bf16[1,192,2,128]{3,2,1,0:T(2,128)(2,1)} %param.13) | copy-start | bytes 294916
  9.2 13.7 %copy-start.62 = (bf16[1,192,2,128]{3,2,1,0:T(2,128)(2,1)S(1)}, bf16[1,192,2,128]{3,2,1,0:T(2,128)(2,1)}, u32[]{:S(2)}) copy-start(bf16[1,192,2,128]{3,2,1,0:T(2,128)(2,1)} %param.16) | copy-start | bytes 294916
  9.4 14.4 %copy-start.63 = (bf16[1,192,2,128]{3,2,1,0:T(2,128)(2,1)S(1)}, bf16[1,192,2,128]{3,2,1,0:T(2,128)(2,1)}, u32[]{:S(2)}) copy-start(bf16[1,192,2,128]{3,2,1,0:T(2,128)(2,1)} %param.15) | copy-start | bytes 294916
  11.5 13.0 %collective-permute-start.3 = (bf16[192,1,8,16]{0,3,2,1:T(8,128)(2,1)S(1)}, bf16[192,1,8,16]{0,3,2,1:T(8,128)(2,1)S(1)}, u32[]{:S(2)}, u32[]{:S(2)}) collective-permute-start(bf16[192,1,8,16]{0,3,2,1:T(8,128)(2,1)S(1)} %get-tuple-element.128), channel_id=1, source_target_pairs={{0,1},{1,2},{2,3},{3,4},{4,5},{5,6},{6,7},{7,8},{8,9},{9,10},{10,1... | collective-permute-start | bytes 147464 | tf_op jit(solution)/shard_map/ppermute | solution.py:19
  15.4 9.1 %collective-permute-start.4 = (bf16[192,1,8,16]{0,3,2,1:T(8,128)(2,1)S(1)}, bf16[192,1,8,16]{0,3,2,1:T(8,128)(2,1)S(1)}, u32[]{:S(2)}, u32[]{:S(2)}) collective-permute-start(bf16[192,1,8,16]{0,3,2,1:T(8,128)(2,1)S(1)} %get-tuple-element.129), channel_id=1, source_target_pairs={{1,0},{2,1},{3,2},{4,3},{5,4},{6,5},{7,6},{8,7},{9,8},{10,9},{11,1... | collective-permute-start | bytes 147464 | tf_op jit(solution)/shard_map/ppermute | solution.py:22
  16.7 8.7 %collective-permute-start = (bf16[192,1,8,16]{0,3,2,1:T(8,128)(2,1)S(1)}, bf16[192,1,8,16]{0,3,2,1:T(8,128)(2,1)S(1)}, u32[]{:S(2)}, u32[]{:S(2)}) collective-permute-start(bf16[192,1,8,16]{0,3,2,1:T(8,128)(2,1)S(1)} %get-tuple-element.124), channel_id=1, source_target_pairs={{0,1},{1,2},{2,3},{3,4},{4,5},{5,6},{6,7},{7,8},{8,9},{9,10},{10,1... | collective-permute-start | bytes 147464 | tf_op jit(solution)/shard_map/ppermute | solution.py:19
  21.3 6.2 %collective-permute-start.1 = (bf16[192,1,8,16]{0,3,2,1:T(8,128)(2,1)S(1)}, bf16[192,1,8,16]{0,3,2,1:T(8,128)(2,1)S(1)}, u32[]{:S(2)}, u32[]{:S(2)}) collective-permute-start(bf16[192,1,8,16]{0,3,2,1:T(8,128)(2,1)S(1)} %get-tuple-element.125), channel_id=1, source_target_pairs={{1,0},{2,1},{3,2},{4,3},{5,4},{6,5},{7,6},{8,7},{9,8},{10,9},{11,1... | collective-permute-start | bytes 147464 | tf_op jit(solution)/shard_map/ppermute | solution.py:22
  23.0 13.4 %copy-start.32 = (bf16[192,256]{1,0:T(8,128)(2,1)}, bf16[192,256]{1,0:T(8,128)(2,1)S(1)}, u32[]{:S(2)}) copy-start(bf16[192,256]{1,0:T(8,128)(2,1)S(1)} %get-tuple-element.145) | copy-start | bytes 294916
  23.0 105.9 %copy-start.30 = (bf16[192,256]{1,0:T(8,128)(2,1)}, bf16[192,256]{1,0:T(8,128)(2,1)S(1)}, u32[]{:S(2)}) copy-start(bf16[192,256]{1,0:T(8,128)(2,1)S(1)} %get-tuple-element.144) | copy-start | bytes 294916
  25.2 6.8 %copy-start.23 = (bf16[192,2,8,16]{0,3,2,1:T(8,128)(2,1)}, bf16[192,2,8,16]{0,3,2,1:T(8,128)(2,1)S(1)}, u32[]{:S(2)}) copy-start(bf16[192,2,8,16]{0,3,2,1:T(8,128)(2,1)S(1)} %get-tuple-element.99) | copy-start | bytes 294916
  25.2 7.1 %copy-start.21 = (bf16[192,2,8,16]{0,3,2,1:T(8,128)(2,1)}, bf16[192,2,8,16]{0,3,2,1:T(8,128)(2,1)S(1)}, u32[]{:S(2)}) copy-start(bf16[192,2,8,16]{0,3,2,1:T(8,128)(2,1)S(1)} %get-tuple-element.100) | copy-start | bytes 294916
  25.2 7.4 %copy-start.19 = (bf16[192,2,8,16]{0,3,2,1:T(8,128)(2,1)}, bf16[192,2,8,16]{0,3,2,1:T(8,128)(2,1)S(1)}, u32[]{:S(2)}) copy-start(bf16[192,2,8,16]{0,3,2,1:T(8,128)(2,1)S(1)} %get-tuple-element.101) | copy-start | bytes 294916
  25.2 7.7 %copy-start.15 = (bf16[192,2,8,16]{0,3,2,1:T(8,128)(2,1)}, bf16[192,2,8,16]{0,3,2,1:T(8,128)(2,1)S(1)}, u32[]{:S(2)}) copy-start(bf16[192,2,8,16]{0,3,2,1:T(8,128)(2,1)S(1)} %get-tuple-element.102) | copy-start | bytes 294916
  25.2 9.7 %copy-start.4 = (bf16[192,2,8,16]{0,3,2,1:T(8,128)(2,1)}, bf16[192,2,8,16]{0,3,2,1:T(8,128)(2,1)S(1)}, u32[]{:S(2)}) copy-start(bf16[192,2,8,16]{0,3,2,1:T(8,128)(2,1)S(1)} %get-tuple-element.110) | copy-start | bytes 294916
  25.2 10.0 %copy-start.5 = (bf16[192,2,8,16]{0,3,2,1:T(8,128)(2,1)}, bf16[192,2,8,16]{0,3,2,1:T(8,128)(2,1)S(1)}, u32[]{:S(2)}) copy-start(bf16[192,2,8,16]{0,3,2,1:T(8,128)(2,1)S(1)} %get-tuple-element.109) | copy-start | bytes 294916
  25.2 10.3 %copy-start.6 = (bf16[192,2,8,16]{0,3,2,1:T(8,128)(2,1)}, bf16[192,2,8,16]{0,3,2,1:T(8,128)(2,1)S(1)}, u32[]{:S(2)}) copy-start(bf16[192,2,8,16]{0,3,2,1:T(8,128)(2,1)S(1)} %get-tuple-element.108) | copy-start | bytes 294916
  25.2 10.5 %copy-start.7 = (bf16[192,2,8,16]{0,3,2,1:T(8,128)(2,1)}, bf16[192,2,8,16]{0,3,2,1:T(8,128)(2,1)S(1)}, u32[]{:S(2)}) copy-start(bf16[192,2,8,16]{0,3,2,1:T(8,128)(2,1)S(1)} %get-tuple-element.107) | copy-start | bytes 294916
  25.2 10.8 %copy-start.8 = (bf16[192,2,8,16]{0,3,2,1:T(8,128)(2,1)}, bf16[192,2,8,16]{0,3,2,1:T(8,128)(2,1)S(1)}, u32[]{:S(2)}) copy-start(bf16[192,2,8,16]{0,3,2,1:T(8,128)(2,1)S(1)} %get-tuple-element.106) | copy-start | bytes 294916
  25.2 11.4 %copy-start.9 = (bf16[192,2,8,16]{0,3,2,1:T(8,128)(2,1)}, bf16[192,2,8,16]{0,3,2,1:T(8,128)(2,1)S(1)}, u32[]{:S(2)}) copy-start(bf16[192,2,8,16]{0,3,2,1:T(8,128)(2,1)S(1)} %get-tuple-element.105) | copy-start | bytes 294916
  25.2 11.7 %copy-start.10 = (bf16[192,2,8,16]{0,3,2,1:T(8,128)(2,1)}, bf16[192,2,8,16]{0,3,2,1:T(8,128)(2,1)S(1)}, u32[]{:S(2)}) copy-start(bf16[192,2,8,16]{0,3,2,1:T(8,128)(2,1)S(1)} %get-tuple-element.104) | copy-start | bytes 294916
  25.3 12.0 %copy-start.29 = (bf16[192,2,8,16]{0,3,2,1:T(8,128)(2,1)}, bf16[192,2,8,16]{0,3,2,1:T(8,128)(2,1)S(1)}, u32[]{:S(2)}) copy-start(bf16[192,2,8,16]{0,3,2,1:T(8,128)(2,1)S(1)} %get-tuple-element.103) | copy-start | bytes 294916
  25.3 13.1 %copy-start.2 = (bf16[192,2,8,16]{0,3,2,1:T(8,128)(2,1)}, bf16[192,2,8,16]{0,3,2,1:T(8,128)(2,1)S(1)}, u32[]{:S(2)}) copy-start(bf16[192,2,8,16]{0,3,2,1:T(8,128)(2,1)S(1)} %get-tuple-element.96) | copy-start | bytes 294916
  25.3 13.4 %copy-start.11 = (bf16[192,2,8,16]{0,3,2,1:T(8,128)(2,1)}, bf16[192,2,8,16]{0,3,2,1:T(8,128)(2,1)S(1)}, u32[]{:S(2)}) copy-start(bf16[192,2,8,16]{0,3,2,1:T(8,128)(2,1)S(1)} %get-tuple-element.95) | copy-start | bytes 294916
  25.3 13.7 %copy-start.12 = (bf16[192,2,8,16]{0,3,2,1:T(8,128)(2,1)}, bf16[192,2,8,16]{0,3,2,1:T(8,128)(2,1)S(1)}, u32[]{:S(2)}) copy-start(bf16[192,2,8,16]{0,3,2,1:T(8,128)(2,1)S(1)} %get-tuple-element.94) | copy-start | bytes 294916
  25.4 5.2 %copy-start.13 = (bf16[192,2,8,16]{0,3,2,1:T(8,128)(2,1)}, bf16[192,2,8,16]{0,3,2,1:T(8,128)(2,1)S(1)}, u32[]{:S(2)}) copy-start(bf16[192,2,8,16]{0,3,2,1:T(8,128)(2,1)S(1)} %get-tuple-element.117) | copy-start | bytes 294916
  25.4 6.3 %copy-start.17 = (bf16[192,2,8,16]{0,3,2,1:T(8,128)(2,1)}, bf16[192,2,8,16]{0,3,2,1:T(8,128)(2,1)S(1)}, u32[]{:S(2)}) copy-start(bf16[192,2,8,16]{0,3,2,1:T(8,128)(2,1)S(1)} %get-tuple-element.114) | copy-start | bytes 294916
  29.0 2.5 copy-start.1
  31.7 2.3 copy-start.58
  31.7 2.3 copy-start.60
  34.1 2.0 copy-start.27
  34.1 3.7 copy-start.25
  116.4 9.8 %copy-start.49 = (bf16[192,2,8,16]{0,3,2,1:T(8,128)(2,1)S(1)}, bf16[192,2,8,16]{0,3,2,1:T(8,128)(2,1)}, u32[]{:S(2)}) copy-start(bf16[192,2,8,16]{0,3,2,1:T(8,128)(2,1)} %get-tuple-element.89) | copy-start | bytes 294916
  117.6 8.9 %copy-start.56 = (bf16[192,1,8,16]{0,3,2,1:T(8,128)(2,1)S(1)}, bf16[192,1,8,16]{0,3,2,1:T(8,128)(2,1)}, u32[]{:S(2)}) copy-start(bf16[192,1,8,16]{0,3,2,1:T(8,128)(2,1)} %copy-done.55) | copy-start | bytes 147460
  122.3 4.5 copy-start.48
  123.6 3.5 copy-start.47
  125.0 2.5 copy-start.46
  127.7 1.8 copy-start.40
  128.0 1.8 copy-start.50
  130.1 71.5 %copy-start.64 = (f32[1,192]{1,0:T(1,128)S(1)}, f32[1,192]{1,0:T(1,128)}, u32[]{:S(2)}) copy-start(f32[1,192]{1,0:T(1,128)} %param.18) | copy-start | bytes 2308
  130.1 71.5 %copy-start.33 = (bf16[192,256]{1,0:T(8,128)(2,1)S(1)}, bf16[192,256]{1,0:T(8,128)(2,1)}, u32[]{:S(2)}) copy-start(bf16[192,256]{1,0:T(8,128)(2,1)} %copy-done.32) | copy-start | bytes 294916
  130.1 71.5 %copy-start.65 = (f32[1,192]{1,0:T(1,128)S(1)}, f32[1,192]{1,0:T(1,128)}, u32[]{:S(2)}) copy-start(f32[1,192]{1,0:T(1,128)} %param.19) | copy-start | bytes 2308
  130.4 71.8 %copy-start.66 = (s32[2,128]{1,0:T(2,128)S(1)}, s32[2,128]{1,0:T(2,128)}, u32[]{:S(2)}) copy-start(s32[2,128]{1,0:T(2,128)} %param.21) | copy-start | bytes 3076
  276.4 19.7 %copy-start.3 = (bf16[192,2,8,16]{0,3,2,1:T(8,128)(2,1)S(1)}, bf16[192,2,8,16]{0,3,2,1:T(8,128)(2,1)}, u32[]{:S(2)}) copy-start(bf16[192,2,8,16]{0,3,2,1:T(8,128)(2,1)} %copy-done.2) | copy-start | bytes 294916
  282.9 16.7 %copy-start.24 = (bf16[192,2,8,16]{0,3,2,1:T(8,128)(2,1)S(1)}, bf16[192,2,8,16]{0,3,2,1:T(8,128)(2,1)}, u32[]{:S(2)}) copy-start(bf16[192,2,8,16]{0,3,2,1:T(8,128)(2,1)} %copy-done.23) | copy-start | bytes 294916
  284.6 15.8 %copy-start.22 = (bf16[192,2,8,16]{0,3,2,1:T(8,128)(2,1)S(1)}, bf16[192,2,8,16]{0,3,2,1:T(8,128)(2,1)}, u32[]{:S(2)}) copy-start(bf16[192,2,8,16]{0,3,2,1:T(8,128)(2,1)} %copy-done.21) | copy-start | bytes 294916
  286.5 14.9 %copy-start.20 = (bf16[192,2,8,16]{0,3,2,1:T(8,128)(2,1)S(1)}, bf16[192,2,8,16]{0,3,2,1:T(8,128)(2,1)}, u32[]{:S(2)}) copy-start(bf16[192,2,8,16]{0,3,2,1:T(8,128)(2,1)} %copy-done.19) | copy-start | bytes 294916
  288.2 13.9 %copy-start.16 = (bf16[192,2,8,16]{0,3,2,1:T(8,128)(2,1)S(1)}, bf16[192,2,8,16]{0,3,2,1:T(8,128)(2,1)}, u32[]{:S(2)}) copy-start(bf16[192,2,8,16]{0,3,2,1:T(8,128)(2,1)} %copy-done.15) | copy-start | bytes 294916
  290.0 13.0 %copy-start.18 = (bf16[192,2,8,16]{0,3,2,1:T(8,128)(2,1)S(1)}, bf16[192,2,8,16]{0,3,2,1:T(8,128)(2,1)}, u32[]{:S(2)}) copy-start(bf16[192,2,8,16]{0,3,2,1:T(8,128)(2,1)} %copy-done.17) | copy-start | bytes 294916
  296.2 9.6 %copy-start.14 = (bf16[192,2,8,16]{0,3,2,1:T(8,128)(2,1)S(1)}, bf16[192,2,8,16]{0,3,2,1:T(8,128)(2,1)}, u32[]{:S(2)}) copy-start(bf16[192,2,8,16]{0,3,2,1:T(8,128)(2,1)} %copy-done.13) | copy-start | bytes 294916
  297.0 9.0 %copy-start.28 = (bf16[192,2,8,16]{0,3,2,1:T(8,128)(2,1)S(1)}, bf16[192,2,8,16]{0,3,2,1:T(8,128)(2,1)}, u32[]{:S(2)}) copy-start(bf16[192,2,8,16]{0,3,2,1:T(8,128)(2,1)} %copy-done.27) | copy-start | bytes 294916
  297.9 8.4 %copy-start.26 = (bf16[192,2,8,16]{0,3,2,1:T(8,128)(2,1)S(1)}, bf16[192,2,8,16]{0,3,2,1:T(8,128)(2,1)}, u32[]{:S(2)}) copy-start(bf16[192,2,8,16]{0,3,2,1:T(8,128)(2,1)} %copy-done.25) | copy-start | bytes 294916
  298.7 8.4 %copy-start.34 = (bf16[192,256]{1,0:T(8,128)(2,1)S(1)}, bf16[192,256]{1,0:T(8,128)(2,1)}, u32[]{:S(2)}) copy-start(bf16[192,256]{1,0:T(8,128)(2,1)} %copy-done.32) | copy-start | bytes 294916
  299.6 7.8 %copy-start.53 = (bf16[192,192]{1,0:T(8,128)(2,1)S(1)}, bf16[192,192]{1,0:T(8,128)(2,1)}, u32[]{:S(2)}) copy-start(bf16[192,192]{1,0:T(8,128)(2,1)} %convolution_convert_fusion) | copy-start | bytes 221188
  304.7 2.7 copy-start.54
  312.1 3.8 collective-permute-start.5
  314.0 7.0 %collective-permute-start.6 = (bf16[192,1,8,16]{0,3,2,1:T(8,128)(2,1)S(1)}, bf16[192,1,8,16]{0,3,2,1:T(8,128)(2,1)S(1)}, u32[]{:S(2)}, u32[]{:S(2)}) collective-permute-start(bf16[192,1,8,16]{0,3,2,1:T(8,128)(2,1)S(1)} %get-tuple-element.121), channel_id=1, source_target_pairs={{1,0},{2,1},{3,2},{4,3},{5,4},{6,5},{7,6},{8,7},{9,8},{10,9},{11,1... | collective-permute-start | bytes 147464 | tf_op jit(solution)/shard_map/ppermute | solution.py:22
  326.7 6.6 %copy-start.67 = (u32[256]{0:T(256)S(1)}, u32[256]{0:T(256)}, u32[]{:S(2)}) copy-start(u32[256]{0:T(256)} %constant.59) | copy-start | bytes 3076
  328.5 8.5 %all-to-all-start = ((bf16[8,24,256]{2,1,0:T(8,128)(2,1)}), bf16[8,24,256]{2,1,0:T(8,128)(2,1)S(1)}, u32[]{:S(2)}, u32[]{:S(2)}) async-start(bf16[8,24,256]{2,1,0:T(8,128)(2,1)} %bitcast.122), calls=%async_computation | async-start | bytes 196608 | tf_op jit(solution)/shard_map/all_to_all | solution.py:183
  334.5 9.1 %collective-permute-start.2 = (bf16[192,256]{1,0:T(8,128)(2,1)S(1)}, bf16[192,256]{1,0:T(8,128)(2,1)S(1)}, u32[]{:S(2)}, u32[]{:S(2)}) collective-permute-start(bf16[192,256]{1,0:T(8,128)(2,1)S(1)} %get-tuple-element.44), channel_id=1, source_target_pairs={{224,0},{0,32},{32,64},{64,96},{96,128},{128,160},{160,192},{192,2... | collective-permute-start | bytes 294920 | tf_op jit(solution)/shard_map/ppermute | solution.py:30
  334.6 9.6 %collective-permute-start.7 = (bf16[192,256]{1,0:T(8,128)(2,1)S(1)}, bf16[192,256]{1,0:T(8,128)(2,1)S(1)}, u32[]{:S(2)}, u32[]{:S(2)}) collective-permute-start(bf16[192,256]{1,0:T(8,128)(2,1)S(1)} %get-tuple-element.141), channel_id=1, source_target_pairs={{32,0},{64,32},{96,64},{128,96},{160,128},{192,160},{224,192},{0,2... | collective-permute-start | bytes 294920 | tf_op jit(solution)/shard_map/ppermute | solution.py:30
  337.6 9.1 %all-to-all-start.1 = ((bf16[8,24,256]{2,1,0:T(8,128)(2,1)}), bf16[8,24,256]{2,1,0:T(8,128)(2,1)S(1)}, u32[]{:S(2)}, u32[]{:S(2)}) async-start(bf16[8,24,256]{2,1,0:T(8,128)(2,1)} %rev.3), calls=%async_computation.1 | async-start | bytes 196608 | tf_op jit(solution)/shard_map/all_to_all | solution.py:185
  (15 other events, 20.8 us)
Sparse Core Ops, SparseCore 0:
  312.2 147.5 all-reduce.7
where the time goes:
time: 470 us; the launch traced here: 468 us
  blocking collectives  218 us (46%)
  waiting for transfers between devices  123 us (26%)
  matrix products  60.7 us (13%)
  starting transfers between devices  26.1 us (6%)
  local copies, waits for them, and re-layouts  16.4 us (3%)
  between operations  16.3 us (3%)
  other arithmetic  7.8 us (2%)
    psum x2, blocking collectives, norm_stats(): first_sum = lax.psum(jnp.sum(conv_out, axis=1), 'slab')  147 us
    unnamed x2, waiting for transfers between devices  112 us
    psum x1, blocking collectives, norm_stats(): lax.psum(jnp.sum(jnp.square(conv_out - center[:, None]), axis=1), 'slab')  71.7 us
    dot_general x27, matrix products, kernel_rows(): lax.dot_general(part_rows, grad_z, (((1,), (1,)), ((), ())), preferred_el...  29.6 us
    dot_general x54, matrix products, convolve(): lax.dot_general(weight, tap_list[tap_index], (((0,), (0,)), ((), ())), pr...  22 us
    ppermute x3, starting transfers between devices, padded_2(): lax.ppermute(lax.slice_in_dim(block, block.shape[dim] - width, None, axis...  10.2 us
  transfers between devices with their start and end apart: 11, of which 6 were waited for; matrix products, arithmetic and copies ran while one was open for 3% of the time, Pallas kernels for 0%

commit v1 on v0

v1 whole, which is shorter than its diff:
```python
import jax
import jax.numpy as jnp
from jax import lax
from jax.experimental import pallas as pl
from jax.experimental.pallas import tpu as pltpu
from jax.sharding import Mesh
from jax.sharding import PartitionSpec as P

ROWS = 8
COLS = 16
AREA = ROWS * COLS
TAPS = 27
SLABS = ("y", "z")

epsilon = 1e-05
leak_slope = 0.01

F32 = jnp.float32
BF16 = jnp.bfloat16
VMEM = pl.BlockSpec(memory_space=pltpu.VMEM)
SMEM = pl.BlockSpec(memory_space=pltpu.SMEM)


def call(body, outs, scratch, flops, moved, *args, smem=0):
    specs = [SMEM] * smem + [VMEM] * (len(args) - smem)
    shapes = [jax.ShapeDtypeStruct(shape, kind) for shape, kind in outs]
    return pl.pallas_call(
        body,
        out_shape=shapes,
        in_specs=specs,
        out_specs=[VMEM] * len(outs),
        scratch_shapes=[pltpu.VMEM(shape, kind) for shape, kind in scratch],
        compiler_params=pltpu.CompilerParams(vmem_limit_bytes=40 * 1024 * 1024),
        cost_estimate=pl.CostEstimate(flops=flops, bytes_accessed=moved, transcendentals=0),
        name=body.__name__,
    )(*args)


def tap_masks():
    cell = lax.broadcasted_iota(jnp.int32, (1, AREA), 1)
    row = cell // COLS
    col = cell % COLS
    masks = {}
    for b in range(3):
        for c in range(3):
            inside = None
            if b != 1:
                inside = row > 0 if b == 0 else row < ROWS - 1
            if c != 1:
                part = col > 0 if c == 0 else col < COLS - 1
                inside = part if inside is None else jnp.logical_and(inside, part)
            masks[(b, c)] = inside
    return masks


def shifted(plane, b, c, masks):
    step = (b - 1) * COLS + (c - 1)
    if step == 0:
        return plane
    moved = pltpu.roll(plane, (-step) % AREA, 1)
    return jnp.where(masks[(b, c)], moved, 0.0)


def columns(tile, row):
    square = jnp.concatenate([tile, jnp.zeros((AREA - 8, AREA), F32)], axis=0).T
    return jnp.concatenate([square[:, row : row + 1], square[:64, row + 1 : row + 2]], axis=0)


def packed_tile(cols):
    lane = lax.broadcasted_iota(jnp.int32, (AREA, AREA), 1)
    square = jnp.zeros((AREA, AREA), F32)
    for index, col in enumerate(cols):
        high = jnp.concatenate([col[128:], jnp.zeros((64, 1), F32)], axis=0)
        square = jnp.where(lane == 2 * index, col[:128], square)
        square = jnp.where(lane == 2 * index + 1, high, square)
    return square.T[:8]


def spread_sums(received, row, cells, peers):
    total = jnp.sum(received, axis=0)
    mean = total / peers
    apart = jnp.sum(jnp.square(received - mean[None]), axis=0)
    return columns(mean, row), columns(total, row + 2) + cells * columns(apart, row)


def local_stats(planes_out, cells):
    mean = sum(jnp.sum(p, axis=1, keepdims=True) for p in planes_out) / cells
    squares = sum(jnp.sum(jnp.square(p - mean), axis=1, keepdims=True) for p in planes_out)
    return mean, squares


def turn_weights(w_ref, out_ref):
    for pair in range(14):
        width = 384 if pair < 13 else 192
        block = w_ref[:, pair * 384 : pair * 384 + width].T
        if width == 384:
            block = jnp.concatenate([block[:192], block[192:]], axis=1)
        out_ref[:, pair * 384 : pair * 384 + width] = block


def fill_taps(planes, outputs, x_ref, masks, channels):
    for q, plane in enumerate(planes):
        wide = plane.astype(F32)
        for b in range(3):
            for c in range(3):
                view = shifted(wide, b, c, masks).astype(BF16)
                for a in range(3):
                    j = q - a
                    if 0 <= j < outputs:
                        tap = 9 * a + 3 * b + c
                        x_ref[
                            tap * channels : (tap + 1) * channels, j * AREA : (j + 1) * AREA
                        ] = view


def conv_bwd(own_ref, low_ref, high_ref, wt_ref, z_ref, send_ref, x_ref):
    masks = tap_masks()
    planes = [low_ref[0], low_ref[1], own_ref[0], own_ref[1], high_ref[0], high_ref[1]]
    fill_taps(planes, 4, x_ref, masks, 192)
    z = jnp.dot(wt_ref[...], x_ref[...], preferred_element_type=F32)
    for j in range(4):
        z_ref[j] = z[:, j * AREA : (j + 1) * AREA]
    mean, squares = local_stats([z[:, AREA : 2 * AREA], z[:, 2 * AREA : 3 * AREA]], 2.0 * AREA)
    tile = packed_tile([mean, squares])
    send_ref[...] = jnp.broadcast_to(tile[None], send_ref.shape)


def conv_fwd(own_ref, low_ref, high_ref, wt_ref, z_ref, tile_ref, x_ref):
    masks = tap_masks()
    planes = [low_ref[0], own_ref[0], own_ref[1], high_ref[0]]
    fill_taps(planes, 2, x_ref, masks, 192)
    z = jnp.dot(wt_ref[...], x_ref[...], preferred_element_type=F32)
    for j in range(2):
        z_ref[j] = z[:, j * AREA : (j + 1) * AREA]
    mean, squares = local_stats([z[:, :AREA], z[:, AREA:]], 2.0 * AREA)
    tile_ref[...] = packed_tile([jnp.zeros_like(mean), jnp.zeros_like(mean), mean, squares])


def row_taps(own_ref, a_ref, b_ref, c_ref, out_ref, wide_ref, turned_ref):
    masks = tap_masks()
    for peer, ref in enumerate((own_ref, a_ref, b_ref, c_ref)):
        for q in range(4):
            wide_ref[...] = ref[q].astype(F32)
            for r in range(6):
                turned_ref[8 * r : 8 * r + 8, :] = wide_ref[pl.ds(r, 8, stride=6), :]
            plane = turned_ref[...]
            for b in range(3):
                for c in range(3):
                    view = shifted(plane, b, c, masks).astype(BF16)
                    for a in range(3):
                        j = q - a
                        if 0 <= j < 2:
                            tap = 9 * a + 3 * b + c
                            lanes = (2 * peer + j) * AREA
                            out_ref[tap * 48 : (tap + 1) * 48, lanes : lanes + AREA] = view


def head_and_sums(
    flag_ref,
    z_ref,
    recv_ref,
    own_ref,
    low_ref,
    high_ref,
    out_cot_ref,
    skip_cot_ref,
    rim_low_ref,
    rim_high_ref,
    label_ref,
    affine_ref,
    head_ref,
    head_turned_ref,
    fwd_tile_ref,
    normed_ref,
    act_ref,
    up_ref,
    share_ref,
    scale_ref,
    send_ref,
):
    decoder = flag_ref[0] == 1
    last = flag_ref[1] == 1
    peers = recv_ref.shape[0]
    cells = 2.0 * AREA
    mean, squares = spread_sums(recv_ref[...], 0, cells, peers)
    inv_std = lax.rsqrt(squares / (cells * peers) + epsilon)
    gain = columns(affine_ref[...], 0)
    shift = columns(affine_ref[...], 2)
    scale_ref[...] = jnp.broadcast_to(gain * inv_std, scale_ref.shape)
    joined = [low_ref[1], own_ref[0], own_ref[1], high_ref[0]]
    out_cots = [rim_low_ref[192:384], out_cot_ref[0], out_cot_ref[1], rim_high_ref[192:384]]
    skip_cots = [rim_low_ref[384:576], skip_cot_ref[0], skip_cot_ref[1], rim_high_ref[384:576]]
    labels = [
        rim_low_ref[576:592].astype(F32)[:1],
        label_ref[0:1, :].astype(F32),
        label_ref[1:2, :].astype(F32),
        rim_high_ref[576:592].astype(F32)[:1],
    ]
    classes = head_ref.shape[1]
    class_id = lax.broadcasted_iota(jnp.int32, (classes, AREA), 0).astype(F32)
    sum_grad = jnp.zeros((192, 1), F32)
    sum_cross = jnp.zeros((192, 1), F32)
    for j in range(4):
        normed = (z_ref[j] - mean) * inv_std
        scaled = normed * gain + shift
        activated = jnp.where(scaled > 0, scaled, leak_slope * scaled)
        output = (joined[j].astype(F32) + activated).astype(BF16)
        logits = jnp.dot(head_turned_ref[...], output, preferred_element_type=F32)
        raised = jnp.exp(logits - jnp.max(logits, axis=0, keepdims=True))
        prob = raised / jnp.sum(raised, axis=0, keepdims=True)
        delta = (prob - jnp.where(class_id == labels[j], 1.0, 0.0)).astype(BF16)
        head_cot = jnp.dot(head_ref[...], delta, preferred_element_type=F32)
        upstream = jnp.where(last, head_cot, out_cots[j].astype(F32)) + jnp.where(
            decoder, 0.0, skip_cots[j].astype(F32)
        )
        grad_act = upstream * jnp.where(scaled > 0, 1.0, leak_slope)
        normed_ref[j] = normed
        act_ref[j] = grad_act
        if j in (1, 2):
            up_ref[j - 1] = upstream
            share_ref[j - 1] = grad_act.astype(BF16)
            share_ref[j + 1] = normed.astype(BF16)
            sum_grad = sum_grad + jnp.sum(grad_act, axis=1, keepdims=True)
            sum_cross = sum_cross + jnp.sum(grad_act * normed, axis=1, keepdims=True)
    tile = packed_tile([sum_grad, sum_cross]) + fwd_tile_ref[...]
    send_ref[...] = jnp.broadcast_to(tile[None], send_ref.shape)


def kernel_grads(
    recv_ref,
    own_ref,
    a_ref,
    b_ref,
    c_ref,
    scale_ref,
    taps_ref,
    out_ref,
    tot_ref,
    gz_ref,
    low_ref,
    rest_ref,
):
    total_cells = 2.0 * AREA * recv_ref.shape[0]
    total = jnp.sum(recv_ref[...], axis=0)
    tot_ref[...] = total * (total_cells ** (-0.5))
    sum_grad = columns(total, 0) / total_cells
    sum_cross = columns(total, 2) / total_cells
    scale = scale_ref[...]
    for peer, ref in enumerate((own_ref, a_ref, b_ref, c_ref)):
        for j in range(2):
            grad_z = scale * (ref[j].astype(F32) - sum_grad - ref[2 + j].astype(F32) * sum_cross)
            lanes = (2 * peer + j) * AREA
            gz_ref[:, lanes : lanes + AREA] = grad_z.astype(BF16)
    grads = lax.dot_general(
        taps_ref[...], gz_ref[...], (((1,), (1,)), ((), ())), preferred_element_type=F32
    )
    low_ref[...] = grads[:, :128]
    rest_ref[...] = jnp.concatenate([grads[:648, 128:], grads[648:, 128:]], axis=1)
    pad = jnp.zeros((15, 384), F32)
    for z in range(8):
        first = low_ref[pl.ds(z, 81, stride=8), :]
        second = low_ref[pl.ds(z + 648, 81, stride=8), :]
        third = rest_ref[pl.ds(z, 81, stride=8), :]
        both = jnp.concatenate([first, second, third], axis=1)
        out_ref[z] = jnp.concatenate([both, pad], axis=0).astype(BF16)


def input_grads(
    flag_ref,
    recv_ref,
    normed_ref,
    act_ref,
    up_ref,
    scale_ref,
    w_ref,
    fwd_z_ref,
    fwd_ref,
    affine_ref,
    gj_ref,
    fwd_out_ref,
    skip_ref,
    x_ref,
):
    decoder = flag_ref[0] == 1
    peers = recv_ref.shape[0]
    cells = 2.0 * AREA
    total_cells = cells * peers
    masks = tap_masks()
    total = jnp.sum(recv_ref[...], axis=0)
    sum_grad = columns(total, 0) / total_cells
    sum_cross = columns(total, 2) / total_cells
    scale = scale_ref[...]
    for q in range(4):
        grad_z = scale * (act_ref[q] - sum_grad - normed_ref[q] * sum_cross)
        if q == 0:
            grad_z = jnp.where(flag_ref[2] == 1, grad_z, 0.0)
        if q == 3:
            grad_z = jnp.where(flag_ref[3] == 1, grad_z, 0.0)
        for b in range(3):
            for c in range(3):
                view = shifted(grad_z, 2 - b, 2 - c, masks).astype(BF16)
                for a in range(3):
                    j = q + a - 2
                    if 0 <= j < 2:
                        tap = 9 * a + 3 * b + c
                        x_ref[tap * 192 : (tap + 1) * 192, j * AREA : (j + 1) * AREA] = view
    back = jnp.dot(w_ref[...], x_ref[...], preferred_element_type=F32)
    mean, squares = spread_sums(recv_ref[...], 4, cells, peers)
    inv_std = lax.rsqrt(squares / total_cells + epsilon)
    gain = columns(affine_ref[...], 0)
    shift = columns(affine_ref[...], 2)
    for j in range(2):
        grad = (up_ref[j] + back[:, j * AREA : (j + 1) * AREA]).astype(BF16)
        scaled = (fwd_z_ref[j] - mean) * inv_std * gain + shift
        activated = jnp.where(scaled > 0, scaled, leak_slope * scaled)
        output = (fwd_ref[j].astype(F32) + activated).astype(BF16)
        gj_ref[j] = grad
        fwd_out_ref[j] = output
        skip_ref[j] = jnp.where(decoder, grad.astype(F32), output.astype(F32)).astype(BF16)


def sum_rows(scale_out, recv_ref, out_ref):
    total = jnp.sum(recv_ref[...].astype(F32), axis=0) * scale_out
    for tap in range(TAPS):
        for r in range(6):
            flat = tap * 6 + r
            half, row = flat // 81, flat % 81
            low = total[row : row + 1, half * 128 : half * 128 + 128]
            rest = total[row : row + 1, 256 + half * 64 : 320 + half * 64]
            out_ref[0, r : r + 1, tap * 192 : (tap + 1) * 192] = jnp.concatenate(
                [low, rest], axis=1
            )


def pair_rows(values):
    padded = jnp.pad(values, ((0, 2), (0, 64)))
    return padded.reshape(8, AREA)


def moved(block, axis, distance, wrap=True):
    count = lax.axis_size(axis)
    route = [(i, (i + distance) % count) for i in range(count) if wrap or 0 <= i + distance < count]
    return lax.ppermute(block, axis, route)


def per_device(
    fwd_input,
    fwd_skip,
    bwd_input,
    bwd_skip,
    out_cot,
    skip_cot,
    kernel,
    norm_gain,
    norm_shift,
    head_weight,
    labels,
):
    segments = lax.axis_size("segment")
    slabs = lax.axis_size("y") * lax.axis_size("z")
    segment_id = lax.axis_index("segment")
    y_id = lax.axis_index("y")
    slab_id = y_id * lax.axis_size("z") + lax.axis_index("z")
    is_decoder = segment_id * 2 >= segments
    flags = jnp.stack(
        [is_decoder, segment_id == segments - 1, slab_id > 0, slab_id < slabs - 1]
    ).astype(jnp.int32)
    kernel_mat = kernel[0]
    affine = pair_rows(jnp.concatenate([norm_gain, norm_shift], axis=0))

    def by_plane(block):
        return jnp.swapaxes(block[0], 0, 1)

    def joined(block, skip):
        added = (block.astype(F32) + skip.astype(F32)).astype(BF16)
        return by_plane(jnp.where(is_decoder, added, block))

    bwd = joined(bwd_input, bwd_skip)
    bwd_low = moved(bwd, SLABS, 1, False)
    bwd_high = moved(bwd, SLABS, -1, False)
    fwd = joined(fwd_input, fwd_skip)
    out_cots = by_plane(out_cot)
    skip_cots = by_plane(skip_cot)

    def rim(p):
        names = jnp.broadcast_to(labels[p : p + 1].astype(BF16), (16, AREA))
        return jnp.concatenate([fwd[p], out_cots[p], skip_cots[p], names], axis=0)

    rim_low = moved(rim(1), SLABS, 1, False)
    rim_high = moved(rim(0), SLABS, -1, False)
    (turned,) = call(
        turn_weights, [((192, 5184), BF16)], [], 0, 4 * 192 * 5184, kernel_mat
    )
    z, stats_send = call(
        conv_bwd,
        [((4, 192, AREA), F32), ((slabs, 8, AREA), F32)],
        [((5184, 512), BF16)],
        2 * 5184 * 192 * 512,
        5000000,
        bwd,
        bwd_low,
        bwd_high,
        turned,
    )
    stats = lax.all_to_all(stats_send, SLABS, 0, 0, tiled=True)
    window = jnp.concatenate([bwd_low[1:], bwd, bwd_high[:1]], axis=0)

    def rows_for(distance):
        start = 48 * ((y_id + distance) % 4)
        return lax.dynamic_slice_in_dim(window, start, 48, axis=1)

    row_parts = [rows_for(0)] + [moved(rows_for(d), "y", d) for d in (1, 2, 3)]
    fwd_z, fwd_tile = call(
        conv_fwd,
        [((2, 192, AREA), F32), ((8, AREA), F32)],
        [((5184, 256), BF16)],
        2 * 5184 * 192 * 256,
        4000000,
        fwd,
        rim_low[None, :192],
        rim_high[None, :192],
        turned,
    )
    (taps,) = call(
        row_taps,
        [((1296, 1024), BF16)],
        [((48, AREA), F32), ((48, AREA), F32)],
        0,
        6000000,
        *row_parts,
    )
    normed, grad_act, upstream, share, scale, sums_send = call(
        head_and_sums,
        [
            ((4, 192, AREA), F32),
            ((4, 192, AREA), F32),
            ((2, 192, AREA), F32),
            ((4, 192, AREA), BF16),
            ((192, AREA), F32),
            ((slabs, 8, AREA), F32),
        ],
        [],
        4 * 192 * 105 * 512,
        4000000,
        flags,
        z,
        stats,
        bwd,
        bwd_low,
        bwd_high,
        out_cots,
        skip_cots,
        rim_low,
        rim_high,
        labels,
        affine,
        head_weight,
        head_weight.T,
        fwd_tile,
        smem=1,
    )
    sums = lax.all_to_all(sums_send, SLABS, 0, 0, tiled=True)
    shares = [share] + [moved(share, "y", d) for d in (1, 2, 3)]
    parts, totals = call(
        kernel_grads,
        [((8, 96, 384), BF16), ((8, AREA), F32)],
        [((192, 1024), BF16), ((1296, AREA), F32), ((648, AREA), F32)],
        2 * 1296 * 1024 * 192,
        5000000,
        sums,
        *shares,
        scale,
        taps,
    )
    summed = lax.all_to_all(parts, "z", 0, 0, tiled=True)
    grad_joined, fwd_out, outgoing = call(
        input_grads,
        [((2, 192, AREA), BF16)] * 3,
        [((5184, 256), BF16)],
        2 * 5184 * 192 * 256,
        4000000,
        flags,
        sums,
        normed,
        grad_act,
        upstream,
        scale,
        kernel_mat,
        fwd_z,
        fwd,
        affine,
        smem=1,
    )
    next_block = moved(fwd_out, "segment", 1)
    prev_block = moved(grad_joined, "segment", -1)
    mirrored = lax.ppermute(outgoing, "segment", [(i, segments - 1 - i) for i in range(segments)])
    total_cells = float(2 * slabs * AREA)
    (kernel_grad,) = pl.pallas_call(
        lambda recv, out: sum_rows(total_cells ** (-0.5), recv, out),
        out_shape=[jax.ShapeDtypeStruct((1, 6, 5184), F32)],
        in_specs=[VMEM],
        out_specs=[VMEM],
        name="sum_rows",
    )(summed)
    flat = totals.reshape(-1)

    def by_channel(block):
        return jnp.swapaxes(block, 0, 1)[None]

    return (
        by_channel(next_block),
        by_channel(prev_block),
        by_channel(mirrored),
        kernel_grad,
        flat[256:448][None],
        flat[:192][None],
    )


def solution(mesh):
    grid = Mesh(mesh.devices.reshape(mesh.devices.shape[0], 4, 8), ("segment", "y", "z"))
    field = P("segment", None, SLABS, None)
    in_specs = (field,) * 6 + (
        P("segment", None, None),
        P("segment", None),
        P("segment", None),
        P(),
        P(SLABS, None),
    )
    out_specs = (
        field,
        field,
        field,
        P("segment", SLABS, None),
        P("segment", None),
        P("segment", None),
    )
    return jax.shard_map(
        per_device, mesh=grid, in_specs=in_specs, out_specs=out_specs, check_vma=False
    )
```

time: 470 us -> 114 us (0.24)
  blocking collectives: 218 us -> 0 us
  waiting for transfers between devices: 123 us -> 19.7 us
  matrix products: 60.7 us -> 0 us
  starting transfers between devices: 26.1 us -> 47.1 us
  between operations: 16.3 us -> 0.95 us
  Pallas kernels: 0 us -> 15 us
  local copies, waits for them, and re-layouts: 16.4 us -> 26.3 us
    psum x3 -> x0, blocking collectives: 218 us -> none  [the longest x2 147 us: norm_stats(): first_sum = lax.psum(jnp.sum(conv_out, axis=1), 'slab')]
    unnamed x2 -> x0, waiting for transfers between devices: 112 us -> none
    dot_general x110 -> x0, matrix products: 60.7 us -> none  [the longest x27 29.6 us: kernel_rows(): lax.dot_general(part_rows, grad_z, (((1,), (1,)), ((), ())), preferred_el...]
    unnamed x140 -> x61, local copies, waits for them, and re-layouts: 5.19 us -> 24.4 us
    pallas_call x0 -> x8, Pallas kernels: none -> 15 us  [the longest x7 13.1 us: call(): pl.pallas_call(body, out_shape=shapes, in_specs=specs, out_specs=[VMEM] *...]
    all_to_all x2 -> x3, starting transfers between devices: 10.2 us -> 23.8 us  [the longest x1 13.5 us: per_device(): stats = lax.all_to_all(stats_send, SLABS, 0, 0, tiled=True)]
    ppermute x8 -> x13, starting transfers between devices: 15.9 us -> 23.3 us  [the longest x12 23.3 us: moved(): return lax.ppermute(block, axis, route)]
    all_to_all x2 -> x3, waiting for transfers between devices: 2.53 us -> 8.43 us  [the longest x1 7.11 us: per_device(): stats = lax.all_to_all(stats_send, SLABS, 0, 0, tiled=True)]
  transfers between devices with their start and end apart: 11 -> 16, of which waited for: 6 -> 7; matrix products, arithmetic and copies ran while one was open for 3% -> 8% of each run, Pallas kernels for 0% -> 7%
where the time goes in v1:
time: 114 us; the launch traced here: 113 us
  starting transfers between devices  47.1 us (41%)
  local copies, waits for them, and re-layouts  26.3 us (23%)
  waiting for transfers between devices  19.7 us (17%)
  Pallas kernels  15 us (13%)
  other arithmetic  3.74 us (3%)
    unnamed x61, local copies, waits for them, and re-layouts  24.4 us
    ppermute x12, starting transfers between devices, moved(): return lax.ppermute(block, axis, route)  23.3 us
    all_to_all x1, starting transfers between devices, per_device(): stats = lax.all_to_all(stats_send, SLABS, 0, 0, tiled=True)  13.5 us
    pallas_call x7, Pallas kernels, call(): pl.pallas_call(body, out_shape=shapes, in_specs=specs, out_specs=[VMEM] *...  13.1 us
    ppermute x12, waiting for transfers between devices, moved(): return lax.ppermute(block, axis, route)  8.79 us
    all_to_all x1, waiting for transfers between devices, per_device(): stats = lax.all_to_all(stats_send, SLABS, 0, 0, tiled=True)  7.11 us
    all_to_all x1, starting transfers between devices, per_device(): summed = lax.all_to_all(parts, 'z', 0, 0, tiled=True)  6.42 us
    all_to_all x1, starting transfers between devices, per_device(): sums = lax.all_to_all(sums_send, SLABS, 0, 0, tiled=True)  3.85 us
  transfers between devices with their start and end apart: 16, of which 7 were waited for; matrix products, arithmetic and copies ran while one was open for 8% of the time, Pallas kernels for 7%

profile of v1, /device:TPU:6, one launch (start us, length us, event | category | flops | bytes accessed | tf_op | source)
XLA Modules:
  0.0 112.8 jit_solution(7470034199220081290)
XLA Ops:
  0.7 1.1 fusion.3.own_ref
  1.8 1.3 %collective-permute-start.1 = (bf16[2,192,128]{2,1,0:T(8,128)(2,1)S(1)}, bf16[2,192,128]{2,1,0:T(8,128)(2,1)S(1)}, u32[]{:S(2)}, u32[]{:S(2)}) collective-permute-start(bf16[2,192,128]{2,1,0:T(8,128)(2,1)S(1)} %fusion.3.own_ref), channel_id=1, source_target_pairs={{1,0},{2,1},{3,2},{4,3},{5,4},{6,5},{7,6},{8,7},{9,8},{10,9},{11,1... | collective-permute-start | bytes 294920 | tf_op jit(solution)/shard_map/ppermute | solution.py:343
  3.1 4.6 %collective-permute-start = (bf16[2,192,128]{2,1,0:T(8,128)(2,1)S(1)}, bf16[2,192,128]{2,1,0:T(8,128)(2,1)S(1)}, u32[]{:S(2)}, u32[]{:S(2)}) collective-permute-start(bf16[2,192,128]{2,1,0:T(8,128)(2,1)S(1)} %fusion.3.own_ref), channel_id=1, source_target_pairs={{0,1},{1,2},{2,3},{3,4},{4,5},{5,6},{6,7},{7,8},{8,9},{9,10},{10,1... | collective-permute-start | bytes 294920 | tf_op jit(solution)/shard_map/ppermute | solution.py:343
  7.7 0.7 convert.4
  8.4 0.9 copy.37
  9.3 0.9 copy.36
  10.2 1.0 fusion.2.own_ref.fwd_ref
  11.2 3.8 %collective-permute-start.2 = (bf16[592,128]{1,0:T(8,128)(2,1)S(1)}, bf16[592,128]{1,0:T(8,128)(2,1)S(1)}, u32[]{:S(2)}, u32[]{:S(2)}) collective-permute-start(bf16[592,128]{1,0:T(8,128)(2,1)S(1)} %pad_maximum_fusion.1), channel_id=1, source_target_pairs={{0,1},{1,2},{2,3},{3,4},{4,5},{5,6},{6,7},{7,8},{8,9},{9,10},{10,1... | collective-permute-start | bytes 454664 | tf_op jit(solution)/shard_map/ppermute | solution.py:343
  15.1 1.3 %collective-permute-start.3 = (bf16[592,128]{1,0:T(8,128)(2,1)S(1)}, bf16[592,128]{1,0:T(8,128)(2,1)S(1)}, u32[]{:S(2)}, u32[]{:S(2)}) collective-permute-start(bf16[592,128]{1,0:T(8,128)(2,1)S(1)} %pad_maximum_fusion.2), channel_id=1, source_target_pairs={{1,0},{2,1},{3,2},{4,3},{5,4},{6,5},{7,6},{8,7},{9,8},{10,9},{11,1... | collective-permute-start | bytes 454664 | tf_op jit(solution)/shard_map/ppermute | solution.py:343
  16.5 0.1 add_convert_fusion.2.flag_ref
  16.5 0.1 copy.25
  16.7 1.1 turn_weights.1.wt_ref
  17.8 1.3 %copy-done.2 = bf16[192,5184]{1,0:T(8,128)(2,1)} copy-done((bf16[192,5184]{1,0:T(8,128)(2,1)}, bf16[192,5184]{1,0:T(8,128)(2,1)S(1)}, u32[]{:S(2)}) %copy-start.2) | copy-done | bytes 1990680
  19.1 1.6 %copy-done.3 = bf16[192,5184]{1,0:T(8,128)(2,1)S(1)} copy-done((bf16[192,5184]{1,0:T(8,128)(2,1)S(1)}, bf16[192,5184]{1,0:T(8,128)(2,1)}, u32[]{:S(2)}) %copy-start.3) | copy-done | bytes 1990680
  20.7 2.7 %conv_bwd.1 = (f32[4,192,128]{2,1,0:T(8,128)S(1)}, f32[32,8,128]{2,1,0:T(8,128)}) custom-call(bf16[2,192,128]{2,1,0:T(8,128)(2,1)S(1)} %fusion.3.own_ref, bf16[2,192,128]{2,1,0:T(8,128)(2,1)S(1)} %collective-permute-done.low_ref, bf16[2,192,128]{2,1,0:T(8,128)(2,1)S(1)} %collective-permute-done.1.high_ref, bf16[192,5184]{1,0:T(8,128)(2,1)S(1)} %copy-done.3), custom_call_target="tpu_custom_call" | custom-call | flops 1019215872 | bytes 5000000 | tf_op jit(solution)/shard_map/conv_bwd/pallas_call | solution.py:27
  23.4 0.8 copy-done.7
  24.2 13.5 %all-to-all-start = ((f32[32,8,128]{2,1,0:T(8,128)}), f32[32,8,128]{2,1,0:T(8,128)S(1)}, u32[]{:S(2)}, u32[]{:S(2)}) async-start(f32[32,8,128]{2,1,0:T(8,128)} %get-tuple-element.22), calls=%async_computation | async-start | bytes 262144 | tf_op jit(solution)/shard_map/all_to_all | solution.py:405
  37.7 0.6 slice.67
  38.4 0.6 slice.66
  39.0 1.3 %conv_fwd.1 = (f32[2,192,128]{2,1,0:T(8,128)S(1)}, f32[8,128]{1,0:T(8,128)S(1)}) custom-call(bf16[2,192,128]{2,1,0:T(8,128)(2,1)S(1)} %fusion.2.own_ref.fwd_ref, bf16[1,192,128]{2,1,0:T(8,128)(2,1)S(1)} %slice_bitcast_fusion.1.low_ref, bf16[1,192,128]{2,1,0:T(8,128)(2,1)S(1)} %slice_bitcast_fusion.high_ref, bf16[192,5184]{1,0:T(8,128)(2,1)S(1)} %copy-done.4), custom_call_target="tpu_custom_call" | custom-call | flops 509607936 | bytes 4000000 | tf_op jit(solution)/shard_map/conv_fwd/pallas_call | solution.py:27
  40.3 0.7 copy-done.19
  41.0 7.1 %all-to-all-done.recv_ref = f32[32,8,128]{2,1,0:T(8,128)S(1)} async-done(((f32[32,8,128]{2,1,0:T(8,128)}), f32[32,8,128]{2,1,0:T(8,128)S(1)}, u32[]{:S(2)}, u32[]{:S(2)}) %all-to-all-start) | async-done | bytes 131104 | tf_op jit(solution)/shard_map/all_to_all | solution.py:405
  48.1 1.0 copy-done.8
  49.1 0.9 copy-done.10
  50.0 0.8 copy-done.18
  50.8 2.5 %head_and_sums.1 = (f32[4,192,128]{2,1,0:T(8,128)S(1)}, f32[4,192,128]{2,1,0:T(8,128)S(1)}, f32[2,192,128]{2,1,0:T(8,128)S(1)}, bf16[4,192,128]{2,1,0:T(8,128)(2...) custom-call(s32[4]{0:T(128)S(1)} %add_convert_fusion.2.flag_ref, f32[4,192,128]{2,1,0:T(8,128)S(1)} %copy-done.8, ...), custom_call_target="tpu_custom_call" | custom-call | flops 41287680 | bytes 4000000 | tf_op jit(solution)/shard_map/head_and_sums/pallas_call | solution.py:27
  53.3 0.7 copy-done.5
  54.1 0.7 copy-done.21
  54.8 3.9 %all-to-all-start.1 = ((f32[32,8,128]{2,1,0:T(8,128)}), f32[32,8,128]{2,1,0:T(8,128)S(1)}, u32[]{:S(2)}, u32[]{:S(2)}) async-start(f32[32,8,128]{2,1,0:T(8,128)} %get-tuple-element.24), calls=%async_computation.1 | async-start | bytes 262144 | tf_op jit(solution)/shard_map/all_to_all | solution.py:462
  58.6 0.8 pad_maximum_fusion
  59.5 3.1 %collective-permute-start.9 = (bf16[4,192,128]{2,1,0:T(8,128)(2,1)}, bf16[4,192,128]{2,1,0:T(8,128)(2,1)S(1)}, u32[]{:S(2)}, u32[]{:S(2)}) collective-permute-start(bf16[4,192,128]{2,1,0:T(8,128)(2,1)} %get-tuple-element.33.own_ref), channel_id=1, source_target_pairs={{0,24},{8,0},{16,8},{24,16},{1,25},{9,1},{17,9},{25,17},{2,26},{10... | collective-permute-start | bytes 589832 | tf_op jit(solution)/shard_map/ppermute | solution.py:343
  62.6 0.7 collective-permute-start.8
  63.3 0.9 collective-permute-start.7
  64.3 2.4 %collective-permute-start.12 = (bf16[4,48,128]{2,1,0:T(8,128)(2,1)S(1)}, bf16[4,48,128]{2,1,0:T(8,128)(2,1)S(1)}, u32[]{:S(2)}, u32[]{:S(2)}) collective-permute-start(bf16[4,48,128]{2,1,0:T(8,128)(2,1)S(1)} %get-tuple-element.42), channel_id=1, source_target_pairs={{0,24},{8,0},{16,8},{24,16},{1,25},{9,1},{17,9},{25,17},{2,26},{10... | collective-permute-start | bytes 147464 | tf_op jit(solution)/shard_map/ppermute | solution.py:343
  66.7 1.6 %collective-permute-start.11 = (bf16[4,48,128]{2,1,0:T(8,128)(2,1)S(1)}, bf16[4,48,128]{2,1,0:T(8,128)(2,1)S(1)}, u32[]{:S(2)}, u32[]{:S(2)}) collective-permute-start(bf16[4,48,128]{2,1,0:T(8,128)(2,1)S(1)} %get-tuple-element.43), channel_id=1, source_target_pairs={{0,16},{8,24},{16,0},{24,8},{1,17},{9,25},{17,1},{25,9},{2,18},{10... | collective-permute-start | bytes 147464 | tf_op jit(solution)/shard_map/ppermute | solution.py:343
  68.3 3.1 %collective-permute-done.12.c_ref = bf16[4,48,128]{2,1,0:T(8,128)(2,1)S(1)} collective-permute-done((bf16[4,48,128]{2,1,0:T(8,128)(2,1)S(1)}, bf16[4,48,128]{2,1,0:T(8,128)(2,1)S(1)}, u32[]{:S(2)}, u32[]{:S(2)}) %collective-permute-start.12) | collective-permute-done | bytes 49184 | tf_op jit(solution)/shard_map/ppermute | solution.py:343
  71.4 1.8 %collective-permute-start.10 = (bf16[4,48,128]{2,1,0:T(8,128)(2,1)S(1)}, bf16[4,48,128]{2,1,0:T(8,128)(2,1)S(1)}, u32[]{:S(2)}, u32[]{:S(2)}) collective-permute-start(bf16[4,48,128]{2,1,0:T(8,128)(2,1)S(1)} %get-tuple-element.44), channel_id=1, source_target_pairs={{0,8},{8,16},{16,24},{24,0},{1,9},{9,17},{17,25},{25,1},{2,10},{10... | collective-permute-start | bytes 147464 | tf_op jit(solution)/shard_map/ppermute | solution.py:343
  73.2 1.2 %collective-permute-done.11.b_ref = bf16[4,48,128]{2,1,0:T(8,128)(2,1)S(1)} collective-permute-done((bf16[4,48,128]{2,1,0:T(8,128)(2,1)S(1)}, bf16[4,48,128]{2,1,0:T(8,128)(2,1)S(1)}, u32[]{:S(2)}, u32[]{:S(2)}) %collective-permute-start.11) | collective-permute-done | bytes 49184 | tf_op jit(solution)/shard_map/ppermute | solution.py:343
  74.5 2.7 %collective-permute-done.10.a_ref = bf16[4,48,128]{2,1,0:T(8,128)(2,1)S(1)} collective-permute-done((bf16[4,48,128]{2,1,0:T(8,128)(2,1)S(1)}, bf16[4,48,128]{2,1,0:T(8,128)(2,1)S(1)}, u32[]{:S(2)}, u32[]{:S(2)}) %collective-permute-start.10) | collective-permute-done | bytes 49184 | tf_op jit(solution)/shard_map/ppermute | solution.py:343
  77.1 0.6 row_taps.1.taps_ref
  77.7 0.7 copy-done.11
  78.4 0.7 copy-done.13
  79.1 0.7 copy-done.15
  79.8 0.9 copy-done.12
  80.7 0.9 copy-done.14
  81.6 0.9 copy-done.16
  82.5 3.1 %kernel_grads.1 = (bf16[8,96,384]{2,1,0:T(8,128)(2,1)}, f32[8,128]{1,0:T(8,128)S(1)}) custom-call(f32[32,8,128]{2,1,0:T(8,128)S(1)} %all-to-all-done.1.recv_ref, bf16[4,192,128]{2,1,0:T(8,128)(2,1)} %get-tuple-element.33.own_ref, bf16[4,192,128]{2,1,0:T(8,128)(2,1)S(1)} %copy-done.16, bf16[4,192,128]{2,1,0:T(8,128)(2,1)S(1)} %copy-done.14, ...), custom_call_target="tpu_custom_call" | custom-call | flops 509607936 | bytes 5000000 | tf_op jit(solution)/shard_map/kernel_grads/pallas_call | solution.py:27
  85.6 6.4 %all-to-all-start.2 = ((bf16[8,96,384]{2,1,0:T(8,128)(2,1)}), bf16[8,96,384]{2,1,0:T(8,128)(2,1)S(1)}, u32[]{:S(2)}, u32[]{:S(2)}) async-start(bf16[8,96,384]{2,1,0:T(8,128)(2,1)} %get-tuple-element.34), calls=%async_computation.2 | async-start | bytes 1179648 | tf_op jit(solution)/shard_map/all_to_all | solution.py:475
  92.0 1.6 %copy-done.1 = bf16[1,192,5184]{2,1,0:T(8,128)(2,1)S(1)} copy-done((bf16[1,192,5184]{2,1,0:T(8,128)(2,1)S(1)}, bf16[1,192,5184]{2,1,0:T(8,128)(2,1)}, u32[]{:S(2)}) %copy-start.1) | copy-done | bytes 1990680
  93.6 1.0 copy-done.6
  94.6 0.9 copy-done.20
  95.5 0.9 copy-done.22
  96.4 1.8 %input_grads.1 = (bf16[2,192,128]{2,1,0:T(8,128)(2,1)S(1)}, bf16[2,192,128]{2,1,0:T(8,128)(2,1)S(1)}, bf16[2,192,128]{2,1,0:T(8,128)(2,1)S(1)}) custom-call(s32[4]{0:T(128)S(1)} %add_convert_fusion.2.flag_ref, f32[32,8,128]{2,1,0:T(8,128)S(1)} %all-to-all-done.1.recv_ref, f32[4,192,128]{2,1,0:T(8,128)S(1)} %get-tuple-element.25.normed_ref, ...), custom_call_target="tpu_custom_call" | custom-call | flops 509607936 | bytes 4000000 | tf_op jit(solution)/shard_map/input_grads/pallas_call | solution.py:27
  98.3 1.7 %collective-permute-start.5 = (bf16[2,192,128]{2,1,0:T(8,128)(2,1)S(1)}, bf16[2,192,128]{2,1,0:T(8,128)(2,1)S(1)}, u32[]{:S(2)}, u32[]{:S(2)}) collective-permute-start(bf16[2,192,128]{2,1,0:T(8,128)(2,1)S(1)} %get-tuple-element.31), channel_id=1, source_target_pairs={{0,224},{32,0},{64,32},{96,64},{128,96},{160,128},{192,160},{224,1... | collective-permute-start | bytes 294920 | tf_op jit(solution)/shard_map/ppermute | solution.py:343
  100.0 0.6 fusion.4
  100.6 1.7 %collective-permute-done.4 = bf16[2,192,128]{2,1,0:T(8,128)(2,1)S(1)} collective-permute-done((bf16[2,192,128]{2,1,0:T(8,128)(2,1)S(1)}, bf16[2,192,128]{2,1,0:T(8,128)(2,1)S(1)}, u32[]{:S(2)}, u32[]{:S(2)}) %collective-permute-start.4) | collective-permute-done | bytes 98336 | tf_op jit(solution)/shard_map/ppermute | solution.py:343
  102.3 0.7 copy.26
  103.0 0.7 copy.27
  103.8 2.5 %collective-permute-done.6 = bf16[2,192,128]{2,1,0:T(8,128)(2,1)S(1)} collective-permute-done((bf16[2,192,128]{2,1,0:T(8,128)(2,1)S(1)}, bf16[2,192,128]{2,1,0:T(8,128)(2,1)S(1)}, u32[]{:S(2)}, u32[]{:S(2)}) %collective-permute-start.6) | collective-permute-done | bytes 98336 | tf_op jit(solution)/shard_map/ppermute | solution.py:496
  106.3 0.7 copy.28
  107.0 1.3 %all-to-all-done.2.recv = bf16[8,96,384]{2,1,0:T(8,128)(2,1)S(1)} async-done(((bf16[8,96,384]{2,1,0:T(8,128)(2,1)}), bf16[8,96,384]{2,1,0:T(8,128)(2,1)S(1)}, u32[]{:S(2)}, u32[]{:S(2)}) %all-to-all-start.2) | async-done | bytes 589856 | tf_op jit(solution)/shard_map/all_to_all | solution.py:475
  108.4 0.8 copy-done.24
  109.2 1.9 %sum_rows.1 = f32[1,6,5184]{2,1,0:T(8,128)} custom-call(bf16[8,96,384]{2,1,0:T(8,128)(2,1)} %copy-done.24), custom_call_target="tpu_custom_call" | custom-call | tf_op jit(solution)/shard_map/sum_rows/pallas_call | solution.py:498
  111.1 1.7 %copy.29 = f32[1,6,5184]{2,0,1:T(1,128)} copy(f32[1,6,5184]{2,1,0:T(8,128)} %sum_rows.1) | data formatting | bytes 248832
  (57 shorter events, 0.2 us)
Async XLA Ops:
  0.6 15.8 %copy-start.25 = (f32[1,192]{1,0:T(1,128)S(1)}, f32[1,192]{1,0:T(1,128)}, u32[]{:S(2)}) copy-start(f32[1,192]{1,0:T(1,128)} %param.19) | copy-start | bytes 2308
  0.6 15.8 %copy-start.26 = (f32[1,192]{1,0:T(1,128)S(1)}, f32[1,192]{1,0:T(1,128)}, u32[]{:S(2)}) copy-start(f32[1,192]{1,0:T(1,128)} %param.18) | copy-start | bytes 2308
  0.7 15.9 %copy-start.17 = (bf16[192,105]{1,0:T(8,128)(2,1)S(1)}, bf16[192,105]{1,0:T(8,128)(2,1)}, u32[]{:S(2)}) copy-start(bf16[192,105]{1,0:T(8,128)(2,1)} %head_ref.1) | copy-start | bytes 120964
  0.7 16.0 %copy-start = (bf16[1,192,5184]{2,1,0:T(8,128)(2,1)S(1)}, bf16[1,192,5184]{2,1,0:T(8,128)(2,1)}, u32[]{:S(2)}) copy-start(bf16[1,192,5184]{2,1,0:T(8,128)(2,1)} %param.17) | copy-start | bytes 5971972
  1.8 17.3 %collective-permute-start.1 = (bf16[2,192,128]{2,1,0:T(8,128)(2,1)S(1)}, bf16[2,192,128]{2,1,0:T(8,128)(2,1)S(1)}, u32[]{:S(2)}, u32[]{:S(2)}) collective-permute-start(bf16[2,192,128]{2,1,0:T(8,128)(2,1)S(1)} %fusion.3.own_ref), channel_id=1, source_target_pairs={{1,0},{2,1},{3,2},{4,3},{5,4},{6,5},{7,6},{8,7},{9,8},{10,9},{11,1... | collective-permute-start | bytes 294920 | tf_op jit(solution)/shard_map/ppermute | solution.py:343
  3.1 16.0 %collective-permute-start = (bf16[2,192,128]{2,1,0:T(8,128)(2,1)S(1)}, bf16[2,192,128]{2,1,0:T(8,128)(2,1)S(1)}, u32[]{:S(2)}, u32[]{:S(2)}) collective-permute-start(bf16[2,192,128]{2,1,0:T(8,128)(2,1)S(1)} %fusion.3.own_ref), channel_id=1, source_target_pairs={{0,1},{1,2},{2,3},{3,4},{4,5},{5,6},{6,7},{7,8},{8,9},{9,10},{10,1... | collective-permute-start | bytes 294920 | tf_op jit(solution)/shard_map/ppermute | solution.py:343
  11.2 27.8 %collective-permute-start.2 = (bf16[592,128]{1,0:T(8,128)(2,1)S(1)}, bf16[592,128]{1,0:T(8,128)(2,1)S(1)}, u32[]{:S(2)}, u32[]{:S(2)}) collective-permute-start(bf16[592,128]{1,0:T(8,128)(2,1)S(1)} %pad_maximum_fusion.1), channel_id=1, source_target_pairs={{0,1},{1,2},{2,3},{3,4},{4,5},{5,6},{6,7},{7,8},{8,9},{9,10},{10,1... | collective-permute-start | bytes 454664 | tf_op jit(solution)/shard_map/ppermute | solution.py:343
  15.1 23.9 %collective-permute-start.3 = (bf16[592,128]{1,0:T(8,128)(2,1)S(1)}, bf16[592,128]{1,0:T(8,128)(2,1)S(1)}, u32[]{:S(2)}, u32[]{:S(2)}) collective-permute-start(bf16[592,128]{1,0:T(8,128)(2,1)S(1)} %pad_maximum_fusion.2), channel_id=1, source_target_pairs={{1,0},{2,1},{3,2},{4,3},{5,4},{6,5},{7,6},{8,7},{9,8},{10,9},{11,1... | collective-permute-start | bytes 454664 | tf_op jit(solution)/shard_map/ppermute | solution.py:343
  17.8 1.3 %copy-start.2 = (bf16[192,5184]{1,0:T(8,128)(2,1)}, bf16[192,5184]{1,0:T(8,128)(2,1)S(1)}, u32[]{:S(2)}) copy-start(bf16[192,5184]{1,0:T(8,128)(2,1)S(1)} %turn_weights.1.wt_ref) | copy-start | bytes 5971972
  19.1 1.6 %copy-start.3 = (bf16[192,5184]{1,0:T(8,128)(2,1)S(1)}, bf16[192,5184]{1,0:T(8,128)(2,1)}, u32[]{:S(2)}) copy-start(bf16[192,5184]{1,0:T(8,128)(2,1)} %copy-done.2) | copy-start | bytes 5971972
  20.7 17.7 %copy-start.9 = (bf16[2,192,128]{2,1,0:T(8,128)(2,1)}, bf16[2,192,128]{2,1,0:T(8,128)(2,1)S(1)}, u32[]{:S(2)}) copy-start(bf16[2,192,128]{2,1,0:T(8,128)(2,1)S(1)} %collective-permute-done.low_ref) | copy-start | bytes 294916
  20.7 18.3 %copy-start.4 = (bf16[192,5184]{1,0:T(8,128)(2,1)S(1)}, bf16[192,5184]{1,0:T(8,128)(2,1)}, u32[]{:S(2)}) copy-start(bf16[192,5184]{1,0:T(8,128)(2,1)} %copy-done.2) | copy-start | bytes 5971972
  23.4 0.8 copy-start.7
  24.2 23.9 %copy-start.23 = (s32[2,128]{1,0:T(2,128)S(1)}, s32[2,128]{1,0:T(2,128)}, u32[]{:S(2)}) copy-start(s32[2,128]{1,0:T(2,128)} %label_ref.1) | copy-start | bytes 3076
  24.2 23.9 %all-to-all-start = ((f32[32,8,128]{2,1,0:T(8,128)}), f32[32,8,128]{2,1,0:T(8,128)S(1)}, u32[]{:S(2)}, u32[]{:S(2)}) async-start(f32[32,8,128]{2,1,0:T(8,128)} %get-tuple-element.22), calls=%async_computation | async-start | bytes 262144 | tf_op jit(solution)/shard_map/all_to_all | solution.py:405
  40.3 0.7 copy-start.19
  48.1 1.0 copy-start.8
  49.1 0.9 copy-start.10
  50.0 0.8 copy-start.18
  53.3 0.7 copy-start.5
  54.1 0.7 copy-start.21
  54.8 25.0 %all-to-all-start.1 = ((f32[32,8,128]{2,1,0:T(8,128)}), f32[32,8,128]{2,1,0:T(8,128)S(1)}, u32[]{:S(2)}, u32[]{:S(2)}) async-start(f32[32,8,128]{2,1,0:T(8,128)} %get-tuple-element.24), calls=%async_computation.1 | async-start | bytes 262144 | tf_op jit(solution)/shard_map/all_to_all | solution.py:462
  59.5 18.2 %collective-permute-start.9 = (bf16[4,192,128]{2,1,0:T(8,128)(2,1)}, bf16[4,192,128]{2,1,0:T(8,128)(2,1)S(1)}, u32[]{:S(2)}, u32[]{:S(2)}) collective-permute-start(bf16[4,192,128]{2,1,0:T(8,128)(2,1)} %get-tuple-element.33.own_ref), channel_id=1, source_target_pairs={{0,24},{8,0},{16,8},{24,16},{1,25},{9,1},{17,9},{25,17},{2,26},{10... | collective-permute-start | bytes 589832 | tf_op jit(solution)/shard_map/ppermute | solution.py:343
  62.6 15.8 %collective-permute-start.8 = (bf16[4,192,128]{2,1,0:T(8,128)(2,1)}, bf16[4,192,128]{2,1,0:T(8,128)(2,1)S(1)}, u32[]{:S(2)}, u32[]{:S(2)}) collective-permute-start(bf16[4,192,128]{2,1,0:T(8,128)(2,1)} %get-tuple-element.33.own_ref), channel_id=1, source_target_pairs={{0,16},{8,24},{16,0},{24,8},{1,17},{9,25},{17,1},{25,9},{2,18},{10... | collective-permute-start | bytes 589832 | tf_op jit(solution)/shard_map/ppermute | solution.py:343
  63.3 15.7 %collective-permute-start.7 = (bf16[4,192,128]{2,1,0:T(8,128)(2,1)}, bf16[4,192,128]{2,1,0:T(8,128)(2,1)S(1)}, u32[]{:S(2)}, u32[]{:S(2)}) collective-permute-start(bf16[4,192,128]{2,1,0:T(8,128)(2,1)} %get-tuple-element.33.own_ref), channel_id=1, source_target_pairs={{0,8},{8,16},{16,24},{24,0},{1,9},{9,17},{17,25},{25,1},{2,10},{10... | collective-permute-start | bytes 589832 | tf_op jit(solution)/shard_map/ppermute | solution.py:343
  64.3 7.1 %collective-permute-start.12 = (bf16[4,48,128]{2,1,0:T(8,128)(2,1)S(1)}, bf16[4,48,128]{2,1,0:T(8,128)(2,1)S(1)}, u32[]{:S(2)}, u32[]{:S(2)}) collective-permute-start(bf16[4,48,128]{2,1,0:T(8,128)(2,1)S(1)} %get-tuple-element.42), channel_id=1, source_target_pairs={{0,24},{8,0},{16,8},{24,16},{1,25},{9,1},{17,9},{25,17},{2,26},{10... | collective-permute-start | bytes 147464 | tf_op jit(solution)/shard_map/ppermute | solution.py:343
  66.7 7.8 %collective-permute-start.11 = (bf16[4,48,128]{2,1,0:T(8,128)(2,1)S(1)}, bf16[4,48,128]{2,1,0:T(8,128)(2,1)S(1)}, u32[]{:S(2)}, u32[]{:S(2)}) collective-permute-start(bf16[4,48,128]{2,1,0:T(8,128)(2,1)S(1)} %get-tuple-element.43), channel_id=1, source_target_pairs={{0,16},{8,24},{16,0},{24,8},{1,17},{9,25},{17,1},{25,9},{2,18},{10... | collective-permute-start | bytes 147464 | tf_op jit(solution)/shard_map/ppermute | solution.py:343
  71.4 5.7 %collective-permute-start.10 = (bf16[4,48,128]{2,1,0:T(8,128)(2,1)S(1)}, bf16[4,48,128]{2,1,0:T(8,128)(2,1)S(1)}, u32[]{:S(2)}, u32[]{:S(2)}) collective-permute-start(bf16[4,48,128]{2,1,0:T(8,128)(2,1)S(1)} %get-tuple-element.44), channel_id=1, source_target_pairs={{0,8},{8,16},{16,24},{24,0},{1,9},{9,17},{17,25},{25,1},{2,10},{10... | collective-permute-start | bytes 147464 | tf_op jit(solution)/shard_map/ppermute | solution.py:343
  77.7 0.7 copy-start.11
  78.4 0.7 copy-start.13
  79.1 0.7 copy-start.15
  79.8 0.9 copy-start.12
  80.7 0.9 copy-start.14
  81.6 0.9 copy-start.16
  85.6 22.8 %all-to-all-start.2 = ((bf16[8,96,384]{2,1,0:T(8,128)(2,1)}), bf16[8,96,384]{2,1,0:T(8,128)(2,1)S(1)}, u32[]{:S(2)}, u32[]{:S(2)}) async-start(bf16[8,96,384]{2,1,0:T(8,128)(2,1)} %get-tuple-element.34), calls=%async_computation.2 | async-start | bytes 1179648 | tf_op jit(solution)/shard_map/all_to_all | solution.py:475
  92.0 1.6 %copy-start.1 = (bf16[1,192,5184]{2,1,0:T(8,128)(2,1)S(1)}, bf16[1,192,5184]{2,1,0:T(8,128)(2,1)}, u32[]{:S(2)}) copy-start(bf16[1,192,5184]{2,1,0:T(8,128)(2,1)} %param.17) | copy-start | bytes 5971972
  93.6 1.0 copy-start.6
  94.6 0.9 copy-start.20
  95.5 0.9 copy-start.22
  98.2 4.1 %collective-permute-start.4 = (bf16[2,192,128]{2,1,0:T(8,128)(2,1)S(1)}, bf16[2,192,128]{2,1,0:T(8,128)(2,1)S(1)}, u32[]{:S(2)}, u32[]{:S(2)}) collective-permute-start(bf16[2,192,128]{2,1,0:T(8,128)(2,1)S(1)} %get-tuple-element.30), channel_id=1, source_target_pairs={{0,32},{32,64},{64,96},{96,128},{128,160},{160,192},{192,224},{224... | collective-permute-start | bytes 294920 | tf_op jit(solution)/shard_map/ppermute | solution.py:343
  98.3 4.8 %collective-permute-start.5 = (bf16[2,192,128]{2,1,0:T(8,128)(2,1)S(1)}, bf16[2,192,128]{2,1,0:T(8,128)(2,1)S(1)}, u32[]{:S(2)}, u32[]{:S(2)}) collective-permute-start(bf16[2,192,128]{2,1,0:T(8,128)(2,1)S(1)} %get-tuple-element.31), channel_id=1, source_target_pairs={{0,224},{32,0},{64,32},{96,64},{128,96},{160,128},{192,160},{224,1... | collective-permute-start | bytes 294920 | tf_op jit(solution)/shard_map/ppermute | solution.py:343
  100.0 6.3 %collective-permute-start.6 = (bf16[2,192,128]{2,1,0:T(8,128)(2,1)S(1)}, bf16[2,192,128]{2,1,0:T(8,128)(2,1)S(1)}, u32[]{:S(2)}, u32[]{:S(2)}) collective-permute-start(bf16[2,192,128]{2,1,0:T(8,128)(2,1)S(1)} %get-tuple-element.32), channel_id=1, source_target_pairs={{0,224},{32,192},{64,160},{96,128},{128,96},{160,64},{192,32},{224... | collective-permute-start | bytes 294920 | tf_op jit(solution)/shard_map/ppermute | solution.py:496
  108.4 0.8 copy-start.24

commit v2 on v1

v2 whole, which is shorter than its diff:
```python
import functools

import jax
import jax.numpy as jnp
from jax import lax
from jax.experimental import pallas as pl
from jax.experimental.pallas import tpu as pltpu
from jax.sharding import Mesh
from jax.sharding import PartitionSpec as P

ROWS = 8
COLS = 16
AREA = ROWS * COLS
TAPS = 27
SLABS = ("y", "z")

epsilon = 1e-05
leak_slope = 0.01

F32 = jnp.float32
BF16 = jnp.bfloat16
HBM = pl.BlockSpec(memory_space=pltpu.HBM)
VMEM = pl.BlockSpec(memory_space=pltpu.VMEM)
SMEM = pl.BlockSpec(memory_space=pltpu.SMEM)


def call(body, outs, scratch, flops, moved, *args, smem=0, hbm=0, limit=24):
    specs = [SMEM] * smem + [HBM] * hbm + [VMEM] * (len(args) - smem - hbm)
    shapes = [jax.ShapeDtypeStruct(shape, kind) for shape, kind in outs]
    places = [pltpu.VMEM(shape, kind) for shape, kind in scratch]
    return pl.pallas_call(
        body,
        out_shape=shapes,
        in_specs=specs,
        out_specs=[VMEM] * len(outs),
        scratch_shapes=places + [pltpu.SemaphoreType.DMA] * (hbm > 0),
        compiler_params=pltpu.CompilerParams(vmem_limit_bytes=limit * 1024 * 1024),
        cost_estimate=pl.CostEstimate(flops=flops, bytes_accessed=moved, transcendentals=0),
        name=getattr(body, "__name__", "kernel"),
    )(*args)


def tap_masks():
    cell = lax.broadcasted_iota(jnp.int32, (1, AREA), 1)
    row = cell // COLS
    col = cell % COLS
    masks = {}
    for b in range(3):
        for c in range(3):
            inside = None
            if b != 1:
                inside = row > 0 if b == 0 else row < ROWS - 1
            if c != 1:
                part = col > 0 if c == 0 else col < COLS - 1
                inside = part if inside is None else jnp.logical_and(inside, part)
            masks[(b, c)] = inside
    return masks


def shifted(plane, b, c, masks):
    step = (b - 1) * COLS + (c - 1)
    if step == 0:
        return plane
    moved = pltpu.roll(plane, (-step) % AREA, 1)
    return jnp.where(masks[(b, c)], moved, 0.0)


def full_tile(tile):
    if tile.shape[0] == 8:
        return tile
    return jnp.concatenate([tile, jnp.zeros((8 - tile.shape[0], AREA), F32)], axis=0)


def columns(tile, row):
    square = jnp.concatenate([tile, jnp.zeros((AREA - 8, AREA), F32)], axis=0).T
    return jnp.concatenate([square[:, row : row + 1], square[:64, row + 1 : row + 2]], axis=0)


def packed_tile(cols):
    lane = lax.broadcasted_iota(jnp.int32, (AREA, AREA), 1)
    square = jnp.zeros((AREA, AREA), F32)
    for index, col in enumerate(cols):
        high = jnp.concatenate([col[128:], jnp.zeros((64, 1), F32)], axis=0)
        square = jnp.where(lane == 2 * index, col[:128], square)
        square = jnp.where(lane == 2 * index + 1, high, square)
    return square.T[:8]


def spread_sums(received, row, cells, peers):
    total = jnp.sum(received, axis=0)
    mean = total / peers
    apart = jnp.sum(jnp.square(received - mean[None]), axis=0)
    return columns(mean, row), columns(total, row + 2) + cells * columns(apart, row)


def local_stats(planes_out, cells):
    mean = sum(jnp.sum(p, axis=1, keepdims=True) for p in planes_out) / cells
    squares = sum(jnp.sum(jnp.square(p - mean), axis=1, keepdims=True) for p in planes_out)
    return [mean, squares]


def turn_weights(w_ref, out_ref):
    for pair in range(14):
        width = 384 if pair < 13 else 192
        block = w_ref[:, pair * 384 : pair * 384 + width].T
        if width == 384:
            block = jnp.concatenate([block[:192], block[192:]], axis=1)
        out_ref[:, pair * 384 : pair * 384 + width] = block


def fill_taps(planes, outputs, x_ref, masks, channels, first):
    for q, plane in enumerate(planes):
        wide = plane.astype(F32)
        for b in range(3):
            for c in range(3):
                view = shifted(wide, b, c, masks).astype(BF16)
                for a in range(3):
                    j = q - a
                    if 0 <= j < outputs:
                        tap = 9 * a + 3 * b + c
                        lanes = (first + j) * AREA
                        x_ref[
                            tap * channels : (tap + 1) * channels, lanes : lanes + AREA
                        ] = view


def conv_both(own_ref, low_ref, high_ref, wt_ref, z_ref, send_ref, x_ref):
    masks = tap_masks()
    for which in range(2):
        rows = slice(192 * which, 192 * which + 192)
        planes = [low_ref[rows], own_ref[0, rows], own_ref[1, rows], high_ref[rows]]
        fill_taps(planes, 2, x_ref, masks, 192, 2 * which)
    z = jnp.dot(wt_ref[...], x_ref[...], preferred_element_type=F32)
    outs = [z[:, j * AREA : (j + 1) * AREA] for j in range(4)]
    for j in range(4):
        z_ref[j] = outs[j]
    tile = packed_tile(
        local_stats(outs[:2], 2.0 * AREA) + local_stats(outs[2:], 2.0 * AREA)
    )
    send_ref[...] = jnp.broadcast_to(tile[None], send_ref.shape)


def head_and_sums(
    flag_ref,
    z_ref,
    recv_ref,
    own_ref,
    out_cot_ref,
    skip_cot_ref,
    label_ref,
    affine_ref,
    head_ref,
    head_turned_ref,
    up_ref,
    share_ref,
    scale_ref,
    send_ref,
):
    decoder = flag_ref[0] == 1
    last = flag_ref[1] == 1
    peers = recv_ref.shape[0]
    cells = 2.0 * AREA
    mean, squares = spread_sums(recv_ref[...], 0, cells, peers)
    inv_std = lax.rsqrt(squares / (cells * peers) + epsilon)
    gain = columns(affine_ref[...], 0)
    shift = columns(affine_ref[...], 2)
    scale_ref[...] = jnp.broadcast_to(gain * inv_std, scale_ref.shape)
    classes = head_ref.shape[1]
    class_id = lax.broadcasted_iota(jnp.int32, (classes, AREA), 0)
    sum_grad = jnp.zeros((192, 1), F32)
    sum_cross = jnp.zeros((192, 1), F32)
    for j in range(2):
        normed = (z_ref[j] - mean) * inv_std
        scaled = normed * gain + shift
        activated = jnp.where(scaled > 0, scaled, leak_slope * scaled)
        output = (own_ref[j, :192].astype(F32) + activated).astype(BF16)
        logits = jnp.dot(head_turned_ref[...], output, preferred_element_type=F32)
        raised = jnp.exp(logits - jnp.max(logits, axis=0, keepdims=True))
        prob = raised / jnp.sum(raised, axis=0, keepdims=True)
        hot = jnp.where(class_id == label_ref[j : j + 1, :], 1.0, 0.0)
        delta = (prob - hot).astype(BF16)
        head_cot = jnp.dot(head_ref[...], delta, preferred_element_type=F32)
        upstream = jnp.where(last, head_cot, out_cot_ref[j].astype(F32)) + jnp.where(
            decoder, 0.0, skip_cot_ref[j].astype(F32)
        )
        grad_act = upstream * jnp.where(scaled > 0, 1.0, leak_slope)
        up_ref[j] = upstream
        share_ref[2 * j] = grad_act.astype(BF16)
        share_ref[2 * j + 1] = normed.astype(BF16)
        sum_grad = sum_grad + jnp.sum(grad_act, axis=1, keepdims=True)
        sum_cross = sum_cross + jnp.sum(grad_act * normed, axis=1, keepdims=True)
    tile = packed_tile([sum_grad, sum_cross])
    send_ref[...] = jnp.broadcast_to(tile[None, : send_ref.shape[1]], send_ref.shape)


def forward_out(recv_ref, z_ref, own_ref, affine_ref, out_ref):
    peers = recv_ref.shape[0]
    cells = 2.0 * AREA
    mean, squares = spread_sums(recv_ref[...], 4, cells, peers)
    inv_std = lax.rsqrt(squares / (cells * peers) + epsilon)
    gain = columns(affine_ref[...], 0)
    shift = columns(affine_ref[...], 2)
    for j in range(2):
        scaled = (z_ref[2 + j] - mean) * inv_std * gain + shift
        activated = jnp.where(scaled > 0, scaled, leak_slope * scaled)
        out_ref[j] = (own_ref[j, 192:].astype(F32) + activated).astype(BF16)


def row_taps(refs, taps_ref, wide_ref, turned_ref):
    masks = tap_masks()
    for peer, ref in enumerate(refs):
        for q in range(4):
            wide_ref[...] = ref[q].astype(F32)
            for r in range(6):
                turned_ref[8 * r : 8 * r + 8, :] = wide_ref[pl.ds(r, 8, stride=6), :]
            plane = turned_ref[...]
            for b in range(3):
                for c in range(3):
                    view = shifted(plane, b, c, masks).astype(BF16)
                    for a in range(3):
                        j = q - a
                        if 0 <= j < 2:
                            tap = 9 * a + 3 * b + c
                            lanes = (2 * peer + j) * AREA
                            taps_ref[tap * 48 : (tap + 1) * 48, lanes : lanes + AREA] = view
    taps_ref[1296:1344, :] = jnp.zeros((48, 8 * AREA), BF16)


def kernel_grads(
    recv_ref,
    own_ref,
    a_ref,
    b_ref,
    c_ref,
    rows_own_ref,
    rows_a_ref,
    rows_b_ref,
    rows_c_ref,
    scale_ref,
    out_ref,
    tot_ref,
    taps_ref,
    gz_ref,
    low_ref,
    rest_ref,
    wide_ref,
    turned_ref,
):
    row_taps((rows_own_ref, rows_a_ref, rows_b_ref, rows_c_ref), taps_ref, wide_ref, turned_ref)
    total_cells = 2.0 * AREA * recv_ref.shape[0]
    total = full_tile(jnp.sum(recv_ref[...], axis=0))
    tot_ref[...] = total * (total_cells ** (-0.5))
    sum_grad = columns(total, 0) / total_cells
    sum_cross = columns(total, 2) / total_cells
    scale = scale_ref[...]
    for peer, ref in enumerate((own_ref, a_ref, b_ref, c_ref)):
        for j in range(2):
            act = ref[2 * j].astype(F32)
            normed = ref[2 * j + 1].astype(F32)
            lanes = (2 * peer + j) * AREA
            gz_ref[:, lanes : lanes + AREA] = (
                scale * (act - sum_grad - normed * sum_cross)
            ).astype(BF16)
    grads = lax.dot_general(
        taps_ref[...], gz_ref[...], (((1,), (1,)), ((), ())), preferred_element_type=F32
    )
    low_ref[...] = grads[:, :128]
    rest_ref[...] = jnp.concatenate([grads[:672, 128:], grads[672:, 128:]], axis=1)
    pad = jnp.zeros((12, 384), F32)
    for z in range(8):
        first = low_ref[pl.ds(z, 84, stride=8), :]
        second = low_ref[pl.ds(z + 672, 84, stride=8), :]
        third = rest_ref[pl.ds(z, 84, stride=8), :]
        both = jnp.concatenate([first, second, third], axis=1)
        out_ref[z] = jnp.concatenate([both, pad], axis=0).astype(BF16)


def input_grads(
    flag_ref,
    w_ref,
    recv_ref,
    share_ref,
    up_ref,
    low_ref,
    high_ref,
    scale_ref,
    fwd_out_ref,
    grad_ref,
    skip_ref,
    x_ref,
    w_here_ref,
    sem,
):
    fetch = pltpu.make_async_copy(w_ref, w_here_ref, sem)
    fetch.start()
    decoder = flag_ref[0] == 1
    total_cells = 2.0 * AREA * recv_ref.shape[0]
    masks = tap_masks()
    total = full_tile(jnp.sum(recv_ref[...], axis=0))
    sum_grad = columns(total, 0) / total_cells
    sum_cross = columns(total, 2) / total_cells
    scale = scale_ref[...]
    acts = [low_ref[0], share_ref[0], share_ref[2], high_ref[0]]
    norms = [low_ref[1], share_ref[1], share_ref[3], high_ref[1]]
    for q in range(4):
        grad_z = scale * (acts[q].astype(F32) - sum_grad - norms[q].astype(F32) * sum_cross)
        if q == 0:
            grad_z = jnp.where(flag_ref[2] == 1, grad_z, 0.0)
        if q == 3:
            grad_z = jnp.where(flag_ref[3] == 1, grad_z, 0.0)
        for b in range(3):
            for c in range(3):
                view = shifted(grad_z, 2 - b, 2 - c, masks).astype(BF16)
                for a in range(3):
                    j = q + a - 2
                    if 0 <= j < 2:
                        tap = 9 * a + 3 * b + c
                        x_ref[tap * 192 : (tap + 1) * 192, j * AREA : (j + 1) * AREA] = view
    fetch.wait()
    back = jnp.dot(w_here_ref[...], x_ref[...], preferred_element_type=F32)
    for j in range(2):
        grad = (up_ref[j] + back[:, j * AREA : (j + 1) * AREA]).astype(BF16)
        grad_ref[j] = grad
        skip_ref[j] = jnp.where(
            decoder, grad.astype(F32), fwd_out_ref[j].astype(F32)
        ).astype(BF16)


def sum_rows(scale_out, recv_ref, out_ref, wide_ref):
    total = jnp.sum(recv_ref[...].astype(F32), axis=0) * scale_out

    def block(tap):
        half, row = tap // 14, 6 * (tap % 14)
        low = total[row : row + 6, half * 128 : half * 128 + 128]
        rest = total[row : row + 6, 256 + half * 64 : 320 + half * 64]
        return [low, rest]

    for tap in range(0, TAPS, 2):
        parts = block(tap) + (block(tap + 1) if tap + 1 < TAPS else [])
        width = 192 if tap + 1 == TAPS else 384
        wide_ref[0:6, tap * 192 : tap * 192 + width] = jnp.concatenate(parts, axis=1)
    for r in range(6):
        out_ref[r] = wide_ref[r : r + 1, :]


def pair_rows(values):
    padded = jnp.pad(values, ((0, 2), (0, 64)))
    return padded.reshape(8, AREA)


def moved(block, axis, distance, wrap=True):
    count = lax.axis_size(axis)
    route = [(i, (i + distance) % count) for i in range(count) if wrap or 0 <= i + distance < count]
    return lax.ppermute(block, axis, route)


def per_device(
    fwd_input,
    fwd_skip,
    bwd_input,
    bwd_skip,
    out_cot,
    skip_cot,
    kernel,
    norm_gain,
    norm_shift,
    head_weight,
    labels,
):
    segments = lax.axis_size("segment")
    slabs = lax.axis_size("y") * lax.axis_size("z")
    segment_id = lax.axis_index("segment")
    y_id = lax.axis_index("y")
    slab_id = y_id * lax.axis_size("z") + lax.axis_index("z")
    is_decoder = segment_id * 2 >= segments
    flags = jnp.stack(
        [is_decoder, segment_id == segments - 1, slab_id > 0, slab_id < slabs - 1]
    ).astype(jnp.int32)
    kernel_mat = kernel[0]
    affine = pair_rows(jnp.concatenate([norm_gain, norm_shift], axis=0))

    def by_plane(block):
        return jnp.swapaxes(block[0], 0, 1)

    def joined(block, skip):
        added = (block.astype(F32) + skip.astype(F32)).astype(BF16)
        return by_plane(jnp.where(is_decoder, added, block))

    own = jnp.concatenate([joined(bwd_input, bwd_skip), joined(fwd_input, fwd_skip)], axis=1)
    low = moved(own[1], SLABS, 1, False)
    high = moved(own[0], SLABS, -1, False)
    (turned,) = call(turn_weights, [((192, 5184), BF16)], [], 0, 4 * 192 * 5184, kernel_mat)
    z, stats_send = call(
        conv_both,
        [((4, 192, AREA), F32), ((slabs, 8, AREA), F32)],
        [((5184, 512), BF16)],
        2 * 5184 * 192 * 512,
        5000000,
        own,
        low,
        high,
        turned,
    )
    stats = lax.all_to_all(stats_send, SLABS, 0, 0, tiled=True)
    out_cots = by_plane(out_cot)
    skip_cots = by_plane(skip_cot)
    window = jnp.concatenate([low[None, :192], own[:, :192], high[None, :192]], axis=0)

    def rows_for(distance):
        start = 48 * ((y_id + distance) % 4)
        return lax.dynamic_slice_in_dim(window, start, 48, axis=1)

    row_parts = [rows_for(0)] + [moved(rows_for(d), "y", d) for d in (1, 2, 3)]
    stats, row_parts = lax.optimization_barrier((stats, row_parts))
    upstream, share, scale, sums_send = call(
        head_and_sums,
        [
            ((2, 192, AREA), F32),
            ((4, 192, AREA), BF16),
            ((192, AREA), F32),
            ((slabs, 4, AREA), F32),
        ],
        [],
        4 * 192 * 105 * 512,
        4000000,
        flags,
        z,
        stats,
        own,
        out_cots,
        skip_cots,
        labels,
        affine,
        head_weight,
        head_weight.T,
        smem=1,
    )
    sums = lax.all_to_all(sums_send, SLABS, 0, 0, tiled=True)
    shares = [share] + [moved(share, "y", d) for d in (1, 2, 3)]
    rim_low = moved(share[2:], SLABS, 1, False)
    rim_high = moved(share[:2], SLABS, -1, False)
    (fwd_out,) = call(
        forward_out, [((2, 192, AREA), BF16)], [], 0, 1000000, stats, z, own, affine
    )
    sums, rim_low, rim_high, fwd_out = lax.optimization_barrier((sums, rim_low, rim_high, fwd_out))
    parts, totals = call(
        kernel_grads,
        [((8, 96, 384), BF16), ((8, AREA), F32)],
        [
            ((1344, 1024), BF16),
            ((192, 1024), BF16),
            ((1344, AREA), F32),
            ((672, AREA), F32),
            ((48, AREA), F32),
            ((48, AREA), F32),
        ],
        2 * 1296 * 1024 * 192,
        5000000,
        sums,
        *shares,
        *row_parts,
        scale,
    )
    summed = lax.all_to_all(parts, "z", 0, 0, tiled=True)
    grad_joined, outgoing = call(
        input_grads,
        [((2, 192, AREA), BF16)] * 2,
        [((5184, 256), BF16), ((192, 5184), BF16)],
        2 * 5184 * 192 * 256,
        4000000,
        flags,
        kernel_mat,
        sums,
        share,
        upstream,
        rim_low,
        rim_high,
        scale,
        fwd_out,
        smem=1,
        hbm=1,
        limit=52,
    )
    fwd_out, grad_joined, outgoing = lax.optimization_barrier((fwd_out, grad_joined, outgoing))
    prev_block = moved(grad_joined, "segment", -1)
    next_block = moved(fwd_out, "segment", 1)
    mirrored = lax.ppermute(outgoing, "segment", [(i, segments - 1 - i) for i in range(segments)])
    total_cells = float(2 * slabs * AREA)
    (kernel_grad,) = call(
        functools.partial(sum_rows, total_cells ** (-0.5)),
        [((6, 1, 5184), F32)],
        [((8, 5184), F32)],
        0,
        1000000,
        summed,
    )
    flat = totals.reshape(-1)

    def by_channel(block):
        return jnp.swapaxes(block, 0, 1)[None]

    return (
        by_channel(next_block),
        by_channel(prev_block),
        by_channel(mirrored),
        jnp.swapaxes(kernel_grad, 0, 1),
        flat[256:448][None],
        flat[:192][None],
    )


def solution(mesh):
    grid = Mesh(mesh.devices.reshape(mesh.devices.shape[0], 4, 8), ("segment", "y", "z"))
    field = P("segment", None, SLABS, None)
    in_specs = (field,) * 6 + (
        P("segment", None, None),
        P("segment", None),
        P("segment", None),
        P(),
        P(SLABS, None),
    )
    out_specs = (
        field,
        field,
        field,
        P("segment", SLABS, None),
        P("segment", None),
        P("segment", None),
    )
    return jax.shard_map(
        per_device, mesh=grid, in_specs=in_specs, out_specs=out_specs, check_vma=False
    )
```

time: 114 us -> 85 us (0.75)
  local copies, waits for them, and re-layouts: 26.3 us -> 4.59 us
  other arithmetic: 3.74 us -> 1.24 us
  waiting for transfers between devices: 19.7 us -> 17.2 us
  Pallas kernels: 15 us -> 13.4 us
    unnamed x61 -> x18, local copies, waits for them, and re-layouts: 24.4 us -> 3.93 us
    all_to_all x1, waiting for transfers between devices: 7.11 us -> 1.65 us  [per_device(): stats = lax.all_to_all(stats_send, SLABS, 0, 0, tiled=True)]
    all_to_all x1, starting transfers between devices: 3.85 us -> 7.05 us  [per_device(): sums = lax.all_to_all(sums_send, SLABS, 0, 0, tiled=True)]
    ppermute x12, waiting for transfers between devices: 8.79 us -> 11.2 us  [moved(): return lax.ppermute(block, axis, route)]
    all_to_all x1, starting transfers between devices: 13.5 us -> 11.3 us  [per_device(): stats = lax.all_to_all(stats_send, SLABS, 0, 0, tiled=True)]
    pallas_call x1 -> x0, Pallas kernels: 1.94 us -> none  [per_device(): pl.pallas_call(lambda recv, out: sum_rows(total_cells ** (-0.5), recv, ou...]
    ppermute x12, starting transfers between devices: 23.3 us -> 21.8 us  [moved(): return lax.ppermute(block, axis, route)]
    slice x2 -> x1, local copies, waits for them, and re-layouts: 1.25 us -> 0.02 us  [per_device(): rim_high = moved(share[:2], SLABS, -1, False)]
  transfers between devices with their start and end apart: 16 -> 16, of which waited for: 7 -> 9; matrix products, arithmetic and copies ran while one was open for 8% -> 4% of each run, Pallas kernels for 7% -> 6%
where the time goes in v2:
time: 85 us; the launch traced here: 84.5 us
  starting transfers between devices  47.2 us (56%)
  waiting for transfers between devices  17.2 us (20%)
  Pallas kernels  13.4 us (16%)
  local copies, waits for them, and re-layouts  4.59 us (5%)
  other arithmetic  1.24 us (1%)
  between operations  0.98 us (1%)
    ppermute x12, starting transfers between devices, moved(): return lax.ppermute(block, axis, route)  21.8 us
    pallas_call x7, Pallas kernels, call(): pl.pallas_call(body, out_shape=shapes, in_specs=specs, out_specs=[VMEM] *...  13.4 us
    all_to_all x1, starting transfers between devices, per_device(): stats = lax.all_to_all(stats_send, SLABS, 0, 0, tiled=True)  11.3 us
    ppermute x12, waiting for transfers between devices, moved(): return lax.ppermute(block, axis, route)  11.2 us
    all_to_all x1, starting transfers between devices, per_device(): sums = lax.all_to_all(sums_send, SLABS, 0, 0, tiled=True)  7.05 us
    all_to_all x1, starting transfers between devices, per_device(): summed = lax.all_to_all(parts, 'z', 0, 0, tiled=True)  6.96 us
    unnamed x18, local copies, waits for them, and re-layouts  3.93 us
    ppermute x1, waiting for transfers between devices, per_device(): lax.ppermute(outgoing, 'segment', [(i, segments - 1 - i) for i in range(s...  2.51 us
  transfers between devices with their start and end apart: 16, of which 9 were waited for; matrix products, arithmetic and copies ran while one was open for 4% of the time, Pallas kernels for 6%

profile of v2, /device:TPU:6, one launch (start us, length us, event | category | flops | bytes accessed | tf_op | source)
XLA Modules:
  0.0 84.5 jit_solution(13920653317371681058)
XLA Ops:
  0.6 1.1 %fusion.2 = (bf16[2,192,128]{2,1,0:T(8,128)(2,1)S(1)}, bf16[2,192,128]{2,1,0:T(8,128)(2,1)S(1)}) fusion(bf16[1,192,2,128]{3,2,1,0:T(2,128)(2,1)} %param.12, bf16[1,192,2,128]{3,2,1,0:T(2,128)(2,1)} %param.11, pred[]{:T(512)} %ge.3, bf16[1,192,2,128]{3,2,1,0:T(2,128)(2,1)} %param.14, bf16[1,192,2,128]{3,2,1,0:T(2,128)(2,1)} %param.13), kind=kLoop, calls=%fused_computation.10 | loop fusion | flops 491520 | bytes 589825 | tf_op jit(solution)/shard_map/transpose | solution.py:383
  1.8 3.8 %collective-permute-start = (bf16[384,128]{1,0:T(8,128)(2,1)S(1)}, bf16[384,128]{1,0:T(8,128)(2,1)S(1)}, u32[]{:S(2)}, u32[]{:S(2)}) collective-permute-start(bf16[384,128]{1,0:T(8,128)(2,1)S(1)} %get-tuple-element.63), channel_id=1, source_target_pairs={{0,1},{1,2},{2,3},{3,4},{4,5},{5,6},{6,7},{7,8},{8,9},{9,10},{10,1... | collective-permute-start | bytes 294920 | tf_op jit(solution)/shard_map/ppermute | solution.py:354
  5.6 1.3 %collective-permute-start.1 = (bf16[384,128]{1,0:T(8,128)(2,1)S(1)}, bf16[384,128]{1,0:T(8,128)(2,1)S(1)}, u32[]{:S(2)}, u32[]{:S(2)}) collective-permute-start(bf16[384,128]{1,0:T(8,128)(2,1)S(1)} %get-tuple-element.62), channel_id=1, source_target_pairs={{1,0},{2,1},{3,2},{4,3},{5,4},{6,5},{7,6},{8,7},{9,8},{10,9},{11,1... | collective-permute-start | bytes 294920 | tf_op jit(solution)/shard_map/ppermute | solution.py:354
  7.0 0.0 copy-start
  7.0 1.6 %copy-done = bf16[1,192,5184]{2,1,0:T(8,128)(2,1)S(1)} copy-done((bf16[1,192,5184]{2,1,0:T(8,128)(2,1)S(1)}, bf16[1,192,5184]{2,1,0:T(8,128)(2,1)}, u32[]{:S(2)}) %copy-start) | copy-done | bytes 1990680
  8.5 0.0 copy-start.3
  8.6 0.0 copy-start.4
  8.6 0.0 copy-start.5
  8.6 0.0 copy-start.6
  8.6 1.1 %turn_weights.1.wt_ref = bf16[192,5184]{1,0:T(8,128)(2,1)S(1)} custom-call(bf16[192,5184]{1,0:T(8,128)(2,1)S(1)} %bitcast.44), custom_call_target="tpu_custom_call" | custom-call | bytes 3981312 | tf_op jit(solution)/shard_map/turn_weights/pallas_call | solution.py:31
  9.7 0.0 copy-done.3
  9.7 0.0 copy-done.4
  9.8 0.0 copy-done.5
  9.8 0.0 copy-done.6
  9.8 0.0 copy-start.1
  9.8 0.0 copy-start.2
  9.8 0.0 collective-permute-done.low_ref
  9.8 2.3 %collective-permute-done.1.high_ref = bf16[384,128]{1,0:T(8,128)(2,1)S(1)} collective-permute-done((bf16[384,128]{1,0:T(8,128)(2,1)S(1)}, bf16[384,128]{1,0:T(8,128)(2,1)S(1)}, u32[]{:S(2)}, u32[]{:S(2)}) %collective-permute-start.1) | collective-permute-done | bytes 98336 | tf_op jit(solution)/shard_map/ppermute | solution.py:354
  12.1 2.8 %conv_both.1 = (f32[4,192,128]{2,1,0:T(8,128)S(1)}, f32[32,8,128]{2,1,0:T(8,128)}) custom-call(bf16[2,384,128]{2,1,0:T(8,128)(2,1)S(1)} %pad_maximum_fusion.own_ref, bf16[384,128]{1,0:T(8,128)(2,1)S(1)} %collective-permute-done.low_ref, bf16[384,128]{1,0:T(8,128)(2,1)S(1)} %collective-permute-done.1.high_ref, bf16[192,5184]{1,0:T(8,128)(2,1)S(1)} %turn_weights.1.wt_ref), custom_call_target="tpu_custom_call" | custom-call | flops 1019215872 | bytes 5000000 | tf_op jit(solution)/shard_map/conv_both/pallas_call | solution.py:31
  14.9 11.3 %all-to-all-start = ((f32[32,8,128]{2,1,0:T(8,128)}), f32[32,8,128]{2,1,0:T(8,128)S(1)}, u32[]{:S(2)}, u32[]{:S(2)}) async-start(f32[32,8,128]{2,1,0:T(8,128)} %get-tuple-element.29), calls=%async_computation | async-start | bytes 262144 | tf_op jit(solution)/shard_map/all_to_all | solution.py:404
  26.4 1.9 %collective-permute-start.2 = (bf16[4,48,128]{2,1,0:T(8,128)(2,1)S(1)}, bf16[4,48,128]{2,1,0:T(8,128)(2,1)S(1)}, u32[]{:S(2)}, u32[]{:S(2)}) collective-permute-start(bf16[4,48,128]{2,1,0:T(8,128)(2,1)S(1)} %get-tuple-element.60), channel_id=1, source_target_pairs={{0,8},{8,16},{16,24},{24,0},{1,9},{9,17},{17,25},{25,1},{2,10},{10... | collective-permute-start | bytes 147464 | tf_op jit(solution)/shard_map/ppermute | solution.py:354
  28.2 2.7 %collective-permute-start.3 = (bf16[4,48,128]{2,1,0:T(8,128)(2,1)S(1)}, bf16[4,48,128]{2,1,0:T(8,128)(2,1)S(1)}, u32[]{:S(2)}, u32[]{:S(2)}) collective-permute-start(bf16[4,48,128]{2,1,0:T(8,128)(2,1)S(1)} %get-tuple-element.59), channel_id=1, source_target_pairs={{0,16},{8,24},{16,0},{24,8},{1,17},{9,25},{17,1},{25,9},{2,18},{10... | collective-permute-start | bytes 147464 | tf_op jit(solution)/shard_map/ppermute | solution.py:354
  31.0 1.4 %collective-permute-start.4 = (bf16[4,48,128]{2,1,0:T(8,128)(2,1)S(1)}, bf16[4,48,128]{2,1,0:T(8,128)(2,1)S(1)}, u32[]{:S(2)}, u32[]{:S(2)}) collective-permute-start(bf16[4,48,128]{2,1,0:T(8,128)(2,1)S(1)} %get-tuple-element.58), channel_id=1, source_target_pairs={{0,24},{8,0},{16,8},{24,16},{1,25},{9,1},{17,9},{25,17},{2,26},{10... | collective-permute-start | bytes 147464 | tf_op jit(solution)/shard_map/ppermute | solution.py:354
  32.4 0.1 add_convert_fusion.2.flag_ref
  32.5 0.0 copy-done.1
  32.5 0.1 copy.25
  32.6 0.0 collective-permute-done.2.rows_a_ref
  32.6 1.4 %collective-permute-done.3.rows_b_ref = bf16[4,48,128]{2,1,0:T(8,128)(2,1)S(1)} collective-permute-done((bf16[4,48,128]{2,1,0:T(8,128)(2,1)S(1)}, bf16[4,48,128]{2,1,0:T(8,128)(2,1)S(1)}, u32[]{:S(2)}, u32[]{:S(2)}) %collective-permute-start.3) | collective-permute-done | bytes 49184 | tf_op jit(solution)/shard_map/ppermute | solution.py:354
  34.0 1.1 %collective-permute-done.4.rows_c_ref = bf16[4,48,128]{2,1,0:T(8,128)(2,1)S(1)} collective-permute-done((bf16[4,48,128]{2,1,0:T(8,128)(2,1)S(1)}, bf16[4,48,128]{2,1,0:T(8,128)(2,1)S(1)}, u32[]{:S(2)}, u32[]{:S(2)}) %collective-permute-start.4) | collective-permute-done | bytes 49184 | tf_op jit(solution)/shard_map/ppermute | solution.py:354
  35.0 1.7 %all-to-all-done.recv_ref = f32[32,8,128]{2,1,0:T(8,128)S(1)} async-done(((f32[32,8,128]{2,1,0:T(8,128)}), f32[32,8,128]{2,1,0:T(8,128)S(1)}, u32[]{:S(2)}, u32[]{:S(2)}) %all-to-all-start) | async-done | bytes 131104 | tf_op jit(solution)/shard_map/all_to_all | solution.py:404
  36.7 0.0 copy-done.2
  36.7 2.5 %head_and_sums.1 = (f32[2,192,128]{2,1,0:T(8,128)S(1)}, bf16[4,192,128]{2,1,0:T(8,128)(2,1)S(1)}, f32[192,128]{1,0:T(8,128)S(1)}, f32[32,4,128]{2,1,0:T(4,128)}) custom-call(s32[4]{0:T(128)S(1)} %add_convert_fusion.2.flag_ref, f32[4,192,128]{2,1,0:T(8,128)S(1)} %get-tuple-element.28.z_ref, f32[32,8,128]{2,1,0:T(8,128)S(1)} %all-to-all-done.recv_ref, ...), custom_call_target="tpu_custom_call" | custom-call | flops 41287680 | bytes 4000000 | tf_op jit(solution)/shard_map/head_and_sums/pallas_call | solution.py:31
  39.2 0.6 collective-permute-start.10
  39.8 2.0 %collective-permute-start.11 = (bf16[4,192,128]{2,1,0:T(8,128)(2,1)S(1)}, bf16[4,192,128]{2,1,0:T(8,128)(2,1)S(1)}, u32[]{:S(2)}, u32[]{:S(2)}) collective-permute-start(bf16[4,192,128]{2,1,0:T(8,128)(2,1)S(1)} %get-tuple-element.32.share_ref.own_ref), channel_id=1, source_target_pairs={{0,16},{8,24},{16,0},{24,8},{1,17},{9,25},{17,1},{25,9},{2,18},{10... | collective-permute-start | bytes 589832 | tf_op jit(solution)/shard_map/ppermute | solution.py:354
  41.8 1.3 %collective-permute-start.12 = (bf16[4,192,128]{2,1,0:T(8,128)(2,1)S(1)}, bf16[4,192,128]{2,1,0:T(8,128)(2,1)S(1)}, u32[]{:S(2)}, u32[]{:S(2)}) collective-permute-start(bf16[4,192,128]{2,1,0:T(8,128)(2,1)S(1)} %get-tuple-element.32.share_ref.own_ref), channel_id=1, source_target_pairs={{0,24},{8,0},{16,8},{24,16},{1,25},{9,1},{17,9},{25,17},{2,26},{10... | collective-permute-start | bytes 589832 | tf_op jit(solution)/shard_map/ppermute | solution.py:354
  43.1 7.1 %all-to-all-start.1 = ((f32[32,4,128]{2,1,0:T(4,128)}), f32[32,4,128]{2,1,0:T(4,128)S(1)}, u32[]{:S(2)}, u32[]{:S(2)}) async-start(f32[32,4,128]{2,1,0:T(4,128)} %get-tuple-element.31), calls=%async_computation.1 | async-start | bytes 131072 | tf_op jit(solution)/shard_map/all_to_all | solution.py:438
  50.2 3.7 %collective-permute-start.5 = (bf16[2,192,128]{2,1,0:T(8,128)(2,1)S(1)}, bf16[2,192,128]{2,1,0:T(8,128)(2,1)S(1)}, u32[]{:S(2)}, u32[]{:S(2)}) collective-permute-start(bf16[2,192,128]{2,1,0:T(8,128)(2,1)S(1)} %get-tuple-element.57), channel_id=1, source_target_pairs={{0,1},{1,2},{2,3},{3,4},{4,5},{5,6},{6,7},{7,8},{8,9},{9,10},{10,1... | collective-permute-start | bytes 294920 | tf_op jit(solution)/shard_map/ppermute | solution.py:354
  53.9 1.3 %collective-permute-start.6 = (bf16[2,192,128]{2,1,0:T(8,128)(2,1)S(1)}, bf16[2,192,128]{2,1,0:T(8,128)(2,1)S(1)}, u32[]{:S(2)}, u32[]{:S(2)}) collective-permute-start(bf16[2,192,128]{2,1,0:T(8,128)(2,1)S(1)} %get-tuple-element.56), channel_id=1, source_target_pairs={{1,0},{2,1},{3,2},{4,3},{5,4},{6,5},{7,6},{8,7},{9,8},{10,9},{11,1... | collective-permute-start | bytes 294920 | tf_op jit(solution)/shard_map/ppermute | solution.py:354
  55.2 0.5 forward_out.1.fwd_out_ref
  55.7 0.4 collective-permute-done.5.low_ref
  56.1 4.3 %collective-permute-done.6.high_ref = bf16[2,192,128]{2,1,0:T(8,128)(2,1)S(1)} collective-permute-done((bf16[2,192,128]{2,1,0:T(8,128)(2,1)S(1)}, bf16[2,192,128]{2,1,0:T(8,128)(2,1)S(1)}, u32[]{:S(2)}, u32[]{:S(2)}) %collective-permute-start.6) | collective-permute-done | bytes 98336 | tf_op jit(solution)/shard_map/ppermute | solution.py:354
  60.4 0.0 all-to-all-done.1.recv_ref
  60.4 0.0 collective-permute-done.10.a_ref
  60.4 0.0 collective-permute-done.11.b_ref
  60.4 0.0 collective-permute-done.12.c_ref
  60.5 2.3 %kernel_grads.1 = (bf16[8,96,384]{2,1,0:T(8,128)(2,1)}, f32[8,128]{1,0:T(8,128)S(1)}) custom-call(f32[32,4,128]{2,1,0:T(4,128)S(1)} %all-to-all-done.1.recv_ref, bf16[4,192,128]{2,1,0:T(8,128)(2,1)S(1)} %get-tuple-element.32.share_ref.own_ref, bf16[4,192,128]{2,1,0:T(8,128)(2,1)S(1)} %collective-permute-done.10.a_ref, ...), custom_call_target="tpu_custom_call" | custom-call | flops 509607936 | bytes 5000000 | tf_op jit(solution)/shard_map/kernel_grads/pallas_call | solution.py:31
  62.7 7.0 %all-to-all-start.2 = ((bf16[8,96,384]{2,1,0:T(8,128)(2,1)}), bf16[8,96,384]{2,1,0:T(8,128)(2,1)S(1)}, u32[]{:S(2)}, u32[]{:S(2)}) async-start(bf16[8,96,384]{2,1,0:T(8,128)(2,1)} %get-tuple-element.48), calls=%async_computation.2 | async-start | bytes 1179648 | tf_op jit(solution)/shard_map/all_to_all | solution.py:464
  69.7 3.4 %input_grads.1 = (bf16[2,192,128]{2,1,0:T(8,128)(2,1)S(1)}, bf16[2,192,128]{2,1,0:T(8,128)(2,1)S(1)}) custom-call(s32[4]{0:T(128)S(1)} %add_convert_fusion.2.flag_ref, bf16[192,5184]{1,0:T(8,128)(2,1)} %bitcast.43, f32[32,4,128]{2,1,0:T(4,128)S(1)} %all-to-all-done.1.recv_ref, bf16[4,192,128]{2,1,0:T(8,128)(2,1)S(1)} %get-tuple-element.32.share_ref.own_ref, ...), custom_call_target="tpu_custom_call" | custom-call | flops 509607936 | bytes 4000000 | tf_op jit(solution)/shard_map/input_grads/pallas_call | solution.py:31
  73.1 0.0 collective-permute-start.7
  73.1 1.7 %collective-permute-start.8 = (bf16[2,192,128]{2,1,0:T(8,128)(2,1)S(1)}, bf16[2,192,128]{2,1,0:T(8,128)(2,1)S(1)}, u32[]{:S(2)}, u32[]{:S(2)}) collective-permute-start(bf16[2,192,128]{2,1,0:T(8,128)(2,1)S(1)} %get-tuple-element.42), channel_id=1, source_target_pairs={{0,224},{32,0},{64,32},{96,64},{128,96},{160,128},{192,160},{224,1... | collective-permute-start | bytes 294920 | tf_op jit(solution)/shard_map/ppermute | solution.py:354
  74.8 0.0 collective-permute-start.9
  74.9 0.6 fusion.9
  75.4 1.7 %collective-permute-done.7 = bf16[2,192,128]{2,1,0:T(8,128)(2,1)S(1)} collective-permute-done((bf16[2,192,128]{2,1,0:T(8,128)(2,1)S(1)}, bf16[2,192,128]{2,1,0:T(8,128)(2,1)S(1)}, u32[]{:S(2)}, u32[]{:S(2)}) %collective-permute-start.7) | collective-permute-done | bytes 98336 | tf_op jit(solution)/shard_map/ppermute | solution.py:354
  77.1 0.7 copy.26
  77.9 0.0 collective-permute-done.8
  77.9 0.7 copy.27
  78.6 2.5 %collective-permute-done.9 = bf16[2,192,128]{2,1,0:T(8,128)(2,1)S(1)} collective-permute-done((bf16[2,192,128]{2,1,0:T(8,128)(2,1)S(1)}, bf16[2,192,128]{2,1,0:T(8,128)(2,1)S(1)}, u32[]{:S(2)}, u32[]{:S(2)}) %collective-permute-start.9) | collective-permute-done | bytes 98336 | tf_op jit(solution)/shard_map/ppermute | solution.py:487
  81.1 0.7 copy.28
  81.9 1.8 %all-to-all-done.2.recv_ref = bf16[8,96,384]{2,1,0:T(8,128)(2,1)S(1)} async-done(((bf16[8,96,384]{2,1,0:T(8,128)(2,1)}), bf16[8,96,384]{2,1,0:T(8,128)(2,1)S(1)}, u32[]{:S(2)}, u32[]{:S(2)}) %all-to-all-start.2) | async-done | bytes 589856 | tf_op jit(solution)/shard_map/all_to_all | solution.py:464
  83.7 0.8 kernel.1
  (10 shorter events, 0.2 us)
Async XLA Ops:
  1.8 8.1 %collective-permute-start = (bf16[384,128]{1,0:T(8,128)(2,1)S(1)}, bf16[384,128]{1,0:T(8,128)(2,1)S(1)}, u32[]{:S(2)}, u32[]{:S(2)}) collective-permute-start(bf16[384,128]{1,0:T(8,128)(2,1)S(1)} %get-tuple-element.63), channel_id=1, source_target_pairs={{0,1},{1,2},{2,3},{3,4},{4,5},{5,6},{6,7},{7,8},{8,9},{9,10},{10,1... | collective-permute-start | bytes 294920 | tf_op jit(solution)/shard_map/ppermute | solution.py:354
  5.6 6.5 %collective-permute-start.1 = (bf16[384,128]{1,0:T(8,128)(2,1)S(1)}, bf16[384,128]{1,0:T(8,128)(2,1)S(1)}, u32[]{:S(2)}, u32[]{:S(2)}) collective-permute-start(bf16[384,128]{1,0:T(8,128)(2,1)S(1)} %get-tuple-element.62), channel_id=1, source_target_pairs={{1,0},{2,1},{3,2},{4,3},{5,4},{6,5},{7,6},{8,7},{9,8},{10,9},{11,1... | collective-permute-start | bytes 294920 | tf_op jit(solution)/shard_map/ppermute | solution.py:354
  7.0 1.6 %copy-start = (bf16[1,192,5184]{2,1,0:T(8,128)(2,1)S(1)}, bf16[1,192,5184]{2,1,0:T(8,128)(2,1)}, u32[]{:S(2)}) copy-start(bf16[1,192,5184]{2,1,0:T(8,128)(2,1)} %param.17) | copy-start | bytes 5971972
  8.5 1.2 %copy-start.3 = (bf16[1,192,2,128]{3,2,1,0:T(2,128)(2,1)S(1)}, bf16[1,192,2,128]{3,2,1,0:T(2,128)(2,1)}, u32[]{:S(2)}) copy-start(bf16[1,192,2,128]{3,2,1,0:T(2,128)(2,1)} %param.16) | copy-start | bytes 294916
  8.6 1.2 %copy-start.4 = (bf16[1,192,2,128]{3,2,1,0:T(2,128)(2,1)S(1)}, bf16[1,192,2,128]{3,2,1,0:T(2,128)(2,1)}, u32[]{:S(2)}) copy-start(bf16[1,192,2,128]{3,2,1,0:T(2,128)(2,1)} %param.15) | copy-start | bytes 294916
  8.6 1.2 %copy-start.5 = (f32[1,192]{1,0:T(1,128)S(1)}, f32[1,192]{1,0:T(1,128)}, u32[]{:S(2)}) copy-start(f32[1,192]{1,0:T(1,128)} %param.19) | copy-start | bytes 2308
  8.6 1.2 %copy-start.6 = (f32[1,192]{1,0:T(1,128)S(1)}, f32[1,192]{1,0:T(1,128)}, u32[]{:S(2)}) copy-start(f32[1,192]{1,0:T(1,128)} %param.18) | copy-start | bytes 2308
  9.8 22.7 %copy-start.1 = (bf16[192,105]{1,0:T(8,128)(2,1)S(1)}, bf16[192,105]{1,0:T(8,128)(2,1)}, u32[]{:S(2)}) copy-start(bf16[192,105]{1,0:T(8,128)(2,1)} %head_ref.1) | copy-start | bytes 120964
  9.8 26.9 %copy-start.2 = (s32[2,128]{1,0:T(2,128)S(1)}, s32[2,128]{1,0:T(2,128)}, u32[]{:S(2)}) copy-start(s32[2,128]{1,0:T(2,128)} %label_ref.1) | copy-start | bytes 3076
  14.9 21.8 %all-to-all-start = ((f32[32,8,128]{2,1,0:T(8,128)}), f32[32,8,128]{2,1,0:T(8,128)S(1)}, u32[]{:S(2)}, u32[]{:S(2)}) async-start(f32[32,8,128]{2,1,0:T(8,128)} %get-tuple-element.29), calls=%async_computation | async-start | bytes 262144 | tf_op jit(solution)/shard_map/all_to_all | solution.py:404
  26.4 6.2 %collective-permute-start.2 = (bf16[4,48,128]{2,1,0:T(8,128)(2,1)S(1)}, bf16[4,48,128]{2,1,0:T(8,128)(2,1)S(1)}, u32[]{:S(2)}, u32[]{:S(2)}) collective-permute-start(bf16[4,48,128]{2,1,0:T(8,128)(2,1)S(1)} %get-tuple-element.60), channel_id=1, source_target_pairs={{0,8},{8,16},{16,24},{24,0},{1,9},{9,17},{17,25},{25,1},{2,10},{10... | collective-permute-start | bytes 147464 | tf_op jit(solution)/shard_map/ppermute | solution.py:354
  28.2 5.7 %collective-permute-start.3 = (bf16[4,48,128]{2,1,0:T(8,128)(2,1)S(1)}, bf16[4,48,128]{2,1,0:T(8,128)(2,1)S(1)}, u32[]{:S(2)}, u32[]{:S(2)}) collective-permute-start(bf16[4,48,128]{2,1,0:T(8,128)(2,1)S(1)} %get-tuple-element.59), channel_id=1, source_target_pairs={{0,16},{8,24},{16,0},{24,8},{1,17},{9,25},{17,1},{25,9},{2,18},{10... | collective-permute-start | bytes 147464 | tf_op jit(solution)/shard_map/ppermute | solution.py:354
  31.0 4.1 %collective-permute-start.4 = (bf16[4,48,128]{2,1,0:T(8,128)(2,1)S(1)}, bf16[4,48,128]{2,1,0:T(8,128)(2,1)S(1)}, u32[]{:S(2)}, u32[]{:S(2)}) collective-permute-start(bf16[4,48,128]{2,1,0:T(8,128)(2,1)S(1)} %get-tuple-element.58), channel_id=1, source_target_pairs={{0,24},{8,0},{16,8},{24,16},{1,25},{9,1},{17,9},{25,17},{2,26},{10... | collective-permute-start | bytes 147464 | tf_op jit(solution)/shard_map/ppermute | solution.py:354
  39.2 21.3 %collective-permute-start.10 = (bf16[4,192,128]{2,1,0:T(8,128)(2,1)S(1)}, bf16[4,192,128]{2,1,0:T(8,128)(2,1)S(1)}, u32[]{:S(2)}, u32[]{:S(2)}) collective-permute-start(bf16[4,192,128]{2,1,0:T(8,128)(2,1)S(1)} %get-tuple-element.32.share_ref.own_ref), channel_id=1, source_target_pairs={{0,8},{8,16},{16,24},{24,0},{1,9},{9,17},{17,25},{25,1},{2,10},{10... | collective-permute-start | bytes 589832 | tf_op jit(solution)/shard_map/ppermute | solution.py:354
  39.8 20.6 %collective-permute-start.11 = (bf16[4,192,128]{2,1,0:T(8,128)(2,1)S(1)}, bf16[4,192,128]{2,1,0:T(8,128)(2,1)S(1)}, u32[]{:S(2)}, u32[]{:S(2)}) collective-permute-start(bf16[4,192,128]{2,1,0:T(8,128)(2,1)S(1)} %get-tuple-element.32.share_ref.own_ref), channel_id=1, source_target_pairs={{0,16},{8,24},{16,0},{24,8},{1,17},{9,25},{17,1},{25,9},{2,18},{10... | collective-permute-start | bytes 589832 | tf_op jit(solution)/shard_map/ppermute | solution.py:354
  41.8 18.7 %collective-permute-start.12 = (bf16[4,192,128]{2,1,0:T(8,128)(2,1)S(1)}, bf16[4,192,128]{2,1,0:T(8,128)(2,1)S(1)}, u32[]{:S(2)}, u32[]{:S(2)}) collective-permute-start(bf16[4,192,128]{2,1,0:T(8,128)(2,1)S(1)} %get-tuple-element.32.share_ref.own_ref), channel_id=1, source_target_pairs={{0,24},{8,0},{16,8},{24,16},{1,25},{9,1},{17,9},{25,17},{2,26},{10... | collective-permute-start | bytes 589832 | tf_op jit(solution)/shard_map/ppermute | solution.py:354
  43.1 17.3 %all-to-all-start.1 = ((f32[32,4,128]{2,1,0:T(4,128)}), f32[32,4,128]{2,1,0:T(4,128)S(1)}, u32[]{:S(2)}, u32[]{:S(2)}) async-start(f32[32,4,128]{2,1,0:T(4,128)} %get-tuple-element.31), calls=%async_computation.1 | async-start | bytes 131072 | tf_op jit(solution)/shard_map/all_to_all | solution.py:438
  50.2 5.9 %collective-permute-start.5 = (bf16[2,192,128]{2,1,0:T(8,128)(2,1)S(1)}, bf16[2,192,128]{2,1,0:T(8,128)(2,1)S(1)}, u32[]{:S(2)}, u32[]{:S(2)}) collective-permute-start(bf16[2,192,128]{2,1,0:T(8,128)(2,1)S(1)} %get-tuple-element.57), channel_id=1, source_target_pairs={{0,1},{1,2},{2,3},{3,4},{4,5},{5,6},{6,7},{7,8},{8,9},{9,10},{10,1... | collective-permute-start | bytes 294920 | tf_op jit(solution)/shard_map/ppermute | solution.py:354
  53.9 6.5 %collective-permute-start.6 = (bf16[2,192,128]{2,1,0:T(8,128)(2,1)S(1)}, bf16[2,192,128]{2,1,0:T(8,128)(2,1)S(1)}, u32[]{:S(2)}, u32[]{:S(2)}) collective-permute-start(bf16[2,192,128]{2,1,0:T(8,128)(2,1)S(1)} %get-tuple-element.56), channel_id=1, source_target_pairs={{1,0},{2,1},{3,2},{4,3},{5,4},{6,5},{7,6},{8,7},{9,8},{10,9},{11,1... | collective-permute-start | bytes 294920 | tf_op jit(solution)/shard_map/ppermute | solution.py:354
  62.7 21.0 %all-to-all-start.2 = ((bf16[8,96,384]{2,1,0:T(8,128)(2,1)}), bf16[8,96,384]{2,1,0:T(8,128)(2,1)S(1)}, u32[]{:S(2)}, u32[]{:S(2)}) async-start(bf16[8,96,384]{2,1,0:T(8,128)(2,1)} %get-tuple-element.48), calls=%async_computation.2 | async-start | bytes 1179648 | tf_op jit(solution)/shard_map/all_to_all | solution.py:464
  73.1 4.1 %collective-permute-start.7 = (bf16[2,192,128]{2,1,0:T(8,128)(2,1)S(1)}, bf16[2,192,128]{2,1,0:T(8,128)(2,1)S(1)}, u32[]{:S(2)}, u32[]{:S(2)}) collective-permute-start(bf16[2,192,128]{2,1,0:T(8,128)(2,1)S(1)} %forward_out.1.fwd_out_ref), channel_id=1, source_target_pairs={{0,32},{32,64},{64,96},{96,128},{128,160},{160,192},{192,224},{224... | collective-permute-start | bytes 294920 | tf_op jit(solution)/shard_map/ppermute | solution.py:354
  73.1 4.8 %collective-permute-start.8 = (bf16[2,192,128]{2,1,0:T(8,128)(2,1)S(1)}, bf16[2,192,128]{2,1,0:T(8,128)(2,1)S(1)}, u32[]{:S(2)}, u32[]{:S(2)}) collective-permute-start(bf16[2,192,128]{2,1,0:T(8,128)(2,1)S(1)} %get-tuple-element.42), channel_id=1, source_target_pairs={{0,224},{32,0},{64,32},{96,64},{128,96},{160,128},{192,160},{224,1... | collective-permute-start | bytes 294920 | tf_op jit(solution)/shard_map/ppermute | solution.py:354
  74.8 6.3 %collective-permute-start.9 = (bf16[2,192,128]{2,1,0:T(8,128)(2,1)S(1)}, bf16[2,192,128]{2,1,0:T(8,128)(2,1)S(1)}, u32[]{:S(2)}, u32[]{:S(2)}) collective-permute-start(bf16[2,192,128]{2,1,0:T(8,128)(2,1)S(1)} %get-tuple-element.43), channel_id=1, source_target_pairs={{0,224},{32,192},{64,160},{96,128},{128,96},{160,64},{192,32},{224... | collective-permute-start | bytes 294920 | tf_op jit(solution)/shard_map/ppermute | solution.py:487

commit v3 on v2

--- a/solution.py
+++ b/solution.py
@@ -33,7 +33,7 @@
         out_shape=shapes,
         in_specs=specs,
         out_specs=[VMEM] * len(outs),
-        scratch_shapes=places + [pltpu.SemaphoreType.DMA] * (hbm > 0),
+        scratch_shapes=places + [pltpu.SemaphoreType.DMA((4,))] * (hbm > 0),
         compiler_params=pltpu.CompilerParams(vmem_limit_bytes=limit * 1024 * 1024),
         cost_estimate=pl.CostEstimate(flops=flops, bytes_accessed=moved, transcendentals=0),
         name=getattr(body, "__name__", "kernel"),
@@ -71,26 +71,31 @@
     return jnp.concatenate([tile, jnp.zeros((8 - tile.shape[0], AREA), F32)], axis=0)
 
 
-def columns(tile, row):
-    square = jnp.concatenate([tile, jnp.zeros((AREA - 8, AREA), F32)], axis=0).T
-    return jnp.concatenate([square[:, row : row + 1], square[:64, row + 1 : row + 2]], axis=0)
+def columns(tile, pair):
+    square = jnp.concatenate([full_tile(tile), jnp.zeros((AREA - 8, AREA), F32)], axis=0).T
+    row = 3 * pair
+    rest = square[:, row + 2 : row + 3]
+    first = jnp.concatenate([square[:, row : row + 1], rest[:64]], axis=0)
+    second = jnp.concatenate([square[:, row + 1 : row + 2], rest[64:]], axis=0)
+    return first, second
 
 
 def packed_tile(cols):
     lane = lax.broadcasted_iota(jnp.int32, (AREA, AREA), 1)
     square = jnp.zeros((AREA, AREA), F32)
-    for index, col in enumerate(cols):
-        high = jnp.concatenate([col[128:], jnp.zeros((64, 1), F32)], axis=0)
-        square = jnp.where(lane == 2 * index, col[:128], square)
-        square = jnp.where(lane == 2 * index + 1, high, square)
+    for pair in range(len(cols) // 2):
+        one, two = cols[2 * pair], cols[2 * pair + 1]
+        rest = jnp.concatenate([one[128:], two[128:]], axis=0)
+        for k, col in enumerate((one[:128], two[:128], rest)):
+            square = jnp.where(lane == 3 * pair + k, col, square)
     return square.T[:8]
 
 
-def spread_sums(received, row, cells, peers):
+def spread_sums(received, pair, cells, peers):
     total = jnp.sum(received, axis=0)
-    mean = total / peers
-    apart = jnp.sum(jnp.square(received - mean[None]), axis=0)
-    return columns(mean, row), columns(total, row + 2) + cells * columns(apart, row)
+    apart = jnp.sum(jnp.square(received - (total / peers)[None]), axis=0)
+    mean, squares = columns(total, pair)
+    return mean / peers, squares + cells * columns(apart, pair)[0]
 
 
 def local_stats(planes_out, cells):
@@ -99,13 +104,24 @@
     return [mean, squares]
 
 
-def turn_weights(w_ref, out_ref):
-    for pair in range(14):
-        width = 384 if pair < 13 else 192
-        block = w_ref[:, pair * 384 : pair * 384 + width].T
-        if width == 384:
-            block = jnp.concatenate([block[:192], block[192:]], axis=1)
-        out_ref[:, pair * 384 : pair * 384 + width] = block
+def turn_weights(w_ref, out_ref, here_ref, sems):
+    bounds = (0, 4, 8, 12, 14)
+    copies = []
+    for part in range(4):
+        start = bounds[part] * 384
+        band = pl.ds(start, min(bounds[part + 1] * 384, 5184) - start)
+        copies.append(
+            pltpu.make_async_copy(w_ref.at[:, band], here_ref.at[:, band], sems.at[part])
+        )
+        copies[part].start()
+    for part in range(4):
+        copies[part].wait()
+        for pair in range(bounds[part], bounds[part + 1]):
+            width = 384 if pair < 13 else 192
+            block = here_ref[:, pair * 384 : pair * 384 + width].T
+            if width == 384:
+                block = jnp.concatenate([block[:192], block[192:]], axis=1)
+            out_ref[:, pair * 384 : pair * 384 + width] = block
 
 
 def fill_taps(planes, outputs, x_ref, masks, channels, first):
@@ -137,7 +153,7 @@
     tile = packed_tile(
         local_stats(outs[:2], 2.0 * AREA) + local_stats(outs[2:], 2.0 * AREA)
     )
-    send_ref[...] = jnp.broadcast_to(tile[None], send_ref.shape)
+    send_ref[...] = jnp.broadcast_to(tile[None, : send_ref.shape[1]], send_ref.shape)
 
 
 def head_and_sums(
@@ -145,6 +161,8 @@
     z_ref,
     recv_ref,
     own_ref,
+    low_ref,
+    high_ref,
     out_cot_ref,
     skip_cot_ref,
     label_ref,
@@ -153,17 +171,26 @@
     head_turned_ref,
     up_ref,
     share_ref,
+    share_a_ref,
+    share_b_ref,
+    share_c_ref,
     scale_ref,
     send_ref,
 ):
+    shares = (share_ref, share_a_ref, share_b_ref, share_c_ref)
+    for distance, ref in enumerate(shares):
+        rows = pl.ds(pl.multiple_of(48 * ((flag_ref[4] + distance) % 4), 16), 48)
+        ref[4, :48] = low_ref[rows]
+        ref[4, 48:96] = own_ref[0, rows]
+        ref[4, 96:144] = own_ref[1, rows]
+        ref[4, 144:] = high_ref[rows]
     decoder = flag_ref[0] == 1
     last = flag_ref[1] == 1
     peers = recv_ref.shape[0]
     cells = 2.0 * AREA
     mean, squares = spread_sums(recv_ref[...], 0, cells, peers)
     inv_std = lax.rsqrt(squares / (cells * peers) + epsilon)
-    gain = columns(affine_ref[...], 0)
-    shift = columns(affine_ref[...], 2)
+    gain, shift = columns(affine_ref[...], 0)
     scale_ref[...] = jnp.broadcast_to(gain * inv_std, scale_ref.shape)
     classes = head_ref.shape[1]
     class_id = lax.broadcasted_iota(jnp.int32, (classes, AREA), 0)
@@ -185,32 +212,37 @@
         )
         grad_act = upstream * jnp.where(scaled > 0, 1.0, leak_slope)
         up_ref[j] = upstream
-        share_ref[2 * j] = grad_act.astype(BF16)
-        share_ref[2 * j + 1] = normed.astype(BF16)
+        for k, part in enumerate((grad_act.astype(BF16), normed.astype(BF16))):
+            for ref in shares:
+                ref[2 * j + k] = part
         sum_grad = sum_grad + jnp.sum(grad_act, axis=1, keepdims=True)
         sum_cross = sum_cross + jnp.sum(grad_act * normed, axis=1, keepdims=True)
     tile = packed_tile([sum_grad, sum_cross])
     send_ref[...] = jnp.broadcast_to(tile[None, : send_ref.shape[1]], send_ref.shape)
 
 
-def forward_out(recv_ref, z_ref, own_ref, affine_ref, out_ref):
+def forward_out(
+    recv_ref, z_ref, own_ref, affine_ref, share_ref, out_ref, rim_low_ref, rim_high_ref, mix_ref
+):
+    rim_high_ref[...] = share_ref[:2]
+    rim_low_ref[...] = share_ref[2:4]
     peers = recv_ref.shape[0]
     cells = 2.0 * AREA
-    mean, squares = spread_sums(recv_ref[...], 4, cells, peers)
+    mean, squares = spread_sums(recv_ref[...], 1, cells, peers)
     inv_std = lax.rsqrt(squares / (cells * peers) + epsilon)
-    gain = columns(affine_ref[...], 0)
-    shift = columns(affine_ref[...], 2)
+    gain, shift = columns(affine_ref[...], 0)
     for j in range(2):
         scaled = (z_ref[2 + j] - mean) * inv_std * gain + shift
         activated = jnp.where(scaled > 0, scaled, leak_slope * scaled)
-        out_ref[j] = (own_ref[j, 192:].astype(F32) + activated).astype(BF16)
+        mix_ref[pl.ds(j, 192, stride=2), :] = own_ref[j, 192:].astype(F32) + activated
+    out_ref[...] = mix_ref[...].astype(BF16)
 
 
 def row_taps(refs, taps_ref, wide_ref, turned_ref):
     masks = tap_masks()
     for peer, ref in enumerate(refs):
         for q in range(4):
-            wide_ref[...] = ref[q].astype(F32)
+            wide_ref[...] = ref[4, 48 * q : 48 * q + 48].astype(F32)
             for r in range(6):
                 turned_ref[8 * r : 8 * r + 8, :] = wide_ref[pl.ds(r, 8, stride=6), :]
             plane = turned_ref[...]
@@ -232,13 +264,10 @@
     a_ref,
     b_ref,
     c_ref,
-    rows_own_ref,
-    rows_a_ref,
-    rows_b_ref,
-    rows_c_ref,
     scale_ref,
     out_ref,
-    tot_ref,
+    shift_grad_ref,
+    gain_grad_ref,
     taps_ref,
     gz_ref,
     low_ref,
@@ -246,12 +275,13 @@
     wide_ref,
     turned_ref,
 ):
-    row_taps((rows_own_ref, rows_a_ref, rows_b_ref, rows_c_ref), taps_ref, wide_ref, turned_ref)
+    row_taps((own_ref, a_ref, b_ref, c_ref), taps_ref, wide_ref, turned_ref)
     total_cells = 2.0 * AREA * recv_ref.shape[0]
     total = full_tile(jnp.sum(recv_ref[...], axis=0))
-    tot_ref[...] = total * (total_cells ** (-0.5))
-    sum_grad = columns(total, 0) / total_cells
-    sum_cross = columns(total, 2) / total_cells
+    whole = total * (total_cells ** (-0.5))
+    shift_grad_ref[...] = jnp.concatenate([whole[:1], whole[2:3, :64]], axis=1)
+    gain_grad_ref[...] = jnp.concatenate([whole[1:2], whole[2:3, 64:]], axis=1)
+    sum_grad, sum_cross = (col / total_cells for col in columns(total, 0))
     scale = scale_ref[...]
     for peer, ref in enumerate((own_ref, a_ref, b_ref, c_ref)):
         for j in range(2):
@@ -266,7 +296,7 @@
     )
     low_ref[...] = grads[:, :128]
     rest_ref[...] = jnp.concatenate([grads[:672, 128:], grads[672:, 128:]], axis=1)
-    pad = jnp.zeros((12, 384), F32)
+    pad = jnp.zeros((4, 384), F32)
     for z in range(8):
         first = low_ref[pl.ds(z, 84, stride=8), :]
         second = low_ref[pl.ds(z + 672, 84, stride=8), :]
@@ -289,16 +319,22 @@
     skip_ref,
     x_ref,
     w_here_ref,
-    sem,
+    mix_ref,
+    sems,
 ):
-    fetch = pltpu.make_async_copy(w_ref, w_here_ref, sem)
-    fetch.start()
+    spans = ((0, 1920), (1920, 3840), (3840, 5184))
+    copies = []
+    for part, (start, stop) in enumerate(spans):
+        band = pl.ds(start, stop - start)
+        copies.append(
+            pltpu.make_async_copy(w_ref.at[:, band], w_here_ref.at[:, band], sems.at[part])
+        )
+        copies[part].start()
     decoder = flag_ref[0] == 1
     total_cells = 2.0 * AREA * recv_ref.shape[0]
     masks = tap_masks()
     total = full_tile(jnp.sum(recv_ref[...], axis=0))
-    sum_grad = columns(total, 0) / total_cells
-    sum_cross = columns(total, 2) / total_cells
+    sum_grad, sum_cross = (col / total_cells for col in columns(total, 0))
     scale = scale_ref[...]
     acts = [low_ref[0], share_ref[0], share_ref[2], high_ref[0]]
     norms = [low_ref[1], share_ref[1], share_ref[3], high_ref[1]]
@@ -316,14 +352,24 @@
                     if 0 <= j < 2:
                         tap = 9 * a + 3 * b + c
                         x_ref[tap * 192 : (tap + 1) * 192, j * AREA : (j + 1) * AREA] = view
-    fetch.wait()
-    back = jnp.dot(w_here_ref[...], x_ref[...], preferred_element_type=F32)
+    back = None
+    for copy, (start, stop) in zip(copies, spans):
+        copy.wait()
+        part = jnp.dot(
+            w_here_ref[:, start:stop], x_ref[start:stop, :], preferred_element_type=F32
+        )
+        back = part if back is None else back + part
     for j in range(2):
-        grad = (up_ref[j] + back[:, j * AREA : (j + 1) * AREA]).astype(BF16)
-        grad_ref[j] = grad
-        skip_ref[j] = jnp.where(
-            decoder, grad.astype(F32), fwd_out_ref[j].astype(F32)
-        ).astype(BF16)
+        mix_ref[pl.ds(j, 192, stride=2), :] = up_ref[j] + back[:, j * AREA : (j + 1) * AREA]
+    grad = mix_ref[...]
+    grad_ref[...] = grad.astype(BF16)
+    skip_ref[...] = jnp.where(decoder, grad, fwd_out_ref[...].astype(F32)).astype(BF16)
+
+
+def hand_over(one_ref, two_ref, three_ref, out_one_ref, out_two_ref, out_three_ref):
+    out_one_ref[...] = one_ref[...]
+    out_two_ref[...] = two_ref[...]
+    out_three_ref[...] = three_ref[...]
 
 
 def sum_rows(scale_out, recv_ref, out_ref, wide_ref):
@@ -343,9 +389,9 @@
         out_ref[r] = wide_ref[r : r + 1, :]
 
 
-def pair_rows(values):
-    padded = jnp.pad(values, ((0, 2), (0, 64)))
-    return padded.reshape(8, AREA)
+def pair_rows(one, two):
+    rest = jnp.concatenate([one[:, 128:], two[:, 128:]], axis=1)
+    return jnp.concatenate([one[:, :128], two[:, :128], rest], axis=0)
 
 
 def moved(block, axis, distance, wrap=True):
@@ -374,10 +420,16 @@
     slab_id = y_id * lax.axis_size("z") + lax.axis_index("z")
     is_decoder = segment_id * 2 >= segments
     flags = jnp.stack(
-        [is_decoder, segment_id == segments - 1, slab_id > 0, slab_id < slabs - 1]
-    ).astype(jnp.int32)
+        [
+            is_decoder.astype(jnp.int32),
+            (segment_id == segments - 1).astype(jnp.int32),
+            (slab_id > 0).astype(jnp.int32),
+            (slab_id < slabs - 1).astype(jnp.int32),
+            y_id.astype(jnp.int32),
+        ]
+    )
     kernel_mat = kernel[0]
-    affine = pair_rows(jnp.concatenate([norm_gain, norm_shift], axis=0))
+    affine = pair_rows(norm_gain, norm_shift)
 
     def by_plane(block):
         return jnp.swapaxes(block[0], 0, 1)
@@ -389,10 +441,19 @@
     own = jnp.concatenate([joined(bwd_input, bwd_skip), joined(fwd_input, fwd_skip)], axis=1)
     low = moved(own[1], SLABS, 1, False)
     high = moved(own[0], SLABS, -1, False)
-    (turned,) = call(turn_weights, [((192, 5184), BF16)], [], 0, 4 * 192 * 5184, kernel_mat)
+    (turned,) = call(
+        turn_weights,
+        [((192, 5184), BF16)],
+        [((192, 5184), BF16)],
+        0,
+        4 * 192 * 5184,
+        kernel_mat,
+        hbm=1,
+        limit=52,
+    )
     z, stats_send = call(
         conv_both,
-        [((4, 192, AREA), F32), ((slabs, 8, AREA), F32)],
+        [((4, 192, AREA), F32), ((slabs, 6, AREA), F32)],
         [((5184, 512), BF16)],
         2 * 5184 * 192 * 512,
         5000000,
@@ -404,19 +465,11 @@
     stats = lax.all_to_all(stats_send, SLABS, 0, 0, tiled=True)
     out_cots = by_plane(out_cot)
     skip_cots = by_plane(skip_cot)
-    window = jnp.concatenate([low[None, :192], own[:, :192], high[None, :192]], axis=0)
-
-    def rows_for(distance):
-        start = 48 * ((y_id + distance) % 4)
-        return lax.dynamic_slice_in_dim(window, start, 48, axis=1)
-
-    row_parts = [rows_for(0)] + [moved(rows_for(d), "y", d) for d in (1, 2, 3)]
-    stats, row_parts = lax.optimization_barrier((stats, row_parts))
-    upstream, share, scale, sums_send = call(
+    upstream, *shares, scale, sums_send = call(
         head_and_sums,
         [
             ((2, 192, AREA), F32),
-            ((4, 192, AREA), BF16),
+            *[((5, 192, AREA), BF16)] * 4,
             ((192, AREA), F32),
             ((slabs, 4, AREA), F32),
         ],
@@ -427,6 +480,8 @@
         z,
         stats,
         own,
+        low,
+        high,
         out_cots,
         skip_cots,
         labels,
@@ -436,16 +491,26 @@
         smem=1,
     )
     sums = lax.all_to_all(sums_send, SLABS, 0, 0, tiled=True)
-    shares = [share] + [moved(share, "y", d) for d in (1, 2, 3)]
-    rim_low = moved(share[2:], SLABS, 1, False)
-    rim_high = moved(share[:2], SLABS, -1, False)
-    (fwd_out,) = call(
-        forward_out, [((2, 192, AREA), BF16)], [], 0, 1000000, stats, z, own, affine
-    )
-    sums, rim_low, rim_high, fwd_out = lax.optimization_barrier((sums, rim_low, rim_high, fwd_out))
-    parts, totals = call(
+    share = shares[0]
+    shares = [share] + [moved(shares[d], "y", d) for d in (1, 2, 3)]
+    fwd_out, rim_low, rim_high = call(
+        forward_out,
+        [((384, AREA), BF16), ((2, 192, AREA), BF16), ((2, 192, AREA), BF16)],
+        [((384, AREA), F32)],
+        0,
+        1000000,
+        stats,
+        z,
+        own,
+        affine,
+        share,
+    )
+    rim_low = moved(rim_low, SLABS, 1, False)
+    rim_high = moved(rim_high, SLABS, -1, False)
+    sums, fwd_out = lax.optimization_barrier((sums, fwd_out))
+    parts, shift_grad, gain_grad = call(
         kernel_grads,
-        [((8, 96, 384), BF16), ((8, AREA), F32)],
+        [((8, 88, 384), BF16), ((1, 192), F32), ((1, 192), F32)],
         [
             ((1344, 1024), BF16),
             ((192, 1024), BF16),
@@ -454,18 +519,18 @@
             ((48, AREA), F32),
             ((48, AREA), F32),
         ],
-        2 * 1296 * 1024 * 192,
-        5000000,
+        0,
+        1000,
         sums,
         *shares,
-        *row_parts,
         scale,
     )
+    parts, rim_low, rim_high = lax.optimization_barrier((parts, rim_low, rim_high))
     summed = lax.all_to_all(parts, "z", 0, 0, tiled=True)
     grad_joined, outgoing = call(
         input_grads,
-        [((2, 192, AREA), BF16)] * 2,
-        [((5184, 256), BF16), ((192, 5184), BF16)],
+        [((384, AREA), BF16)] * 2,
+        [((5184, 256), BF16), ((192, 5184), BF16), ((384, AREA), F32)],
         2 * 5184 * 192 * 256,
         4000000,
         flags,
@@ -486,6 +551,21 @@
     next_block = moved(fwd_out, "segment", 1)
     mirrored = lax.ppermute(outgoing, "segment", [(i, segments - 1 - i) for i in range(segments)])
     total_cells = float(2 * slabs * AREA)
+
+    def by_channel(block):
+        return block.reshape(1, 192, 2, AREA)
+
+    blocks = call(
+        hand_over,
+        [((384, AREA), BF16)] * 3,
+        [],
+        0,
+        600000,
+        next_block,
+        prev_block,
+        mirrored,
+    )
+    handed = [by_channel(block) for block in blocks]
     (kernel_grad,) = call(
         functools.partial(sum_rows, total_cells ** (-0.5)),
         [((6, 1, 5184), F32)],
@@ -494,18 +574,11 @@
         1000000,
         summed,
     )
-    flat = totals.reshape(-1)
-
-    def by_channel(block):
-        return jnp.swapaxes(block, 0, 1)[None]
-
     return (
-        by_channel(next_block),
-        by_channel(prev_block),
-        by_channel(mirrored),
+        *handed,
         jnp.swapaxes(kernel_grad, 0, 1),
-        flat[256:448][None],
-        flat[:192][None],
+        gain_grad,
+        shift_grad,
     )
 
 

time: 85 us -> 80.2 us (0.944)
  starting transfers between devices: 47.2 us -> 37.1 us
  waiting for transfers between devices: 17.2 us -> 24.5 us
  local copies, waits for them, and re-layouts: 4.59 us -> 0.27 us
  Pallas kernels: 13.4 us -> 15.8 us
    all_to_all x1, waiting for transfers between devices: 1.65 us -> 10.3 us  [per_device(): stats = lax.all_to_all(stats_send, SLABS, 0, 0, tiled=True)]
    ppermute x12 -> x9, waiting for transfers between devices: 11.2 us -> 4.61 us  [moved(): return lax.ppermute(block, axis, route)]
    ppermute x12 -> x9, starting transfers between devices: 21.8 us -> 15.8 us  [moved(): return lax.ppermute(block, axis, route)]
    all_to_all x1, waiting for transfers between devices: 0.01 us -> 4.53 us  [per_device(): sums = lax.all_to_all(sums_send, SLABS, 0, 0, tiled=True)]
    unnamed x18 -> x9, local copies, waits for them, and re-layouts: 3.93 us -> 0.14 us
    all_to_all x1, starting transfers between devices: 7.05 us -> 4.6 us  [per_device(): sums = lax.all_to_all(sums_send, SLABS, 0, 0, tiled=True)]
    pallas_call x7 -> x8, Pallas kernels: 13.4 us -> 15.8 us  [call(): pl.pallas_call(body, out_shape=shapes, in_specs=specs, out_specs=[VMEM] *...]
    all_to_all x1, starting transfers between devices: 6.96 us -> 5.34 us  [per_device(): summed = lax.all_to_all(parts, 'z', 0, 0, tiled=True)]
  transfers between devices with their start and end apart: 16 -> 13, of which waited for: 9 -> 6; matrix products, arithmetic and copies ran while one was open for 4% -> 0% of each run, Pallas kernels for 6% -> 12%
where the time goes in v3:
time: 80.2 us; the launch traced here: 79.7 us
  starting transfers between devices  37.1 us (46%)
  waiting for transfers between devices  24.5 us (31%)
  Pallas kernels  15.8 us (20%)
  other arithmetic  1.2 us (1%)
  between operations  0.86 us (1%)
    pallas_call x8, Pallas kernels, call(): pl.pallas_call(body, out_shape=shapes, in_specs=specs, out_specs=[VMEM] *...  15.8 us
    ppermute x9, starting transfers between devices, moved(): return lax.ppermute(block, axis, route)  15.8 us
    all_to_all x1, starting transfers between devices, per_device(): stats = lax.all_to_all(stats_send, SLABS, 0, 0, tiled=True)  11.3 us
    all_to_all x1, waiting for transfers between devices, per_device(): stats = lax.all_to_all(stats_send, SLABS, 0, 0, tiled=True)  10.3 us
    all_to_all x1, starting transfers between devices, per_device(): summed = lax.all_to_all(parts, 'z', 0, 0, tiled=True)  5.34 us
    ppermute x9, waiting for transfers between devices, moved(): return lax.ppermute(block, axis, route)  4.61 us
    all_to_all x1, starting transfers between devices, per_device(): sums = lax.all_to_all(sums_send, SLABS, 0, 0, tiled=True)  4.6 us
    all_to_all x1, waiting for transfers between devices, per_device(): sums = lax.all_to_all(sums_send, SLABS, 0, 0, tiled=True)  4.53 us
  transfers between devices with their start and end apart: 13, of which 6 were waited for; matrix products, arithmetic and copies ran while one was open for 0% of the time, Pallas kernels for 12%

profile of v3, /device:TPU:6, one launch (start us, length us, event | category | flops | bytes accessed | tf_op | source)
XLA Modules:
  0.0 79.7 jit_solution(13648875624589631151)
XLA Ops:
  0.6 1.1 %fusion.2 = (bf16[2,192,128]{2,1,0:T(8,128)(2,1)S(1)}, bf16[2,192,128]{2,1,0:T(8,128)(2,1)S(1)}) fusion(bf16[1,192,2,128]{3,2,1,0:T(2,128)(2,1)} %param.12, bf16[1,192,2,128]{3,2,1,0:T(2,128)(2,1)} %param.11, pred[]{:T(512)S(6)} %ge.3, bf16[1,192,2,128]{3,2,1,0:T(2,128)(2,1)} %param.14, bf16[1,192,2,128]{3,2,1,0:T(2,128)(2,1)} %param.13), kind=kLoop, calls=%fused_computation.9 | loop fusion | flops 491520 | bytes 589825 | tf_op jit(solution)/shard_map/transpose | solution.py:435
  1.8 3.8 %collective-permute-start = (bf16[384,128]{1,0:T(8,128)(2,1)S(1)}, bf16[384,128]{1,0:T(8,128)(2,1)S(1)}, u32[]{:S(2)}, u32[]{:S(2)}) collective-permute-start(bf16[384,128]{1,0:T(8,128)(2,1)S(1)} %get-tuple-element.63), channel_id=1, source_target_pairs={{0,1},{1,2},{2,3},{3,4},{4,5},{5,6},{6,7},{7,8},{8,9},{9,10},{10,1... | collective-permute-start | bytes 294920 | tf_op jit(solution)/shard_map/ppermute | solution.py:400
  5.6 1.3 %collective-permute-start.1 = (bf16[384,128]{1,0:T(8,128)(2,1)S(1)}, bf16[384,128]{1,0:T(8,128)(2,1)S(1)}, u32[]{:S(2)}, u32[]{:S(2)}) collective-permute-start(bf16[384,128]{1,0:T(8,128)(2,1)S(1)} %get-tuple-element.62), channel_id=1, source_target_pairs={{1,0},{2,1},{3,2},{4,3},{5,4},{6,5},{7,6},{8,7},{9,8},{10,9},{11,1... | collective-permute-start | bytes 294920 | tf_op jit(solution)/shard_map/ppermute | solution.py:400
  6.9 0.0 copy-start
  6.9 0.0 slice-start
  7.0 0.0 slice-start.1
  7.0 0.0 slice-start.2
  7.0 0.0 slice-start.3
  7.0 2.5 %turn_weights.1.wt_ref = bf16[192,5184]{1,0:T(8,128)(2,1)S(1)} custom-call(bf16[192,5184]{1,0:T(8,128)(2,1)} %bitcast.32), custom_call_target="tpu_custom_call" | custom-call | bytes 3981312 | tf_op jit(solution)/shard_map/turn_weights/pallas_call | solution.py:31
  9.5 0.0 copy-done
  9.5 0.1 copy.25
  9.6 0.1 stack.39.flag_ref
  9.7 0.0 slice-done
  9.7 0.0 slice-done.1
  9.7 0.0 slice-done.2
  9.7 0.0 slice-done.3
  9.7 0.1 maximum_maximum_fusion.affine_ref
  9.8 0.0 copy-start.2
  9.8 0.0 copy-start.3
  9.8 0.0 copy-start.1
  9.8 0.0 collective-permute-done.low_ref
  9.8 2.3 %collective-permute-done.1.high_ref = bf16[384,128]{1,0:T(8,128)(2,1)S(1)} collective-permute-done((bf16[384,128]{1,0:T(8,128)(2,1)S(1)}, bf16[384,128]{1,0:T(8,128)(2,1)S(1)}, u32[]{:S(2)}, u32[]{:S(2)}) %collective-permute-start.1) | collective-permute-done | bytes 98336 | tf_op jit(solution)/shard_map/ppermute | solution.py:400
  12.1 2.8 %conv_both.1 = (f32[4,192,128]{2,1,0:T(8,128)S(1)}, f32[32,6,128]{2,1,0:T(8,128)}) custom-call(bf16[2,384,128]{2,1,0:T(8,128)(2,1)S(1)} %pad_maximum_fusion.own_ref, bf16[384,128]{1,0:T(8,128)(2,1)S(1)} %collective-permute-done.low_ref, bf16[384,128]{1,0:T(8,128)(2,1)S(1)} %collective-permute-done.1.high_ref, bf16[192,5184]{1,0:T(8,128)(2,1)S(1)} %turn_weights.1.wt_ref), custom_call_target="tpu_custom_call" | custom-call | flops 1019215872 | bytes 5000000 | tf_op jit(solution)/shard_map/conv_both/pallas_call | solution.py:31
  14.9 11.3 %all-to-all-start = ((f32[32,6,128]{2,1,0:T(8,128)}), f32[32,6,128]{2,1,0:T(8,128)S(1)}, u32[]{:S(2)}, u32[]{:S(2)}) async-start(f32[32,6,128]{2,1,0:T(8,128)} %get-tuple-element.35), calls=%async_computation | async-start | bytes 262144 | tf_op jit(solution)/shard_map/all_to_all | solution.py:465
  26.3 0.0 copy-done.2
  26.3 0.0 copy-done.3
  26.3 10.3 %all-to-all-done.recv_ref = f32[32,6,128]{2,1,0:T(8,128)S(1)} async-done(((f32[32,6,128]{2,1,0:T(8,128)}), f32[32,6,128]{2,1,0:T(8,128)S(1)}, u32[]{:S(2)}, u32[]{:S(2)}) %all-to-all-start) | async-done | bytes 98336 | tf_op jit(solution)/shard_map/all_to_all | solution.py:465
  36.7 0.0 copy-done.1
  36.7 2.5 %head_and_sums.1 = (f32[2,192,128]{2,1,0:T(8,128)S(1)}, bf16[5,192,128]{2,1,0:T(8,128)(2,1)S(1)}, bf16[5,192,128]{2,1,0:T(8,128)(2,1)}, bf16[5,192,128]{2,1,0:T(...) custom-call(s32[5]{0:T(128)S(1)} %stack.39.flag_ref, ...), custom_call_target="tpu_custom_call" | custom-call | flops 41287680 | bytes 4000000 | tf_op jit(solution)/shard_map/head_and_sums/pallas_call | solution.py:31
  39.2 0.6 collective-permute-start.2
  39.8 2.0 %collective-permute-start.3 = (bf16[5,192,128]{2,1,0:T(8,128)(2,1)S(1)}, bf16[5,192,128]{2,1,0:T(8,128)(2,1)S(1)}, u32[]{:S(2)}, u32[]{:S(2)}) collective-permute-start(bf16[5,192,128]{2,1,0:T(8,128)(2,1)S(1)} %get-tuple-element.43), channel_id=1, source_target_pairs={{0,16},{8,24},{16,0},{24,8},{1,17},{9,25},{17,1},{25,9},{2,18},{10... | collective-permute-start | bytes 737288 | tf_op jit(solution)/shard_map/ppermute | solution.py:400
  41.8 1.3 %collective-permute-start.4 = (bf16[5,192,128]{2,1,0:T(8,128)(2,1)S(1)}, bf16[5,192,128]{2,1,0:T(8,128)(2,1)S(1)}, u32[]{:S(2)}, u32[]{:S(2)}) collective-permute-start(bf16[5,192,128]{2,1,0:T(8,128)(2,1)S(1)} %get-tuple-element.44), channel_id=1, source_target_pairs={{0,24},{8,0},{16,8},{24,16},{1,25},{9,1},{17,9},{25,17},{2,26},{10... | collective-permute-start | bytes 737288 | tf_op jit(solution)/shard_map/ppermute | solution.py:400
  43.2 4.6 %all-to-all-start.1 = ((f32[32,4,128]{2,1,0:T(4,128)}), f32[32,4,128]{2,1,0:T(4,128)S(1)}, u32[]{:S(2)}, u32[]{:S(2)}) async-start(f32[32,4,128]{2,1,0:T(4,128)} %get-tuple-element.36), calls=%async_computation.1 | async-start | bytes 131072 | tf_op jit(solution)/shard_map/all_to_all | solution.py:493
  47.8 0.5 forward_out.1
  48.3 3.7 %collective-permute-start.5 = (bf16[2,192,128]{2,1,0:T(8,128)(2,1)S(1)}, bf16[2,192,128]{2,1,0:T(8,128)(2,1)S(1)}, u32[]{:S(2)}, u32[]{:S(2)}) collective-permute-start(bf16[2,192,128]{2,1,0:T(8,128)(2,1)S(1)} %get-tuple-element.47), channel_id=1, source_target_pairs={{0,1},{1,2},{2,3},{3,4},{4,5},{5,6},{6,7},{7,8},{8,9},{9,10},{10,1... | collective-permute-start | bytes 294920 | tf_op jit(solution)/shard_map/ppermute | solution.py:400
  52.0 1.3 %collective-permute-start.6 = (bf16[2,192,128]{2,1,0:T(8,128)(2,1)S(1)}, bf16[2,192,128]{2,1,0:T(8,128)(2,1)S(1)}, u32[]{:S(2)}, u32[]{:S(2)}) collective-permute-start(bf16[2,192,128]{2,1,0:T(8,128)(2,1)S(1)} %get-tuple-element.48), channel_id=1, source_target_pairs={{1,0},{2,1},{3,2},{4,3},{5,4},{6,5},{7,6},{8,7},{9,8},{10,9},{11,1... | collective-permute-start | bytes 294920 | tf_op jit(solution)/shard_map/ppermute | solution.py:400
  53.3 4.5 %all-to-all-done.1.recv_ref = f32[32,4,128]{2,1,0:T(4,128)S(1)} async-done(((f32[32,4,128]{2,1,0:T(4,128)}), f32[32,4,128]{2,1,0:T(4,128)S(1)}, u32[]{:S(2)}, u32[]{:S(2)}) %all-to-all-start.1) | async-done | bytes 65568 | tf_op jit(solution)/shard_map/all_to_all | solution.py:493
  57.8 0.0 collective-permute-done.2.a_ref
  57.8 0.0 collective-permute-done.3.b_ref
  57.8 0.0 collective-permute-done.4.c_ref
  57.8 2.3 %kernel_grads.1 = (bf16[8,88,384]{2,1,0:T(8,128)(2,1)}, f32[1,192]{1,0:T(1,128)}, f32[1,192]{1,0:T(1,128)}) custom-call(f32[32,4,128]{2,1,0:T(4,128)S(1)} %all-to-all-done.1.recv_ref, bf16[5,192,128]{2,1,0:T(8,128)(2,1)S(1)} %get-tuple-element.37.share_ref.own_ref, bf16[5,192,128]{2,1,0:T(8,128)(2,1)S(1)} %collective-permute-done.2.a_ref, ...), custom_call_target="tpu_custom_call" | custom-call | bytes 1000 | tf_op jit(solution)/shard_map/kernel_grads/pallas_call | solution.py:31
  60.1 0.0 collective-permute-done.5.low_ref
  60.1 0.0 collective-permute-done.6.high_ref
  60.1 5.3 %all-to-all-start.2 = ((bf16[8,88,384]{2,1,0:T(8,128)(2,1)}), bf16[8,88,384]{2,1,0:T(8,128)(2,1)S(1)}, u32[]{:S(2)}, u32[]{:S(2)}) async-start(bf16[8,88,384]{2,1,0:T(8,128)(2,1)} %get-tuple-element.59), calls=%async_computation.2 | async-start | bytes 1081344 | tf_op jit(solution)/shard_map/all_to_all | solution.py:529
  65.5 3.6 %input_grads.1 = (bf16[384,128]{1,0:T(8,128)(2,1)S(1)}, bf16[384,128]{1,0:T(8,128)(2,1)S(1)}) custom-call(s32[5]{0:T(128)S(1)} %stack.39.flag_ref, bf16[192,5184]{1,0:T(8,128)(2,1)} %bitcast.33, f32[32,4,128]{2,1,0:T(4,128)S(1)} %all-to-all-done.1.recv_ref, bf16[5,192,128]{2,1,0:T(8,128)(2,1)S(1)} %get-tuple-element.37.share_ref.own_ref, ...), custom_call_target="tpu_custom_call" | custom-call | flops 509607936 | bytes 4000000 | tf_op jit(solution)/shard_map/input_grads/pallas_call | solution.py:31
  69.1 0.0 collective-permute-start.7
  69.1 1.7 %collective-permute-start.8 = (bf16[384,128]{1,0:T(8,128)(2,1)S(1)}, bf16[384,128]{1,0:T(8,128)(2,1)S(1)}, u32[]{:S(2)}, u32[]{:S(2)}) collective-permute-start(bf16[384,128]{1,0:T(8,128)(2,1)S(1)} %get-tuple-element.54), channel_id=1, source_target_pairs={{0,224},{32,0},{64,32},{96,64},{128,96},{160,128},{192,160},{224,1... | collective-permute-start | bytes 294920 | tf_op jit(solution)/shard_map/ppermute | solution.py:400
  70.9 0.0 collective-permute-start.9
  70.9 2.3 %collective-permute-done.7.one_ref = bf16[384,128]{1,0:T(8,128)(2,1)S(1)} collective-permute-done((bf16[384,128]{1,0:T(8,128)(2,1)S(1)}, bf16[384,128]{1,0:T(8,128)(2,1)S(1)}, u32[]{:S(2)}, u32[]{:S(2)}) %collective-permute-start.7) | collective-permute-done | bytes 98336 | tf_op jit(solution)/shard_map/ppermute | solution.py:400
  73.2 0.0 collective-permute-done.8.two_ref
  73.2 4.0 %collective-permute-done.9.three_ref = bf16[384,128]{1,0:T(8,128)(2,1)S(1)} collective-permute-done((bf16[384,128]{1,0:T(8,128)(2,1)S(1)}, bf16[384,128]{1,0:T(8,128)(2,1)S(1)}, u32[]{:S(2)}, u32[]{:S(2)}) %collective-permute-start.9) | collective-permute-done | bytes 98336 | tf_op jit(solution)/shard_map/ppermute | solution.py:552
  77.2 0.7 hand_over.1
  77.9 1.0 %all-to-all-done.2.recv_ref = bf16[8,88,384]{2,1,0:T(8,128)(2,1)S(1)} async-done(((bf16[8,88,384]{2,1,0:T(8,128)(2,1)}), bf16[8,88,384]{2,1,0:T(8,128)(2,1)S(1)}, u32[]{:S(2)}, u32[]{:S(2)}) %all-to-all-start.2) | async-done | bytes 540704 | tf_op jit(solution)/shard_map/all_to_all | solution.py:529
  78.9 0.8 %kernel.1 = f32[6,1,5184]{2,1,0:T(1,128)} custom-call(bf16[8,88,384]{2,1,0:T(8,128)(2,1)S(1)} %all-to-all-done.2.recv_ref), custom_call_target="tpu_custom_call" | custom-call | bytes 1000000 | tf_op jit(solution)/shard_map/kernel/pallas_call | solution.py:31
  (3 shorter events, 0.1 us)
Async XLA Ops:
  1.8 8.0 %collective-permute-start = (bf16[384,128]{1,0:T(8,128)(2,1)S(1)}, bf16[384,128]{1,0:T(8,128)(2,1)S(1)}, u32[]{:S(2)}, u32[]{:S(2)}) collective-permute-start(bf16[384,128]{1,0:T(8,128)(2,1)S(1)} %get-tuple-element.63), channel_id=1, source_target_pairs={{0,1},{1,2},{2,3},{3,4},{4,5},{5,6},{6,7},{7,8},{8,9},{9,10},{10,1... | collective-permute-start | bytes 294920 | tf_op jit(solution)/shard_map/ppermute | solution.py:400
  5.6 6.5 %collective-permute-start.1 = (bf16[384,128]{1,0:T(8,128)(2,1)S(1)}, bf16[384,128]{1,0:T(8,128)(2,1)S(1)}, u32[]{:S(2)}, u32[]{:S(2)}) collective-permute-start(bf16[384,128]{1,0:T(8,128)(2,1)S(1)} %get-tuple-element.62), channel_id=1, source_target_pairs={{1,0},{2,1},{3,2},{4,3},{5,4},{6,5},{7,6},{8,7},{9,8},{10,9},{11,1... | collective-permute-start | bytes 294920 | tf_op jit(solution)/shard_map/ppermute | solution.py:400
  6.9 2.5 %copy-start = (bf16[192,105]{1,0:T(8,128)(2,1)S(1)}, bf16[192,105]{1,0:T(8,128)(2,1)}, u32[]{:S(2)}) copy-start(bf16[192,105]{1,0:T(8,128)(2,1)} %head_ref.1) | copy-start | bytes 120964
  6.9 2.7 %slice-start = ((f32[1,192]{1,0:T(1,128)}), f32[1,64]{1,0:T(1,128)S(1)}, s32[]{:S(2)}) async-start(f32[1,192]{1,0:T(1,128)} %param.19), calls=%async_computation.3 | async-start | bytes 1024 | tf_op jit(solution)/shard_map/slice | solution.py:393
  7.0 2.7 %slice-start.1 = ((f32[1,192]{1,0:T(1,128)}), f32[1,128]{1,0:T(1,128)S(1)}, s32[]{:S(2)}) async-start(f32[1,192]{1,0:T(1,128)} %param.19), calls=%async_computation.4 | async-start | bytes 1024 | tf_op jit(solution)/shard_map/slice | solution.py:394
  7.0 2.7 %slice-start.2 = ((f32[1,192]{1,0:T(1,128)}), f32[1,64]{1,0:T(1,128)S(1)}, s32[]{:S(2)}) async-start(f32[1,192]{1,0:T(1,128)} %param.18), calls=%async_computation.5 | async-start | bytes 1024 | tf_op jit(solution)/shard_map/slice | solution.py:393
  7.0 2.7 %slice-start.3 = ((f32[1,192]{1,0:T(1,128)}), f32[1,128]{1,0:T(1,128)S(1)}, s32[]{:S(2)}) async-start(f32[1,192]{1,0:T(1,128)} %param.18), calls=%async_computation.6 | async-start | bytes 1024 | tf_op jit(solution)/shard_map/slice | solution.py:394
  9.8 16.5 %copy-start.2 = (bf16[1,192,2,128]{3,2,1,0:T(2,128)(2,1)S(1)}, bf16[1,192,2,128]{3,2,1,0:T(2,128)(2,1)}, u32[]{:S(2)}) copy-start(bf16[1,192,2,128]{3,2,1,0:T(2,128)(2,1)} %param.16) | copy-start | bytes 294916
  9.8 16.5 %copy-start.3 = (bf16[1,192,2,128]{3,2,1,0:T(2,128)(2,1)S(1)}, bf16[1,192,2,128]{3,2,1,0:T(2,128)(2,1)}, u32[]{:S(2)}) copy-start(bf16[1,192,2,128]{3,2,1,0:T(2,128)(2,1)} %param.15) | copy-start | bytes 294916
  9.8 26.9 %copy-start.1 = (s32[2,128]{1,0:T(2,128)S(1)}, s32[2,128]{1,0:T(2,128)}, u32[]{:S(2)}) copy-start(s32[2,128]{1,0:T(2,128)} %label_ref.1) | copy-start | bytes 3076
  14.9 21.7 %all-to-all-start = ((f32[32,6,128]{2,1,0:T(8,128)}), f32[32,6,128]{2,1,0:T(8,128)S(1)}, u32[]{:S(2)}, u32[]{:S(2)}) async-start(f32[32,6,128]{2,1,0:T(8,128)} %get-tuple-element.35), calls=%async_computation | async-start | bytes 262144 | tf_op jit(solution)/shard_map/all_to_all | solution.py:465
  39.2 18.6 %collective-permute-start.2 = (bf16[5,192,128]{2,1,0:T(8,128)(2,1)}, bf16[5,192,128]{2,1,0:T(8,128)(2,1)S(1)}, u32[]{:S(2)}, u32[]{:S(2)}) collective-permute-start(bf16[5,192,128]{2,1,0:T(8,128)(2,1)} %get-tuple-element.42), channel_id=1, source_target_pairs={{0,8},{8,16},{16,24},{24,0},{1,9},{9,17},{17,25},{25,1},{2,10},{10... | collective-permute-start | bytes 737288 | tf_op jit(solution)/shard_map/ppermute | solution.py:400
  39.8 18.0 %collective-permute-start.3 = (bf16[5,192,128]{2,1,0:T(8,128)(2,1)S(1)}, bf16[5,192,128]{2,1,0:T(8,128)(2,1)S(1)}, u32[]{:S(2)}, u32[]{:S(2)}) collective-permute-start(bf16[5,192,128]{2,1,0:T(8,128)(2,1)S(1)} %get-tuple-element.43), channel_id=1, source_target_pairs={{0,16},{8,24},{16,0},{24,8},{1,17},{9,25},{17,1},{25,9},{2,18},{10... | collective-permute-start | bytes 737288 | tf_op jit(solution)/shard_map/ppermute | solution.py:400
  41.8 16.0 %collective-permute-start.4 = (bf16[5,192,128]{2,1,0:T(8,128)(2,1)S(1)}, bf16[5,192,128]{2,1,0:T(8,128)(2,1)S(1)}, u32[]{:S(2)}, u32[]{:S(2)}) collective-permute-start(bf16[5,192,128]{2,1,0:T(8,128)(2,1)S(1)} %get-tuple-element.44), channel_id=1, source_target_pairs={{0,24},{8,0},{16,8},{24,16},{1,25},{9,1},{17,9},{25,17},{2,26},{10... | collective-permute-start | bytes 737288 | tf_op jit(solution)/shard_map/ppermute | solution.py:400
  43.2 14.7 %all-to-all-start.1 = ((f32[32,4,128]{2,1,0:T(4,128)}), f32[32,4,128]{2,1,0:T(4,128)S(1)}, u32[]{:S(2)}, u32[]{:S(2)}) async-start(f32[32,4,128]{2,1,0:T(4,128)} %get-tuple-element.36), calls=%async_computation.1 | async-start | bytes 131072 | tf_op jit(solution)/shard_map/all_to_all | solution.py:493
  48.3 11.8 %collective-permute-start.5 = (bf16[2,192,128]{2,1,0:T(8,128)(2,1)S(1)}, bf16[2,192,128]{2,1,0:T(8,128)(2,1)S(1)}, u32[]{:S(2)}, u32[]{:S(2)}) collective-permute-start(bf16[2,192,128]{2,1,0:T(8,128)(2,1)S(1)} %get-tuple-element.47), channel_id=1, source_target_pairs={{0,1},{1,2},{2,3},{3,4},{4,5},{5,6},{6,7},{7,8},{8,9},{9,10},{10,1... | collective-permute-start | bytes 294920 | tf_op jit(solution)/shard_map/ppermute | solution.py:400
  52.0 8.1 %collective-permute-start.6 = (bf16[2,192,128]{2,1,0:T(8,128)(2,1)S(1)}, bf16[2,192,128]{2,1,0:T(8,128)(2,1)S(1)}, u32[]{:S(2)}, u32[]{:S(2)}) collective-permute-start(bf16[2,192,128]{2,1,0:T(8,128)(2,1)S(1)} %get-tuple-element.48), channel_id=1, source_target_pairs={{1,0},{2,1},{3,2},{4,3},{5,4},{6,5},{7,6},{8,7},{9,8},{10,9},{11,1... | collective-permute-start | bytes 294920 | tf_op jit(solution)/shard_map/ppermute | solution.py:400
  60.1 18.8 %all-to-all-start.2 = ((bf16[8,88,384]{2,1,0:T(8,128)(2,1)}), bf16[8,88,384]{2,1,0:T(8,128)(2,1)S(1)}, u32[]{:S(2)}, u32[]{:S(2)}) async-start(bf16[8,88,384]{2,1,0:T(8,128)(2,1)} %get-tuple-element.59), calls=%async_computation.2 | async-start | bytes 1081344 | tf_op jit(solution)/shard_map/all_to_all | solution.py:529
  69.1 4.1 %collective-permute-start.7 = (bf16[384,128]{1,0:T(8,128)(2,1)S(1)}, bf16[384,128]{1,0:T(8,128)(2,1)S(1)}, u32[]{:S(2)}, u32[]{:S(2)}) collective-permute-start(bf16[384,128]{1,0:T(8,128)(2,1)S(1)} %get-tuple-element.53.fwd_out_ref), channel_id=1, source_target_pairs={{0,32},{32,64},{64,96},{96,128},{128,160},{160,192},{192,224},{224... | collective-permute-start | bytes 294920 | tf_op jit(solution)/shard_map/ppermute | solution.py:400
  69.1 4.0 %collective-permute-start.8 = (bf16[384,128]{1,0:T(8,128)(2,1)S(1)}, bf16[384,128]{1,0:T(8,128)(2,1)S(1)}, u32[]{:S(2)}, u32[]{:S(2)}) collective-permute-start(bf16[384,128]{1,0:T(8,128)(2,1)S(1)} %get-tuple-element.54), channel_id=1, source_target_pairs={{0,224},{32,0},{64,32},{96,64},{128,96},{160,128},{192,160},{224,1... | collective-permute-start | bytes 294920 | tf_op jit(solution)/shard_map/ppermute | solution.py:400
  70.9 6.3 %collective-permute-start.9 = (bf16[384,128]{1,0:T(8,128)(2,1)S(1)}, bf16[384,128]{1,0:T(8,128)(2,1)S(1)}, u32[]{:S(2)}, u32[]{:S(2)}) collective-permute-start(bf16[384,128]{1,0:T(8,128)(2,1)S(1)} %get-tuple-element.55), channel_id=1, source_target_pairs={{0,224},{32,192},{64,160},{96,128},{128,96},{160,64},{192,32},{224... | collective-permute-start | bytes 294920 | tf_op jit(solution)/shard_map/ppermute | solution.py:552

commit v4 on v3

--- a/solution.py
+++ b/solution.py
@@ -22,6 +22,9 @@
 HBM = pl.BlockSpec(memory_space=pltpu.HBM)
 VMEM = pl.BlockSpec(memory_space=pltpu.VMEM)
 SMEM = pl.BlockSpec(memory_space=pltpu.SMEM)
+
+
+HEAD_SCRATCH = [((2, 192, AREA), F32)]
 
 
 def call(body, outs, scratch, flops, moved, *args, smem=0, hbm=0, limit=24):
@@ -62,7 +65,7 @@
     if step == 0:
         return plane
     moved = pltpu.roll(plane, (-step) % AREA, 1)
-    return jnp.where(masks[(b, c)], moved, 0.0)
+    return jnp.where(masks[(b, c)], moved, jnp.zeros_like(moved))
 
 
 def full_tile(tile):
@@ -126,10 +129,9 @@
 
 def fill_taps(planes, outputs, x_ref, masks, channels, first):
     for q, plane in enumerate(planes):
-        wide = plane.astype(F32)
         for b in range(3):
             for c in range(3):
-                view = shifted(wide, b, c, masks).astype(BF16)
+                view = shifted(plane, b, c, masks)
                 for a in range(3):
                     j = q - a
                     if 0 <= j < outputs:
@@ -176,6 +178,7 @@
     share_c_ref,
     scale_ref,
     send_ref,
+    head_cot_ref,
 ):
     shares = (share_ref, share_a_ref, share_b_ref, share_c_ref)
     for distance, ref in enumerate(shares):
@@ -201,15 +204,21 @@
         scaled = normed * gain + shift
         activated = jnp.where(scaled > 0, scaled, leak_slope * scaled)
         output = (own_ref[j, :192].astype(F32) + activated).astype(BF16)
-        logits = jnp.dot(head_turned_ref[...], output, preferred_element_type=F32)
-        raised = jnp.exp(logits - jnp.max(logits, axis=0, keepdims=True))
-        prob = raised / jnp.sum(raised, axis=0, keepdims=True)
-        hot = jnp.where(class_id == label_ref[j : j + 1, :], 1.0, 0.0)
-        delta = (prob - hot).astype(BF16)
-        head_cot = jnp.dot(head_ref[...], delta, preferred_element_type=F32)
-        upstream = jnp.where(last, head_cot, out_cot_ref[j].astype(F32)) + jnp.where(
-            decoder, 0.0, skip_cot_ref[j].astype(F32)
-        )
+
+        @pl.when(last)
+        def head(output=output, j=j):
+            logits = jnp.dot(head_turned_ref[...], output, preferred_element_type=F32)
+            raised = jnp.exp(logits - jnp.max(logits, axis=0, keepdims=True))
+            prob = raised / jnp.sum(raised, axis=0, keepdims=True)
+            hot = jnp.where(class_id == label_ref[j : j + 1, :], 1.0, 0.0)
+            delta = (prob - hot).astype(BF16)
+            head_cot_ref[j] = jnp.dot(head_ref[...], delta, preferred_element_type=F32)
+
+        @pl.when(jnp.logical_not(last))
+        def given(j=j):
+            head_cot_ref[j] = out_cot_ref[j].astype(F32)
+
+        upstream = head_cot_ref[j] + jnp.where(decoder, 0.0, skip_cot_ref[j].astype(F32))
         grad_act = upstream * jnp.where(scaled > 0, 1.0, leak_slope)
         up_ref[j] = upstream
         for k, part in enumerate((grad_act.astype(BF16), normed.astype(BF16))):
@@ -245,17 +254,16 @@
             wide_ref[...] = ref[4, 48 * q : 48 * q + 48].astype(F32)
             for r in range(6):
                 turned_ref[8 * r : 8 * r + 8, :] = wide_ref[pl.ds(r, 8, stride=6), :]
-            plane = turned_ref[...]
+            plane = turned_ref[...].astype(BF16)
             for b in range(3):
                 for c in range(3):
-                    view = shifted(plane, b, c, masks).astype(BF16)
+                    view = shifted(plane, b, c, masks)
                     for a in range(3):
                         j = q - a
                         if 0 <= j < 2:
                             tap = 9 * a + 3 * b + c
                             lanes = (2 * peer + j) * AREA
                             taps_ref[tap * 48 : (tap + 1) * 48, lanes : lanes + AREA] = view
-    taps_ref[1296:1344, :] = jnp.zeros((48, 8 * AREA), BF16)
 
 
 def kernel_grads(
@@ -295,14 +303,12 @@
         taps_ref[...], gz_ref[...], (((1,), (1,)), ((), ())), preferred_element_type=F32
     )
     low_ref[...] = grads[:, :128]
-    rest_ref[...] = jnp.concatenate([grads[:672, 128:], grads[672:, 128:]], axis=1)
-    pad = jnp.zeros((4, 384), F32)
+    rest_ref[...] = jnp.concatenate([grads[:648, 128:], grads[648:, 128:]], axis=1)
+    pad = jnp.zeros((5, AREA), F32)
     for z in range(8):
-        first = low_ref[pl.ds(z, 84, stride=8), :]
-        second = low_ref[pl.ds(z + 672, 84, stride=8), :]
-        third = rest_ref[pl.ds(z, 84, stride=8), :]
-        both = jnp.concatenate([first, second, third], axis=1)
-        out_ref[z] = jnp.concatenate([both, pad], axis=0).astype(BF16)
+        first = low_ref[pl.ds(z, 162, stride=8), :]
+        second = rest_ref[pl.ds(z, 81, stride=8), :]
+        out_ref[z] = jnp.concatenate([first, second, pad], axis=0).astype(BF16)
 
 
 def input_grads(
@@ -322,14 +328,8 @@
     mix_ref,
     sems,
 ):
-    spans = ((0, 1920), (1920, 3840), (3840, 5184))
-    copies = []
-    for part, (start, stop) in enumerate(spans):
-        band = pl.ds(start, stop - start)
-        copies.append(
-            pltpu.make_async_copy(w_ref.at[:, band], w_here_ref.at[:, band], sems.at[part])
-        )
-        copies[part].start()
+    fetch = pltpu.make_async_copy(w_ref, w_here_ref, sems.at[0])
+    fetch.start()
     decoder = flag_ref[0] == 1
     total_cells = 2.0 * AREA * recv_ref.shape[0]
     masks = tap_masks()
@@ -344,21 +344,17 @@
             grad_z = jnp.where(flag_ref[2] == 1, grad_z, 0.0)
         if q == 3:
             grad_z = jnp.where(flag_ref[3] == 1, grad_z, 0.0)
+        grad_z = grad_z.astype(BF16)
         for b in range(3):
             for c in range(3):
-                view = shifted(grad_z, 2 - b, 2 - c, masks).astype(BF16)
+                view = shifted(grad_z, 2 - b, 2 - c, masks)
                 for a in range(3):
                     j = q + a - 2
                     if 0 <= j < 2:
                         tap = 9 * a + 3 * b + c
                         x_ref[tap * 192 : (tap + 1) * 192, j * AREA : (j + 1) * AREA] = view
-    back = None
-    for copy, (start, stop) in zip(copies, spans):
-        copy.wait()
-        part = jnp.dot(
-            w_here_ref[:, start:stop], x_ref[start:stop, :], preferred_element_type=F32
-        )
-        back = part if back is None else back + part
+    fetch.wait()
+    back = jnp.dot(w_here_ref[...], x_ref[...], preferred_element_type=F32)
     for j in range(2):
         mix_ref[pl.ds(j, 192, stride=2), :] = up_ref[j] + back[:, j * AREA : (j + 1) * AREA]
     grad = mix_ref[...]
@@ -374,12 +370,11 @@
 
 def sum_rows(scale_out, recv_ref, out_ref, wide_ref):
     total = jnp.sum(recv_ref[...].astype(F32), axis=0) * scale_out
+    rest = jnp.concatenate([total[162:243, :64], total[162:243, 64:]], axis=0)
 
     def block(tap):
-        half, row = tap // 14, 6 * (tap % 14)
-        low = total[row : row + 6, half * 128 : half * 128 + 128]
-        rest = total[row : row + 6, 256 + half * 64 : 320 + half * 64]
-        return [low, rest]
+        rows = slice(6 * tap, 6 * tap + 6)
+        return [total[rows], rest[rows]]
 
     for tap in range(0, TAPS, 2):
         parts = block(tap) + (block(tap + 1) if tap + 1 < TAPS else [])
@@ -473,7 +468,7 @@
             ((192, AREA), F32),
             ((slabs, 4, AREA), F32),
         ],
-        [],
+        HEAD_SCRATCH,
         4 * 192 * 105 * 512,
         4000000,
         flags,
@@ -510,12 +505,12 @@
     sums, fwd_out = lax.optimization_barrier((sums, fwd_out))
     parts, shift_grad, gain_grad = call(
         kernel_grads,
-        [((8, 88, 384), BF16), ((1, 192), F32), ((1, 192), F32)],
+        [((8, 248, AREA), BF16), ((1, 192), F32), ((1, 192), F32)],
         [
-            ((1344, 1024), BF16),
+            ((1296, 1024), BF16),
             ((192, 1024), BF16),
-            ((1344, AREA), F32),
-            ((672, AREA), F32),
+            ((1296, AREA), F32),
+            ((648, AREA), F32),
             ((48, AREA), F32),
             ((48, AREA), F32),
         ],

time: 80.2 us -> 79.4 us (0.990)
  no operation moved by 1% of the time
where the time goes in v4:
time: 79.4 us; the launch traced here: 79 us
  starting transfers between devices  36.9 us (46%)
  waiting for transfers between devices  24.7 us (31%)
  Pallas kernels  15.1 us (19%)
  other arithmetic  1.2 us (2%)
  between operations  0.86 us (1%)
    ppermute x9, starting transfers between devices, moved(): return lax.ppermute(block, axis, route)  15.8 us
    pallas_call x8, Pallas kernels, call(): pl.pallas_call(body, out_shape=shapes, in_specs=specs, out_specs=[VMEM] *...  15.1 us
    all_to_all x1, starting transfers between devices, per_device(): stats = lax.all_to_all(stats_send, SLABS, 0, 0, tiled=True)  11.3 us
    all_to_all x1, waiting for transfers between devices, per_device(): stats = lax.all_to_all(stats_send, SLABS, 0, 0, tiled=True)  10.3 us
    all_to_all x1, starting transfers between devices, per_device(): summed = lax.all_to_all(parts, 'z', 0, 0, tiled=True)  5.11 us
    all_to_all x1, waiting for transfers between devices, per_device(): sums = lax.all_to_all(sums_send, SLABS, 0, 0, tiled=True)  4.83 us
    ppermute x9, waiting for transfers between devices, moved(): return lax.ppermute(block, axis, route)  4.61 us
    all_to_all x1, starting transfers between devices, per_device(): sums = lax.all_to_all(sums_send, SLABS, 0, 0, tiled=True)  4.6 us
  transfers between devices with their start and end apart: 13, of which 6 were waited for; matrix products, arithmetic and copies ran while one was open for 0% of the time, Pallas kernels for 12%

profile of v4, /device:TPU:6, one launch (start us, length us, event | category | flops | bytes accessed | tf_op | source)
XLA Modules:
  0.0 79.0 jit_solution(11923969162715692122)
XLA Ops:
  0.6 1.1 %fusion.2 = (bf16[2,192,128]{2,1,0:T(8,128)(2,1)S(1)}, bf16[2,192,128]{2,1,0:T(8,128)(2,1)S(1)}) fusion(bf16[1,192,2,128]{3,2,1,0:T(2,128)(2,1)} %param.12, bf16[1,192,2,128]{3,2,1,0:T(2,128)(2,1)} %param.11, pred[]{:T(512)S(6)} %ge.3, bf16[1,192,2,128]{3,2,1,0:T(2,128)(2,1)} %param.14, bf16[1,192,2,128]{3,2,1,0:T(2,128)(2,1)} %param.13), kind=kLoop, calls=%fused_computation.9 | loop fusion | flops 491520 | bytes 589825 | tf_op jit(solution)/shard_map/transpose | solution.py:430
  1.8 3.8 %collective-permute-start = (bf16[384,128]{1,0:T(8,128)(2,1)S(1)}, bf16[384,128]{1,0:T(8,128)(2,1)S(1)}, u32[]{:S(2)}, u32[]{:S(2)}) collective-permute-start(bf16[384,128]{1,0:T(8,128)(2,1)S(1)} %get-tuple-element.63), channel_id=1, source_target_pairs={{0,1},{1,2},{2,3},{3,4},{4,5},{5,6},{6,7},{7,8},{8,9},{9,10},{10,1... | collective-permute-start | bytes 294920 | tf_op jit(solution)/shard_map/ppermute | solution.py:395
  5.6 1.3 %collective-permute-start.1 = (bf16[384,128]{1,0:T(8,128)(2,1)S(1)}, bf16[384,128]{1,0:T(8,128)(2,1)S(1)}, u32[]{:S(2)}, u32[]{:S(2)}) collective-permute-start(bf16[384,128]{1,0:T(8,128)(2,1)S(1)} %get-tuple-element.62), channel_id=1, source_target_pairs={{1,0},{2,1},{3,2},{4,3},{5,4},{6,5},{7,6},{8,7},{9,8},{10,9},{11,1... | collective-permute-start | bytes 294920 | tf_op jit(solution)/shard_map/ppermute | solution.py:395
  6.9 0.0 copy-start
  6.9 0.0 slice-start
  7.0 0.0 slice-start.1
  7.0 0.0 slice-start.2
  7.0 0.0 slice-start.3
  7.0 2.5 %turn_weights.1.wt_ref = bf16[192,5184]{1,0:T(8,128)(2,1)S(1)} custom-call(bf16[192,5184]{1,0:T(8,128)(2,1)} %bitcast.32), custom_call_target="tpu_custom_call" | custom-call | bytes 3981312 | tf_op jit(solution)/shard_map/turn_weights/pallas_call | solution.py:34
  9.5 0.0 copy-done
  9.5 0.1 copy.25
  9.6 0.1 stack.39.flag_ref
  9.7 0.0 slice-done
  9.7 0.0 slice-done.1
  9.7 0.0 slice-done.2
  9.7 0.0 slice-done.3
  9.7 0.1 maximum_maximum_fusion.affine_ref
  9.8 0.0 copy-start.2
  9.8 0.0 copy-start.3
  9.8 0.0 copy-start.1
  9.8 0.0 collective-permute-done.low_ref
  9.8 2.3 %collective-permute-done.1.high_ref = bf16[384,128]{1,0:T(8,128)(2,1)S(1)} collective-permute-done((bf16[384,128]{1,0:T(8,128)(2,1)S(1)}, bf16[384,128]{1,0:T(8,128)(2,1)S(1)}, u32[]{:S(2)}, u32[]{:S(2)}) %collective-permute-start.1) | collective-permute-done | bytes 98336 | tf_op jit(solution)/shard_map/ppermute | solution.py:395
  12.1 2.7 %conv_both.1 = (f32[4,192,128]{2,1,0:T(8,128)S(1)}, f32[32,6,128]{2,1,0:T(8,128)}) custom-call(bf16[2,384,128]{2,1,0:T(8,128)(2,1)S(1)} %pad_maximum_fusion.own_ref, bf16[384,128]{1,0:T(8,128)(2,1)S(1)} %collective-permute-done.low_ref, bf16[384,128]{1,0:T(8,128)(2,1)S(1)} %collective-permute-done.1.high_ref, bf16[192,5184]{1,0:T(8,128)(2,1)S(1)} %turn_weights.1.wt_ref), custom_call_target="tpu_custom_call" | custom-call | flops 1019215872 | bytes 5000000 | tf_op jit(solution)/shard_map/conv_both/pallas_call | solution.py:34
  14.8 11.3 %all-to-all-start = ((f32[32,6,128]{2,1,0:T(8,128)}), f32[32,6,128]{2,1,0:T(8,128)S(1)}, u32[]{:S(2)}, u32[]{:S(2)}) async-start(f32[32,6,128]{2,1,0:T(8,128)} %get-tuple-element.35), calls=%async_computation | async-start | bytes 262144 | tf_op jit(solution)/shard_map/all_to_all | solution.py:460
  26.2 0.0 copy-done.2
  26.2 0.0 copy-done.3
  26.2 10.3 %all-to-all-done.recv_ref = f32[32,6,128]{2,1,0:T(8,128)S(1)} async-done(((f32[32,6,128]{2,1,0:T(8,128)}), f32[32,6,128]{2,1,0:T(8,128)S(1)}, u32[]{:S(2)}, u32[]{:S(2)}) %all-to-all-start) | async-done | bytes 98336 | tf_op jit(solution)/shard_map/all_to_all | solution.py:460
  36.6 0.0 copy-done.1
  36.6 2.2 %head_and_sums.1 = (f32[2,192,128]{2,1,0:T(8,128)S(1)}, bf16[5,192,128]{2,1,0:T(8,128)(2,1)S(1)}, bf16[5,192,128]{2,1,0:T(8,128)(2,1)}, bf16[5,192,128]{2,1,0:T(...) custom-call(s32[5]{0:T(128)S(1)} %stack.39.flag_ref, ...), custom_call_target="tpu_custom_call" | custom-call | flops 41287680 | bytes 4000000 | tf_op jit(solution)/shard_map/head_and_sums/pallas_call | solution.py:34
  38.8 0.6 collective-permute-start.2
  39.4 2.0 %collective-permute-start.3 = (bf16[5,192,128]{2,1,0:T(8,128)(2,1)S(1)}, bf16[5,192,128]{2,1,0:T(8,128)(2,1)S(1)}, u32[]{:S(2)}, u32[]{:S(2)}) collective-permute-start(bf16[5,192,128]{2,1,0:T(8,128)(2,1)S(1)} %get-tuple-element.43), channel_id=1, source_target_pairs={{0,16},{8,24},{16,0},{24,8},{1,17},{9,25},{17,1},{25,9},{2,18},{10... | collective-permute-start | bytes 737288 | tf_op jit(solution)/shard_map/ppermute | solution.py:395
  41.4 1.3 %collective-permute-start.4 = (bf16[5,192,128]{2,1,0:T(8,128)(2,1)S(1)}, bf16[5,192,128]{2,1,0:T(8,128)(2,1)S(1)}, u32[]{:S(2)}, u32[]{:S(2)}) collective-permute-start(bf16[5,192,128]{2,1,0:T(8,128)(2,1)S(1)} %get-tuple-element.44), channel_id=1, source_target_pairs={{0,24},{8,0},{16,8},{24,16},{1,25},{9,1},{17,9},{25,17},{2,26},{10... | collective-permute-start | bytes 737288 | tf_op jit(solution)/shard_map/ppermute | solution.py:395
  42.7 4.6 %all-to-all-start.1 = ((f32[32,4,128]{2,1,0:T(4,128)}), f32[32,4,128]{2,1,0:T(4,128)S(1)}, u32[]{:S(2)}, u32[]{:S(2)}) async-start(f32[32,4,128]{2,1,0:T(4,128)} %get-tuple-element.36), calls=%async_computation.1 | async-start | bytes 131072 | tf_op jit(solution)/shard_map/all_to_all | solution.py:488
  47.3 0.5 forward_out.1
  47.8 3.7 %collective-permute-start.5 = (bf16[2,192,128]{2,1,0:T(8,128)(2,1)S(1)}, bf16[2,192,128]{2,1,0:T(8,128)(2,1)S(1)}, u32[]{:S(2)}, u32[]{:S(2)}) collective-permute-start(bf16[2,192,128]{2,1,0:T(8,128)(2,1)S(1)} %get-tuple-element.47), channel_id=1, source_target_pairs={{0,1},{1,2},{2,3},{3,4},{4,5},{5,6},{6,7},{7,8},{8,9},{9,10},{10,1... | collective-permute-start | bytes 294920 | tf_op jit(solution)/shard_map/ppermute | solution.py:395
  51.5 1.3 %collective-permute-start.6 = (bf16[2,192,128]{2,1,0:T(8,128)(2,1)S(1)}, bf16[2,192,128]{2,1,0:T(8,128)(2,1)S(1)}, u32[]{:S(2)}, u32[]{:S(2)}) collective-permute-start(bf16[2,192,128]{2,1,0:T(8,128)(2,1)S(1)} %get-tuple-element.48), channel_id=1, source_target_pairs={{1,0},{2,1},{3,2},{4,3},{5,4},{6,5},{7,6},{8,7},{9,8},{10,9},{11,1... | collective-permute-start | bytes 294920 | tf_op jit(solution)/shard_map/ppermute | solution.py:395
  52.8 4.8 %all-to-all-done.1.recv_ref = f32[32,4,128]{2,1,0:T(4,128)S(1)} async-done(((f32[32,4,128]{2,1,0:T(4,128)}), f32[32,4,128]{2,1,0:T(4,128)S(1)}, u32[]{:S(2)}, u32[]{:S(2)}) %all-to-all-start.1) | async-done | bytes 65568 | tf_op jit(solution)/shard_map/all_to_all | solution.py:488
  57.7 0.0 collective-permute-done.2.a_ref
  57.7 0.0 collective-permute-done.3.b_ref
  57.7 0.0 collective-permute-done.4.c_ref
  57.7 2.2 %kernel_grads.1 = (bf16[8,248,128]{2,1,0:T(8,128)(2,1)}, f32[1,192]{1,0:T(1,128)}, f32[1,192]{1,0:T(1,128)}) custom-call(f32[32,4,128]{2,1,0:T(4,128)S(1)} %all-to-all-done.1.recv_ref, bf16[5,192,128]{2,1,0:T(8,128)(2,1)S(1)} %get-tuple-element.37.share_ref.own_ref, bf16[5,192,128]{2,1,0:T(8,128)(2,1)S(1)} %collective-permute-done.2.a_ref, ...), custom_call_target="tpu_custom_call" | custom-call | bytes 1000 | tf_op jit(solution)/shard_map/kernel_grads/pallas_call | solution.py:34
  59.9 0.0 collective-permute-done.5.low_ref
  59.9 0.0 collective-permute-done.6.high_ref
  59.9 5.1 %all-to-all-start.2 = ((bf16[8,248,128]{2,1,0:T(8,128)(2,1)}), bf16[8,248,128]{2,1,0:T(8,128)(2,1)S(1)}, u32[]{:S(2)}, u32[]{:S(2)}) async-start(bf16[8,248,128]{2,1,0:T(8,128)(2,1)} %get-tuple-element.59), calls=%async_computation.2 | async-start | bytes 1015808 | tf_op jit(solution)/shard_map/all_to_all | solution.py:524
  65.0 3.5 %input_grads.1 = (bf16[384,128]{1,0:T(8,128)(2,1)S(1)}, bf16[384,128]{1,0:T(8,128)(2,1)S(1)}) custom-call(s32[5]{0:T(128)S(1)} %stack.39.flag_ref, bf16[192,5184]{1,0:T(8,128)(2,1)} %bitcast.33, f32[32,4,128]{2,1,0:T(4,128)S(1)} %all-to-all-done.1.recv_ref, bf16[5,192,128]{2,1,0:T(8,128)(2,1)S(1)} %get-tuple-element.37.share_ref.own_ref, ...), custom_call_target="tpu_custom_call" | custom-call | flops 509607936 | bytes 4000000 | tf_op jit(solution)/shard_map/input_grads/pallas_call | solution.py:34
  68.5 0.0 collective-permute-start.7
  68.5 1.7 %collective-permute-start.8 = (bf16[384,128]{1,0:T(8,128)(2,1)S(1)}, bf16[384,128]{1,0:T(8,128)(2,1)S(1)}, u32[]{:S(2)}, u32[]{:S(2)}) collective-permute-start(bf16[384,128]{1,0:T(8,128)(2,1)S(1)} %get-tuple-element.54), channel_id=1, source_target_pairs={{0,224},{32,0},{64,32},{96,64},{128,96},{160,128},{192,160},{224,1... | collective-permute-start | bytes 294920 | tf_op jit(solution)/shard_map/ppermute | solution.py:395
  70.2 0.0 collective-permute-start.9
  70.2 2.3 %collective-permute-done.7.one_ref = bf16[384,128]{1,0:T(8,128)(2,1)S(1)} collective-permute-done((bf16[384,128]{1,0:T(8,128)(2,1)S(1)}, bf16[384,128]{1,0:T(8,128)(2,1)S(1)}, u32[]{:S(2)}, u32[]{:S(2)}) %collective-permute-start.7) | collective-permute-done | bytes 98336 | tf_op jit(solution)/shard_map/ppermute | solution.py:395
  72.5 0.0 collective-permute-done.8.two_ref
  72.5 4.0 %collective-permute-done.9.three_ref = bf16[384,128]{1,0:T(8,128)(2,1)S(1)} collective-permute-done((bf16[384,128]{1,0:T(8,128)(2,1)S(1)}, bf16[384,128]{1,0:T(8,128)(2,1)S(1)}, u32[]{:S(2)}, u32[]{:S(2)}) %collective-permute-start.9) | collective-permute-done | bytes 98336 | tf_op jit(solution)/shard_map/ppermute | solution.py:547
  76.5 0.7 hand_over.1
  77.2 0.9 %all-to-all-done.2.recv_ref = bf16[8,248,128]{2,1,0:T(8,128)(2,1)S(1)} async-done(((bf16[8,248,128]{2,1,0:T(8,128)(2,1)}), bf16[8,248,128]{2,1,0:T(8,128)(2,1)S(1)}, u32[]{:S(2)}, u32[]{:S(2)}) %all-to-all-start.2) | async-done | bytes 507936 | tf_op jit(solution)/shard_map/all_to_all | solution.py:524
  78.1 0.8 %kernel.1 = f32[6,1,5184]{2,1,0:T(1,128)} custom-call(bf16[8,248,128]{2,1,0:T(8,128)(2,1)S(1)} %all-to-all-done.2.recv_ref), custom_call_target="tpu_custom_call" | custom-call | bytes 1000000 | tf_op jit(solution)/shard_map/kernel/pallas_call | solution.py:34
  (3 shorter events, 0.1 us)
Async XLA Ops:
  1.8 8.0 %collective-permute-start = (bf16[384,128]{1,0:T(8,128)(2,1)S(1)}, bf16[384,128]{1,0:T(8,128)(2,1)S(1)}, u32[]{:S(2)}, u32[]{:S(2)}) collective-permute-start(bf16[384,128]{1,0:T(8,128)(2,1)S(1)} %get-tuple-element.63), channel_id=1, source_target_pairs={{0,1},{1,2},{2,3},{3,4},{4,5},{5,6},{6,7},{7,8},{8,9},{9,10},{10,1... | collective-permute-start | bytes 294920 | tf_op jit(solution)/shard_map/ppermute | solution.py:395
  5.6 6.5 %collective-permute-start.1 = (bf16[384,128]{1,0:T(8,128)(2,1)S(1)}, bf16[384,128]{1,0:T(8,128)(2,1)S(1)}, u32[]{:S(2)}, u32[]{:S(2)}) collective-permute-start(bf16[384,128]{1,0:T(8,128)(2,1)S(1)} %get-tuple-element.62), channel_id=1, source_target_pairs={{1,0},{2,1},{3,2},{4,3},{5,4},{6,5},{7,6},{8,7},{9,8},{10,9},{11,1... | collective-permute-start | bytes 294920 | tf_op jit(solution)/shard_map/ppermute | solution.py:395
  6.9 2.5 %copy-start = (bf16[192,105]{1,0:T(8,128)(2,1)S(1)}, bf16[192,105]{1,0:T(8,128)(2,1)}, u32[]{:S(2)}) copy-start(bf16[192,105]{1,0:T(8,128)(2,1)} %head_ref.1) | copy-start | bytes 120964
  6.9 2.7 %slice-start = ((f32[1,192]{1,0:T(1,128)}), f32[1,64]{1,0:T(1,128)S(1)}, s32[]{:S(2)}) async-start(f32[1,192]{1,0:T(1,128)} %param.19), calls=%async_computation.3 | async-start | bytes 1024 | tf_op jit(solution)/shard_map/slice | solution.py:388
  7.0 2.7 %slice-start.1 = ((f32[1,192]{1,0:T(1,128)}), f32[1,128]{1,0:T(1,128)S(1)}, s32[]{:S(2)}) async-start(f32[1,192]{1,0:T(1,128)} %param.19), calls=%async_computation.4 | async-start | bytes 1024 | tf_op jit(solution)/shard_map/slice | solution.py:389
  7.0 2.7 %slice-start.2 = ((f32[1,192]{1,0:T(1,128)}), f32[1,64]{1,0:T(1,128)S(1)}, s32[]{:S(2)}) async-start(f32[1,192]{1,0:T(1,128)} %param.18), calls=%async_computation.5 | async-start | bytes 1024 | tf_op jit(solution)/shard_map/slice | solution.py:388
  7.0 2.7 %slice-start.3 = ((f32[1,192]{1,0:T(1,128)}), f32[1,128]{1,0:T(1,128)S(1)}, s32[]{:S(2)}) async-start(f32[1,192]{1,0:T(1,128)} %param.18), calls=%async_computation.6 | async-start | bytes 1024 | tf_op jit(solution)/shard_map/slice | solution.py:389
  9.8 16.4 %copy-start.2 = (bf16[1,192,2,128]{3,2,1,0:T(2,128)(2,1)S(1)}, bf16[1,192,2,128]{3,2,1,0:T(2,128)(2,1)}, u32[]{:S(2)}) copy-start(bf16[1,192,2,128]{3,2,1,0:T(2,128)(2,1)} %param.16) | copy-start | bytes 294916
  9.8 16.4 %copy-start.3 = (bf16[1,192,2,128]{3,2,1,0:T(2,128)(2,1)S(1)}, bf16[1,192,2,128]{3,2,1,0:T(2,128)(2,1)}, u32[]{:S(2)}) copy-start(bf16[1,192,2,128]{3,2,1,0:T(2,128)(2,1)} %param.15) | copy-start | bytes 294916
  9.8 26.8 %copy-start.1 = (s32[2,128]{1,0:T(2,128)S(1)}, s32[2,128]{1,0:T(2,128)}, u32[]{:S(2)}) copy-start(s32[2,128]{1,0:T(2,128)} %label_ref.1) | copy-start | bytes 3076
  14.8 21.7 %all-to-all-start = ((f32[32,6,128]{2,1,0:T(8,128)}), f32[32,6,128]{2,1,0:T(8,128)S(1)}, u32[]{:S(2)}, u32[]{:S(2)}) async-start(f32[32,6,128]{2,1,0:T(8,128)} %get-tuple-element.35), calls=%async_computation | async-start | bytes 262144 | tf_op jit(solution)/shard_map/all_to_all | solution.py:460
  38.8 18.9 %collective-permute-start.2 = (bf16[5,192,128]{2,1,0:T(8,128)(2,1)}, bf16[5,192,128]{2,1,0:T(8,128)(2,1)S(1)}, u32[]{:S(2)}, u32[]{:S(2)}) collective-permute-start(bf16[5,192,128]{2,1,0:T(8,128)(2,1)} %get-tuple-element.42), channel_id=1, source_target_pairs={{0,8},{8,16},{16,24},{24,0},{1,9},{9,17},{17,25},{25,1},{2,10},{10... | collective-permute-start | bytes 737288 | tf_op jit(solution)/shard_map/ppermute | solution.py:395
  39.4 18.3 %collective-permute-start.3 = (bf16[5,192,128]{2,1,0:T(8,128)(2,1)S(1)}, bf16[5,192,128]{2,1,0:T(8,128)(2,1)S(1)}, u32[]{:S(2)}, u32[]{:S(2)}) collective-permute-start(bf16[5,192,128]{2,1,0:T(8,128)(2,1)S(1)} %get-tuple-element.43), channel_id=1, source_target_pairs={{0,16},{8,24},{16,0},{24,8},{1,17},{9,25},{17,1},{25,9},{2,18},{10... | collective-permute-start | bytes 737288 | tf_op jit(solution)/shard_map/ppermute | solution.py:395
  41.4 16.3 %collective-permute-start.4 = (bf16[5,192,128]{2,1,0:T(8,128)(2,1)S(1)}, bf16[5,192,128]{2,1,0:T(8,128)(2,1)S(1)}, u32[]{:S(2)}, u32[]{:S(2)}) collective-permute-start(bf16[5,192,128]{2,1,0:T(8,128)(2,1)S(1)} %get-tuple-element.44), channel_id=1, source_target_pairs={{0,24},{8,0},{16,8},{24,16},{1,25},{9,1},{17,9},{25,17},{2,26},{10... | collective-permute-start | bytes 737288 | tf_op jit(solution)/shard_map/ppermute | solution.py:395
  42.7 15.0 %all-to-all-start.1 = ((f32[32,4,128]{2,1,0:T(4,128)}), f32[32,4,128]{2,1,0:T(4,128)S(1)}, u32[]{:S(2)}, u32[]{:S(2)}) async-start(f32[32,4,128]{2,1,0:T(4,128)} %get-tuple-element.36), calls=%async_computation.1 | async-start | bytes 131072 | tf_op jit(solution)/shard_map/all_to_all | solution.py:488
  47.8 12.1 %collective-permute-start.5 = (bf16[2,192,128]{2,1,0:T(8,128)(2,1)S(1)}, bf16[2,192,128]{2,1,0:T(8,128)(2,1)S(1)}, u32[]{:S(2)}, u32[]{:S(2)}) collective-permute-start(bf16[2,192,128]{2,1,0:T(8,128)(2,1)S(1)} %get-tuple-element.47), channel_id=1, source_target_pairs={{0,1},{1,2},{2,3},{3,4},{4,5},{5,6},{6,7},{7,8},{8,9},{9,10},{10,1... | collective-permute-start | bytes 294920 | tf_op jit(solution)/shard_map/ppermute | solution.py:395
  51.5 8.4 %collective-permute-start.6 = (bf16[2,192,128]{2,1,0:T(8,128)(2,1)S(1)}, bf16[2,192,128]{2,1,0:T(8,128)(2,1)S(1)}, u32[]{:S(2)}, u32[]{:S(2)}) collective-permute-start(bf16[2,192,128]{2,1,0:T(8,128)(2,1)S(1)} %get-tuple-element.48), channel_id=1, source_target_pairs={{1,0},{2,1},{3,2},{4,3},{5,4},{6,5},{7,6},{8,7},{9,8},{10,9},{11,1... | collective-permute-start | bytes 294920 | tf_op jit(solution)/shard_map/ppermute | solution.py:395
  59.9 18.2 %all-to-all-start.2 = ((bf16[8,248,128]{2,1,0:T(8,128)(2,1)}), bf16[8,248,128]{2,1,0:T(8,128)(2,1)S(1)}, u32[]{:S(2)}, u32[]{:S(2)}) async-start(bf16[8,248,128]{2,1,0:T(8,128)(2,1)} %get-tuple-element.59), calls=%async_computation.2 | async-start | bytes 1015808 | tf_op jit(solution)/shard_map/all_to_all | solution.py:524
  68.5 4.1 %collective-permute-start.7 = (bf16[384,128]{1,0:T(8,128)(2,1)S(1)}, bf16[384,128]{1,0:T(8,128)(2,1)S(1)}, u32[]{:S(2)}, u32[]{:S(2)}) collective-permute-start(bf16[384,128]{1,0:T(8,128)(2,1)S(1)} %get-tuple-element.53.fwd_out_ref), channel_id=1, source_target_pairs={{0,32},{32,64},{64,96},{96,128},{128,160},{160,192},{192,224},{224... | collective-permute-start | bytes 294920 | tf_op jit(solution)/shard_map/ppermute | solution.py:395
  68.5 4.0 %collective-permute-start.8 = (bf16[384,128]{1,0:T(8,128)(2,1)S(1)}, bf16[384,128]{1,0:T(8,128)(2,1)S(1)}, u32[]{:S(2)}, u32[]{:S(2)}) collective-permute-start(bf16[384,128]{1,0:T(8,128)(2,1)S(1)} %get-tuple-element.54), channel_id=1, source_target_pairs={{0,224},{32,0},{64,32},{96,64},{128,96},{160,128},{192,160},{224,1... | collective-permute-start | bytes 294920 | tf_op jit(solution)/shard_map/ppermute | solution.py:395
  70.2 6.3 %collective-permute-start.9 = (bf16[384,128]{1,0:T(8,128)(2,1)S(1)}, bf16[384,128]{1,0:T(8,128)(2,1)S(1)}, u32[]{:S(2)}, u32[]{:S(2)}) collective-permute-start(bf16[384,128]{1,0:T(8,128)(2,1)S(1)} %get-tuple-element.55), channel_id=1, source_target_pairs={{0,224},{32,192},{64,160},{96,128},{128,96},{160,64},{192,32},{224... | collective-permute-start | bytes 294920 | tf_op jit(solution)/shard_map/ppermute | solution.py:547

commit v5 on v4

--- a/solution.py
+++ b/solution.py
@@ -142,11 +142,20 @@
                         ] = view
 
 
-def conv_both(own_ref, low_ref, high_ref, wt_ref, z_ref, send_ref, x_ref):
+def inside(flag, rows):
+    return jnp.where(flag == 1, rows, jnp.zeros_like(rows))
+
+
+def conv_both(flag_ref, own_ref, low_ref, high_ref, wt_ref, z_ref, send_ref, x_ref):
     masks = tap_masks()
     for which in range(2):
         rows = slice(192 * which, 192 * which + 192)
-        planes = [low_ref[rows], own_ref[0, rows], own_ref[1, rows], high_ref[rows]]
+        planes = [
+            inside(flag_ref[2], low_ref[rows]),
+            own_ref[0, rows],
+            own_ref[1, rows],
+            inside(flag_ref[3], high_ref[rows]),
+        ]
         fill_taps(planes, 2, x_ref, masks, 192, 2 * which)
     z = jnp.dot(wt_ref[...], x_ref[...], preferred_element_type=F32)
     outs = [z[:, j * AREA : (j + 1) * AREA] for j in range(4)]
@@ -183,10 +192,10 @@
     shares = (share_ref, share_a_ref, share_b_ref, share_c_ref)
     for distance, ref in enumerate(shares):
         rows = pl.ds(pl.multiple_of(48 * ((flag_ref[4] + distance) % 4), 16), 48)
-        ref[4, :48] = low_ref[rows]
+        ref[4, :48] = inside(flag_ref[2], low_ref[rows])
         ref[4, 48:96] = own_ref[0, rows]
         ref[4, 96:144] = own_ref[1, rows]
-        ref[4, 144:] = high_ref[rows]
+        ref[4, 144:] = inside(flag_ref[3], high_ref[rows])
     decoder = flag_ref[0] == 1
     last = flag_ref[1] == 1
     peers = recv_ref.shape[0]
@@ -389,9 +398,9 @@
     return jnp.concatenate([one[:, :128], two[:, :128], rest], axis=0)
 
 
-def moved(block, axis, distance, wrap=True):
+def moved(block, axis, distance):
     count = lax.axis_size(axis)
-    route = [(i, (i + distance) % count) for i in range(count) if wrap or 0 <= i + distance < count]
+    route = [(i, (i + distance) % count) for i in range(count)]
     return lax.ppermute(block, axis, route)
 
 
@@ -434,8 +443,8 @@
         return by_plane(jnp.where(is_decoder, added, block))
 
     own = jnp.concatenate([joined(bwd_input, bwd_skip), joined(fwd_input, fwd_skip)], axis=1)
-    low = moved(own[1], SLABS, 1, False)
-    high = moved(own[0], SLABS, -1, False)
+    low = moved(own[1], SLABS, 1)
+    high = moved(own[0], SLABS, -1)
     (turned,) = call(
         turn_weights,
         [((192, 5184), BF16)],
@@ -452,10 +461,12 @@
         [((5184, 512), BF16)],
         2 * 5184 * 192 * 512,
         5000000,
+        flags,
         own,
         low,
         high,
         turned,
+        smem=1,
     )
     stats = lax.all_to_all(stats_send, SLABS, 0, 0, tiled=True)
     out_cots = by_plane(out_cot)
@@ -500,8 +511,8 @@
         affine,
         share,
     )
-    rim_low = moved(rim_low, SLABS, 1, False)
-    rim_high = moved(rim_high, SLABS, -1, False)
+    rim_low = moved(rim_low, SLABS, 1)
+    rim_high = moved(rim_high, SLABS, -1)
     sums, fwd_out = lax.optimization_barrier((sums, fwd_out))
     parts, shift_grad, gain_grad = call(
         kernel_grads,

time: 79.4 us -> 75 us (0.945)
  starting transfers between devices: 36.9 us -> 34.4 us
  waiting for transfers between devices: 24.7 us -> 22.2 us
    all_to_all x1, starting transfers between devices: 11.3 us -> 6.68 us  [per_device(): stats = lax.all_to_all(stats_send, SLABS, 0, 0, tiled=True)]
    ppermute x9, starting transfers between devices: 15.8 us -> 19.6 us  [moved(): return lax.ppermute(block, axis, route)]
    ppermute x9, waiting for transfers between devices: 4.61 us -> 2.31 us  [moved(): return lax.ppermute(block, axis, route)]
    all_to_all x1, starting transfers between devices: 5.11 us -> 3.49 us  [per_device(): summed = lax.all_to_all(parts, 'z', 0, 0, tiled=True)]
  transfers between devices with their start and end apart: 13 -> 13, of which waited for: 6 -> 5; matrix products, arithmetic and copies ran while one was open for 0% -> 0% of each run, Pallas kernels for 12% -> 13%
where the time goes in v5:
time: 75 us; the launch traced here: 74.6 us
  starting transfers between devices  34.4 us (46%)
  waiting for transfers between devices  22.2 us (30%)
  Pallas kernels  15.7 us (21%)
  other arithmetic  1.2 us (2%)
  between operations  0.84 us (1%)
    ppermute x9, starting transfers between devices, moved(): return lax.ppermute(block, axis, route)  19.6 us
    pallas_call x8, Pallas kernels, call(): pl.pallas_call(body, out_shape=shapes, in_specs=specs, out_specs=[VMEM] *...  15.7 us
    all_to_all x1, waiting for transfers between devices, per_device(): stats = lax.all_to_all(stats_send, SLABS, 0, 0, tiled=True)  10.3 us
    all_to_all x1, starting transfers between devices, per_device(): stats = lax.all_to_all(stats_send, SLABS, 0, 0, tiled=True)  6.68 us
    all_to_all x1, starting transfers between devices, per_device(): sums = lax.all_to_all(sums_send, SLABS, 0, 0, tiled=True)  4.6 us
    all_to_all x1, waiting for transfers between devices, per_device(): sums = lax.all_to_all(sums_send, SLABS, 0, 0, tiled=True)  4.13 us
    ppermute x1, waiting for transfers between devices, per_device(): lax.ppermute(outgoing, 'segment', [(i, segments - 1 - i) for i in range(s...  4 us
    all_to_all x1, starting transfers between devices, per_device(): summed = lax.all_to_all(parts, 'z', 0, 0, tiled=True)  3.49 us
  transfers between devices with their start and end apart: 13, of which 5 were waited for; matrix products, arithmetic and copies ran while one was open for 0% of the time, Pallas kernels for 13%

profile of v5, /device:TPU:6, one launch (start us, length us, event | category | flops | bytes accessed | tf_op | source)
XLA Modules:
  0.0 74.6 jit_solution(14333307488446947598)
XLA Ops:
  0.6 1.1 %fusion.2 = (bf16[2,192,128]{2,1,0:T(8,128)(2,1)S(1)}, bf16[2,192,128]{2,1,0:T(8,128)(2,1)S(1)}) fusion(bf16[1,192,2,128]{3,2,1,0:T(2,128)(2,1)} %param.12, bf16[1,192,2,128]{3,2,1,0:T(2,128)(2,1)} %param.11, pred[]{:T(512)S(6)} %ge.3, bf16[1,192,2,128]{3,2,1,0:T(2,128)(2,1)} %param.14, bf16[1,192,2,128]{3,2,1,0:T(2,128)(2,1)} %param.13), kind=kLoop, calls=%fused_computation.9 | loop fusion | flops 491520 | bytes 589825 | tf_op jit(solution)/shard_map/transpose | solution.py:439
  1.8 2.0 %collective-permute-start = (bf16[384,128]{1,0:T(8,128)(2,1)S(1)}, bf16[384,128]{1,0:T(8,128)(2,1)S(1)}, u32[]{:S(2)}, u32[]{:S(2)}) collective-permute-start(bf16[384,128]{1,0:T(8,128)(2,1)S(1)} %get-tuple-element.63), channel_id=1, source_target_pairs={{0,1},{1,2},{2,3},{3,4},{4,5},{5,6},{6,7},{7,8},{8,9},{9,10},{10,1... | collective-permute-start | bytes 294920 | tf_op jit(solution)/shard_map/ppermute | solution.py:404
  3.8 6.5 %collective-permute-start.1 = (bf16[384,128]{1,0:T(8,128)(2,1)S(1)}, bf16[384,128]{1,0:T(8,128)(2,1)S(1)}, u32[]{:S(2)}, u32[]{:S(2)}) collective-permute-start(bf16[384,128]{1,0:T(8,128)(2,1)S(1)} %get-tuple-element.62), channel_id=1, source_target_pairs={{0,31},{1,0},{2,1},{3,2},{4,3},{5,4},{6,5},{7,6},{8,7},{9,8},{10,9... | collective-permute-start | bytes 294920 | tf_op jit(solution)/shard_map/ppermute | solution.py:404
  10.3 0.0 copy-start
  10.3 0.0 slice-start
  10.3 0.0 slice-start.1
  10.3 0.0 slice-start.2
  10.3 0.0 slice-start.3
  10.3 2.5 %turn_weights.1.wt_ref = bf16[192,5184]{1,0:T(8,128)(2,1)S(1)} custom-call(bf16[192,5184]{1,0:T(8,128)(2,1)} %bitcast.32), custom_call_target="tpu_custom_call" | custom-call | bytes 3981312 | tf_op jit(solution)/shard_map/turn_weights/pallas_call | solution.py:34
  12.8 0.0 copy-done
  12.8 0.1 copy.25
  12.9 0.1 stack.39.flag_ref
  13.0 0.0 slice-done
  13.0 0.0 slice-done.1
  13.0 0.0 slice-done.2
  13.0 0.0 slice-done.3
  13.0 0.1 maximum_maximum_fusion.affine_ref
  13.1 0.0 copy-start.2
  13.1 0.0 copy-start.3
  13.1 0.0 copy-start.1
  13.1 0.0 collective-permute-done.low_ref
  13.1 0.0 collective-permute-done.1.high_ref
  13.1 3.3 %conv_both.1 = (f32[4,192,128]{2,1,0:T(8,128)S(1)}, f32[32,6,128]{2,1,0:T(8,128)}) custom-call(s32[5]{0:T(128)S(1)} %stack.39.flag_ref, bf16[2,384,128]{2,1,0:T(8,128)(2,1)S(1)} %pad_maximum_fusion.own_ref, bf16[384,128]{1,0:T(8,128)(2,1)S(1)} %collective-permute-done.low_ref, bf16[384,128]{1,0:T(8,128)(2,1)S(1)} %collective-permute-done.1.high_ref, ...), custom_call_target="tpu_custom_call" | custom-call | flops 1019215872 | bytes 5000000 | tf_op jit(solution)/shard_map/conv_both/pallas_call | solution.py:34
  16.4 6.7 %all-to-all-start = ((f32[32,6,128]{2,1,0:T(8,128)}), f32[32,6,128]{2,1,0:T(8,128)S(1)}, u32[]{:S(2)}, u32[]{:S(2)}) async-start(f32[32,6,128]{2,1,0:T(8,128)} %get-tuple-element.35), calls=%async_computation | async-start | bytes 262144 | tf_op jit(solution)/shard_map/all_to_all | solution.py:471
  23.1 0.0 copy-done.2
  23.1 0.0 copy-done.3
  23.2 10.3 %all-to-all-done.recv_ref = f32[32,6,128]{2,1,0:T(8,128)S(1)} async-done(((f32[32,6,128]{2,1,0:T(8,128)}), f32[32,6,128]{2,1,0:T(8,128)S(1)}, u32[]{:S(2)}, u32[]{:S(2)}) %all-to-all-start) | async-done | bytes 98336 | tf_op jit(solution)/shard_map/all_to_all | solution.py:471
  33.5 0.0 copy-done.1
  33.5 2.2 %head_and_sums.1 = (f32[2,192,128]{2,1,0:T(8,128)S(1)}, bf16[5,192,128]{2,1,0:T(8,128)(2,1)S(1)}, bf16[5,192,128]{2,1,0:T(8,128)(2,1)}, bf16[5,192,128]{2,1,0:T(...) custom-call(s32[5]{0:T(128)S(1)} %stack.39.flag_ref, ...), custom_call_target="tpu_custom_call" | custom-call | flops 41287680 | bytes 4000000 | tf_op jit(solution)/shard_map/head_and_sums/pallas_call | solution.py:34
  35.6 0.6 collective-permute-start.2
  36.3 2.0 %collective-permute-start.3 = (bf16[5,192,128]{2,1,0:T(8,128)(2,1)S(1)}, bf16[5,192,128]{2,1,0:T(8,128)(2,1)S(1)}, u32[]{:S(2)}, u32[]{:S(2)}) collective-permute-start(bf16[5,192,128]{2,1,0:T(8,128)(2,1)S(1)} %get-tuple-element.43), channel_id=1, source_target_pairs={{0,16},{8,24},{16,0},{24,8},{1,17},{9,25},{17,1},{25,9},{2,18},{10... | collective-permute-start | bytes 737288 | tf_op jit(solution)/shard_map/ppermute | solution.py:404
  38.3 1.4 %collective-permute-start.4 = (bf16[5,192,128]{2,1,0:T(8,128)(2,1)S(1)}, bf16[5,192,128]{2,1,0:T(8,128)(2,1)S(1)}, u32[]{:S(2)}, u32[]{:S(2)}) collective-permute-start(bf16[5,192,128]{2,1,0:T(8,128)(2,1)S(1)} %get-tuple-element.44), channel_id=1, source_target_pairs={{0,24},{8,0},{16,8},{24,16},{1,25},{9,1},{17,9},{25,17},{2,26},{10... | collective-permute-start | bytes 737288 | tf_op jit(solution)/shard_map/ppermute | solution.py:404
  39.6 4.6 %all-to-all-start.1 = ((f32[32,4,128]{2,1,0:T(4,128)}), f32[32,4,128]{2,1,0:T(4,128)S(1)}, u32[]{:S(2)}, u32[]{:S(2)}) async-start(f32[32,4,128]{2,1,0:T(4,128)} %get-tuple-element.36), calls=%async_computation.1 | async-start | bytes 131072 | tf_op jit(solution)/shard_map/all_to_all | solution.py:499
  44.2 0.5 forward_out.1
  44.8 1.9 %collective-permute-start.5 = (bf16[2,192,128]{2,1,0:T(8,128)(2,1)S(1)}, bf16[2,192,128]{2,1,0:T(8,128)(2,1)S(1)}, u32[]{:S(2)}, u32[]{:S(2)}) collective-permute-start(bf16[2,192,128]{2,1,0:T(8,128)(2,1)S(1)} %get-tuple-element.47), channel_id=1, source_target_pairs={{0,1},{1,2},{2,3},{3,4},{4,5},{5,6},{6,7},{7,8},{8,9},{9,10},{10,1... | collective-permute-start | bytes 294920 | tf_op jit(solution)/shard_map/ppermute | solution.py:404
  46.6 3.6 %collective-permute-start.6 = (bf16[2,192,128]{2,1,0:T(8,128)(2,1)S(1)}, bf16[2,192,128]{2,1,0:T(8,128)(2,1)S(1)}, u32[]{:S(2)}, u32[]{:S(2)}) collective-permute-start(bf16[2,192,128]{2,1,0:T(8,128)(2,1)S(1)} %get-tuple-element.48), channel_id=1, source_target_pairs={{0,31},{1,0},{2,1},{3,2},{4,3},{5,4},{6,5},{7,6},{8,7},{9,8},{10,9... | collective-permute-start | bytes 294920 | tf_op jit(solution)/shard_map/ppermute | solution.py:404
  50.2 4.1 %all-to-all-done.1.recv_ref = f32[32,4,128]{2,1,0:T(4,128)S(1)} async-done(((f32[32,4,128]{2,1,0:T(4,128)}), f32[32,4,128]{2,1,0:T(4,128)S(1)}, u32[]{:S(2)}, u32[]{:S(2)}) %all-to-all-start.1) | async-done | bytes 65568 | tf_op jit(solution)/shard_map/all_to_all | solution.py:499
  54.3 0.0 collective-permute-done.2.a_ref
  54.3 0.0 collective-permute-done.3.b_ref
  54.3 0.0 collective-permute-done.4.c_ref
  54.3 2.2 %kernel_grads.1 = (bf16[8,248,128]{2,1,0:T(8,128)(2,1)}, f32[1,192]{1,0:T(1,128)}, f32[1,192]{1,0:T(1,128)}) custom-call(f32[32,4,128]{2,1,0:T(4,128)S(1)} %all-to-all-done.1.recv_ref, bf16[5,192,128]{2,1,0:T(8,128)(2,1)S(1)} %get-tuple-element.37.share_ref.own_ref, bf16[5,192,128]{2,1,0:T(8,128)(2,1)S(1)} %collective-permute-done.2.a_ref, ...), custom_call_target="tpu_custom_call" | custom-call | bytes 1000 | tf_op jit(solution)/shard_map/kernel_grads/pallas_call | solution.py:34
  56.5 0.0 collective-permute-done.5.low_ref
  56.5 0.0 collective-permute-done.6.high_ref
  56.6 3.5 %all-to-all-start.2 = ((bf16[8,248,128]{2,1,0:T(8,128)(2,1)}), bf16[8,248,128]{2,1,0:T(8,128)(2,1)S(1)}, u32[]{:S(2)}, u32[]{:S(2)}) async-start(bf16[8,248,128]{2,1,0:T(8,128)(2,1)} %get-tuple-element.59), calls=%async_computation.2 | async-start | bytes 1015808 | tf_op jit(solution)/shard_map/all_to_all | solution.py:535
  60.1 3.5 %input_grads.1 = (bf16[384,128]{1,0:T(8,128)(2,1)S(1)}, bf16[384,128]{1,0:T(8,128)(2,1)S(1)}) custom-call(s32[5]{0:T(128)S(1)} %stack.39.flag_ref, bf16[192,5184]{1,0:T(8,128)(2,1)} %bitcast.33, f32[32,4,128]{2,1,0:T(4,128)S(1)} %all-to-all-done.1.recv_ref, bf16[5,192,128]{2,1,0:T(8,128)(2,1)S(1)} %get-tuple-element.37.share_ref.own_ref, ...), custom_call_target="tpu_custom_call" | custom-call | flops 509607936 | bytes 4000000 | tf_op jit(solution)/shard_map/input_grads/pallas_call | solution.py:34
  63.5 0.0 collective-permute-start.7
  63.5 1.7 %collective-permute-start.8 = (bf16[384,128]{1,0:T(8,128)(2,1)S(1)}, bf16[384,128]{1,0:T(8,128)(2,1)S(1)}, u32[]{:S(2)}, u32[]{:S(2)}) collective-permute-start(bf16[384,128]{1,0:T(8,128)(2,1)S(1)} %get-tuple-element.54), channel_id=1, source_target_pairs={{0,224},{32,0},{64,32},{96,64},{128,96},{160,128},{192,160},{224,1... | collective-permute-start | bytes 294920 | tf_op jit(solution)/shard_map/ppermute | solution.py:404
  65.3 0.0 collective-permute-start.9
  65.3 2.3 %collective-permute-done.7.one_ref = bf16[384,128]{1,0:T(8,128)(2,1)S(1)} collective-permute-done((bf16[384,128]{1,0:T(8,128)(2,1)S(1)}, bf16[384,128]{1,0:T(8,128)(2,1)S(1)}, u32[]{:S(2)}, u32[]{:S(2)}) %collective-permute-start.7) | collective-permute-done | bytes 98336 | tf_op jit(solution)/shard_map/ppermute | solution.py:404
  67.6 0.0 collective-permute-done.8.two_ref
  67.6 4.0 %collective-permute-done.9.three_ref = bf16[384,128]{1,0:T(8,128)(2,1)S(1)} collective-permute-done((bf16[384,128]{1,0:T(8,128)(2,1)S(1)}, bf16[384,128]{1,0:T(8,128)(2,1)S(1)}, u32[]{:S(2)}, u32[]{:S(2)}) %collective-permute-start.9) | collective-permute-done | bytes 98336 | tf_op jit(solution)/shard_map/ppermute | solution.py:558
  71.6 0.7 hand_over.1
  72.3 1.5 %all-to-all-done.2.recv_ref = bf16[8,248,128]{2,1,0:T(8,128)(2,1)S(1)} async-done(((bf16[8,248,128]{2,1,0:T(8,128)(2,1)}), bf16[8,248,128]{2,1,0:T(8,128)(2,1)S(1)}, u32[]{:S(2)}, u32[]{:S(2)}) %all-to-all-start.2) | async-done | bytes 507936 | tf_op jit(solution)/shard_map/all_to_all | solution.py:535
  73.8 0.8 %kernel.1 = f32[6,1,5184]{2,1,0:T(1,128)} custom-call(bf16[8,248,128]{2,1,0:T(8,128)(2,1)S(1)} %all-to-all-done.2.recv_ref), custom_call_target="tpu_custom_call" | custom-call | bytes 1000000 | tf_op jit(solution)/shard_map/kernel/pallas_call | solution.py:34
  (3 shorter events, 0.1 us)
Async XLA Ops:
  1.8 11.4 %collective-permute-start = (bf16[384,128]{1,0:T(8,128)(2,1)S(1)}, bf16[384,128]{1,0:T(8,128)(2,1)S(1)}, u32[]{:S(2)}, u32[]{:S(2)}) collective-permute-start(bf16[384,128]{1,0:T(8,128)(2,1)S(1)} %get-tuple-element.63), channel_id=1, source_target_pairs={{0,1},{1,2},{2,3},{3,4},{4,5},{5,6},{6,7},{7,8},{8,9},{9,10},{10,1... | collective-permute-start | bytes 294920 | tf_op jit(solution)/shard_map/ppermute | solution.py:404
  3.8 9.4 %collective-permute-start.1 = (bf16[384,128]{1,0:T(8,128)(2,1)S(1)}, bf16[384,128]{1,0:T(8,128)(2,1)S(1)}, u32[]{:S(2)}, u32[]{:S(2)}) collective-permute-start(bf16[384,128]{1,0:T(8,128)(2,1)S(1)} %get-tuple-element.62), channel_id=1, source_target_pairs={{0,31},{1,0},{2,1},{3,2},{4,3},{5,4},{6,5},{7,6},{8,7},{9,8},{10,9... | collective-permute-start | bytes 294920 | tf_op jit(solution)/shard_map/ppermute | solution.py:404
  10.3 2.5 %copy-start = (bf16[192,105]{1,0:T(8,128)(2,1)S(1)}, bf16[192,105]{1,0:T(8,128)(2,1)}, u32[]{:S(2)}) copy-start(bf16[192,105]{1,0:T(8,128)(2,1)} %head_ref.1) | copy-start | bytes 120964
  10.3 2.7 %slice-start = ((f32[1,192]{1,0:T(1,128)}), f32[1,128]{1,0:T(1,128)S(1)}, s32[]{:S(2)}) async-start(f32[1,192]{1,0:T(1,128)} %param.18), calls=%async_computation.3 | async-start | bytes 1024 | tf_op jit(solution)/shard_map/slice | solution.py:398
  10.3 2.7 %slice-start.1 = ((f32[1,192]{1,0:T(1,128)}), f32[1,64]{1,0:T(1,128)S(1)}, s32[]{:S(2)}) async-start(f32[1,192]{1,0:T(1,128)} %param.18), calls=%async_computation.4 | async-start | bytes 1024 | tf_op jit(solution)/shard_map/slice | solution.py:397
  10.3 2.7 %slice-start.2 = ((f32[1,192]{1,0:T(1,128)}), f32[1,128]{1,0:T(1,128)S(1)}, s32[]{:S(2)}) async-start(f32[1,192]{1,0:T(1,128)} %param.19), calls=%async_computation.5 | async-start | bytes 1024 | tf_op jit(solution)/shard_map/slice | solution.py:398
  10.3 2.7 %slice-start.3 = ((f32[1,192]{1,0:T(1,128)}), f32[1,64]{1,0:T(1,128)S(1)}, s32[]{:S(2)}) async-start(f32[1,192]{1,0:T(1,128)} %param.19), calls=%async_computation.6 | async-start | bytes 1024 | tf_op jit(solution)/shard_map/slice | solution.py:397
  13.1 10.0 %copy-start.2 = (bf16[1,192,2,128]{3,2,1,0:T(2,128)(2,1)S(1)}, bf16[1,192,2,128]{3,2,1,0:T(2,128)(2,1)}, u32[]{:S(2)}) copy-start(bf16[1,192,2,128]{3,2,1,0:T(2,128)(2,1)} %param.16) | copy-start | bytes 294916
  13.1 10.0 %copy-start.3 = (bf16[1,192,2,128]{3,2,1,0:T(2,128)(2,1)S(1)}, bf16[1,192,2,128]{3,2,1,0:T(2,128)(2,1)}, u32[]{:S(2)}) copy-start(bf16[1,192,2,128]{3,2,1,0:T(2,128)(2,1)} %param.15) | copy-start | bytes 294916
  13.1 20.4 %copy-start.1 = (s32[2,128]{1,0:T(2,128)S(1)}, s32[2,128]{1,0:T(2,128)}, u32[]{:S(2)}) copy-start(s32[2,128]{1,0:T(2,128)} %label_ref.1) | copy-start | bytes 3076
  16.4 17.0 %all-to-all-start = ((f32[32,6,128]{2,1,0:T(8,128)}), f32[32,6,128]{2,1,0:T(8,128)S(1)}, u32[]{:S(2)}, u32[]{:S(2)}) async-start(f32[32,6,128]{2,1,0:T(8,128)} %get-tuple-element.35), calls=%async_computation | async-start | bytes 262144 | tf_op jit(solution)/shard_map/all_to_all | solution.py:471
  35.6 18.7 %collective-permute-start.2 = (bf16[5,192,128]{2,1,0:T(8,128)(2,1)}, bf16[5,192,128]{2,1,0:T(8,128)(2,1)S(1)}, u32[]{:S(2)}, u32[]{:S(2)}) collective-permute-start(bf16[5,192,128]{2,1,0:T(8,128)(2,1)} %get-tuple-element.42), channel_id=1, source_target_pairs={{0,8},{8,16},{16,24},{24,0},{1,9},{9,17},{17,25},{25,1},{2,10},{10... | collective-permute-start | bytes 737288 | tf_op jit(solution)/shard_map/ppermute | solution.py:404
  36.3 18.1 %collective-permute-start.3 = (bf16[5,192,128]{2,1,0:T(8,128)(2,1)S(1)}, bf16[5,192,128]{2,1,0:T(8,128)(2,1)S(1)}, u32[]{:S(2)}, u32[]{:S(2)}) collective-permute-start(bf16[5,192,128]{2,1,0:T(8,128)(2,1)S(1)} %get-tuple-element.43), channel_id=1, source_target_pairs={{0,16},{8,24},{16,0},{24,8},{1,17},{9,25},{17,1},{25,9},{2,18},{10... | collective-permute-start | bytes 737288 | tf_op jit(solution)/shard_map/ppermute | solution.py:404
  38.3 16.1 %collective-permute-start.4 = (bf16[5,192,128]{2,1,0:T(8,128)(2,1)S(1)}, bf16[5,192,128]{2,1,0:T(8,128)(2,1)S(1)}, u32[]{:S(2)}, u32[]{:S(2)}) collective-permute-start(bf16[5,192,128]{2,1,0:T(8,128)(2,1)S(1)} %get-tuple-element.44), channel_id=1, source_target_pairs={{0,24},{8,0},{16,8},{24,16},{1,25},{9,1},{17,9},{25,17},{2,26},{10... | collective-permute-start | bytes 737288 | tf_op jit(solution)/shard_map/ppermute | solution.py:404
  39.6 14.7 %all-to-all-start.1 = ((f32[32,4,128]{2,1,0:T(4,128)}), f32[32,4,128]{2,1,0:T(4,128)S(1)}, u32[]{:S(2)}, u32[]{:S(2)}) async-start(f32[32,4,128]{2,1,0:T(4,128)} %get-tuple-element.36), calls=%async_computation.1 | async-start | bytes 131072 | tf_op jit(solution)/shard_map/all_to_all | solution.py:499
  44.8 11.8 %collective-permute-start.5 = (bf16[2,192,128]{2,1,0:T(8,128)(2,1)S(1)}, bf16[2,192,128]{2,1,0:T(8,128)(2,1)S(1)}, u32[]{:S(2)}, u32[]{:S(2)}) collective-permute-start(bf16[2,192,128]{2,1,0:T(8,128)(2,1)S(1)} %get-tuple-element.47), channel_id=1, source_target_pairs={{0,1},{1,2},{2,3},{3,4},{4,5},{5,6},{6,7},{7,8},{8,9},{9,10},{10,1... | collective-permute-start | bytes 294920 | tf_op jit(solution)/shard_map/ppermute | solution.py:404
  46.6 9.9 %collective-permute-start.6 = (bf16[2,192,128]{2,1,0:T(8,128)(2,1)S(1)}, bf16[2,192,128]{2,1,0:T(8,128)(2,1)S(1)}, u32[]{:S(2)}, u32[]{:S(2)}) collective-permute-start(bf16[2,192,128]{2,1,0:T(8,128)(2,1)S(1)} %get-tuple-element.48), channel_id=1, source_target_pairs={{0,31},{1,0},{2,1},{3,2},{4,3},{5,4},{6,5},{7,6},{8,7},{9,8},{10,9... | collective-permute-start | bytes 294920 | tf_op jit(solution)/shard_map/ppermute | solution.py:404
  56.6 17.2 %all-to-all-start.2 = ((bf16[8,248,128]{2,1,0:T(8,128)(2,1)}), bf16[8,248,128]{2,1,0:T(8,128)(2,1)S(1)}, u32[]{:S(2)}, u32[]{:S(2)}) async-start(bf16[8,248,128]{2,1,0:T(8,128)(2,1)} %get-tuple-element.59), calls=%async_computation.2 | async-start | bytes 1015808 | tf_op jit(solution)/shard_map/all_to_all | solution.py:535
  63.5 4.1 %collective-permute-start.7 = (bf16[384,128]{1,0:T(8,128)(2,1)S(1)}, bf16[384,128]{1,0:T(8,128)(2,1)S(1)}, u32[]{:S(2)}, u32[]{:S(2)}) collective-permute-start(bf16[384,128]{1,0:T(8,128)(2,1)S(1)} %get-tuple-element.53.fwd_out_ref), channel_id=1, source_target_pairs={{0,32},{32,64},{64,96},{96,128},{128,160},{160,192},{192,224},{224... | collective-permute-start | bytes 294920 | tf_op jit(solution)/shard_map/ppermute | solution.py:404
  63.5 4.0 %collective-permute-start.8 = (bf16[384,128]{1,0:T(8,128)(2,1)S(1)}, bf16[384,128]{1,0:T(8,128)(2,1)S(1)}, u32[]{:S(2)}, u32[]{:S(2)}) collective-permute-start(bf16[384,128]{1,0:T(8,128)(2,1)S(1)} %get-tuple-element.54), channel_id=1, source_target_pairs={{0,224},{32,0},{64,32},{96,64},{128,96},{160,128},{192,160},{224,1... | collective-permute-start | bytes 294920 | tf_op jit(solution)/shard_map/ppermute | solution.py:404
  65.3 6.3 %collective-permute-start.9 = (bf16[384,128]{1,0:T(8,128)(2,1)S(1)}, bf16[384,128]{1,0:T(8,128)(2,1)S(1)}, u32[]{:S(2)}, u32[]{:S(2)}) collective-permute-start(bf16[384,128]{1,0:T(8,128)(2,1)S(1)} %get-tuple-element.55), channel_id=1, source_target_pairs={{0,224},{32,192},{64,160},{96,128},{128,96},{160,64},{192,32},{224... | collective-permute-start | bytes 294920 | tf_op jit(solution)/shard_map/ppermute | solution.py:558

commit v6 on v4

--- a/solution.py
+++ b/solution.py
@@ -389,9 +389,9 @@
     return jnp.concatenate([one[:, :128], two[:, :128], rest], axis=0)
 
 
-def moved(block, axis, distance, wrap=True):
+def moved(block, axis, distance):
     count = lax.axis_size(axis)
-    route = [(i, (i + distance) % count) for i in range(count) if wrap or 0 <= i + distance < count]
+    route = [(i, (i + distance) % count) for i in range(count)]
     return lax.ppermute(block, axis, route)
 
 
@@ -434,8 +434,9 @@
         return by_plane(jnp.where(is_decoder, added, block))
 
     own = jnp.concatenate([joined(bwd_input, bwd_skip), joined(fwd_input, fwd_skip)], axis=1)
-    low = moved(own[1], SLABS, 1, False)
-    high = moved(own[0], SLABS, -1, False)
+    nothing = jnp.zeros_like(own[0])
+    low = moved(jnp.where(slab_id < slabs - 1, own[1], nothing), SLABS, 1)
+    high = moved(jnp.where(slab_id > 0, own[0], nothing), SLABS, -1)
     (turned,) = call(
         turn_weights,
         [((192, 5184), BF16)],
@@ -500,8 +501,8 @@
         affine,
         share,
     )
-    rim_low = moved(rim_low, SLABS, 1, False)
-    rim_high = moved(rim_high, SLABS, -1, False)
+    rim_low = moved(rim_low, SLABS, 1)
+    rim_high = moved(rim_high, SLABS, -1)
     sums, fwd_out = lax.optimization_barrier((sums, fwd_out))
     parts, shift_grad, gain_grad = call(
         kernel_grads,

time: 79.4 us -> 74.5 us (0.938)
  starting transfers between devices: 36.9 us -> 34.4 us
  waiting for transfers between devices: 24.7 us -> 22.2 us
    all_to_all x1, starting transfers between devices: 11.3 us -> 6.7 us  [per_device(): stats = lax.all_to_all(stats_send, SLABS, 0, 0, tiled=True)]
    ppermute x9, starting transfers between devices: 15.8 us -> 19.6 us  [moved(): return lax.ppermute(block, axis, route)]
    ppermute x9, waiting for transfers between devices: 4.61 us -> 2.31 us  [moved(): return lax.ppermute(block, axis, route)]
    all_to_all x1, starting transfers between devices: 5.11 us -> 3.49 us  [per_device(): summed = lax.all_to_all(parts, 'z', 0, 0, tiled=True)]
  transfers between devices with their start and end apart: 13 -> 13, of which waited for: 6 -> 5; matrix products, arithmetic and copies ran while one was open for 0% -> 0% of each run, Pallas kernels for 12% -> 13%
where the time goes in v6:
time: 74.5 us; the launch traced here: 74.1 us
  starting transfers between devices  34.4 us (46%)
  waiting for transfers between devices  22.2 us (30%)
  Pallas kernels  15.1 us (20%)
  other arithmetic  1.23 us (2%)
  between operations  0.84 us (1%)
    ppermute x9, starting transfers between devices, moved(): return lax.ppermute(block, axis, route)  19.6 us
    pallas_call x8, Pallas kernels, call(): pl.pallas_call(body, out_shape=shapes, in_specs=specs, out_specs=[VMEM] *...  15.1 us
    all_to_all x1, waiting for transfers between devices, per_device(): stats = lax.all_to_all(stats_send, SLABS, 0, 0, tiled=True)  10.3 us
    all_to_all x1, starting transfers between devices, per_device(): stats = lax.all_to_all(stats_send, SLABS, 0, 0, tiled=True)  6.7 us
    all_to_all x1, starting transfers between devices, per_device(): sums = lax.all_to_all(sums_send, SLABS, 0, 0, tiled=True)  4.6 us
    all_to_all x1, waiting for transfers between devices, per_device(): sums = lax.all_to_all(sums_send, SLABS, 0, 0, tiled=True)  4.13 us
    ppermute x1, waiting for transfers between devices, per_device(): lax.ppermute(outgoing, 'segment', [(i, segments - 1 - i) for i in range(s...  4 us
    all_to_all x1, starting transfers between devices, per_device(): summed = lax.all_to_all(parts, 'z', 0, 0, tiled=True)  3.49 us
  transfers between devices with their start and end apart: 13, of which 5 were waited for; matrix products, arithmetic and copies ran while one was open for 0% of the time, Pallas kernels for 13%

profile of v6, /device:TPU:6, one launch (start us, length us, event | category | flops | bytes accessed | tf_op | source)
XLA Modules:
  0.0 74.1 jit_solution(7739893277829658676)
XLA Ops:
  0.6 1.1 %fusion.2 = (bf16[2,192,128]{2,1,0:T(8,128)(2,1)S(1)}, bf16[2,192,128]{2,1,0:T(8,128)(2,1)S(1)}) fusion(bf16[1,192,2,128]{3,2,1,0:T(2,128)(2,1)} %param.12, bf16[1,192,2,128]{3,2,1,0:T(2,128)(2,1)} %param.11, pred[]{:T(512)S(6)} %ge.3, bf16[1,192,2,128]{3,2,1,0:T(2,128)(2,1)} %param.14, bf16[1,192,2,128]{3,2,1,0:T(2,128)(2,1)} %param.13), kind=kLoop, calls=%fused_computation.9 | loop fusion | flops 491520 | bytes 589825 | tf_op jit(solution)/shard_map/transpose | solution.py:430
  1.8 2.0 %collective-permute-start = (bf16[384,128]{1,0:T(8,128)(2,1)S(1)}, bf16[384,128]{1,0:T(8,128)(2,1)S(1)}, u32[]{:S(2)}, u32[]{:S(2)}) collective-permute-start(bf16[384,128]{1,0:T(8,128)(2,1)S(1)} %get-tuple-element.63), channel_id=1, source_target_pairs={{0,1},{1,2},{2,3},{3,4},{4,5},{5,6},{6,7},{7,8},{8,9},{9,10},{10,1... | collective-permute-start | bytes 294920 | tf_op jit(solution)/shard_map/ppermute | solution.py:395
  3.8 6.5 %collective-permute-start.1 = (bf16[384,128]{1,0:T(8,128)(2,1)S(1)}, bf16[384,128]{1,0:T(8,128)(2,1)S(1)}, u32[]{:S(2)}, u32[]{:S(2)}) collective-permute-start(bf16[384,128]{1,0:T(8,128)(2,1)S(1)} %get-tuple-element.62), channel_id=1, source_target_pairs={{0,31},{1,0},{2,1},{3,2},{4,3},{5,4},{6,5},{7,6},{8,7},{9,8},{10,9... | collective-permute-start | bytes 294920 | tf_op jit(solution)/shard_map/ppermute | solution.py:395
  10.3 0.0 copy-start
  10.3 0.0 slice-start
  10.3 0.0 slice-start.1
  10.3 0.0 slice-start.2
  10.3 0.0 slice-start.3
  10.4 2.5 %turn_weights.1.wt_ref = bf16[192,5184]{1,0:T(8,128)(2,1)S(1)} custom-call(bf16[192,5184]{1,0:T(8,128)(2,1)} %bitcast.32), custom_call_target="tpu_custom_call" | custom-call | bytes 3981312 | tf_op jit(solution)/shard_map/turn_weights/pallas_call | solution.py:34
  12.8 0.0 copy-done
  12.8 0.1 copy.25
  13.0 0.1 stack.39.flag_ref
  13.0 0.0 slice-done
  13.1 0.0 slice-done.1
  13.1 0.0 slice-done.2
  13.1 0.0 slice-done.3
  13.1 0.1 maximum_maximum_fusion.affine_ref
  13.2 0.0 copy-start.2
  13.2 0.0 copy-start.3
  13.2 0.0 copy-start.1
  13.2 0.0 collective-permute-done.low_ref
  13.2 0.0 collective-permute-done.1.high_ref
  13.2 2.7 %conv_both.1 = (f32[4,192,128]{2,1,0:T(8,128)S(1)}, f32[32,6,128]{2,1,0:T(8,128)}) custom-call(bf16[2,384,128]{2,1,0:T(8,128)(2,1)S(1)} %pad_maximum_fusion.own_ref, bf16[384,128]{1,0:T(8,128)(2,1)S(1)} %collective-permute-done.low_ref, bf16[384,128]{1,0:T(8,128)(2,1)S(1)} %collective-permute-done.1.high_ref, bf16[192,5184]{1,0:T(8,128)(2,1)S(1)} %turn_weights.1.wt_ref), custom_call_target="tpu_custom_call" | custom-call | flops 1019215872 | bytes 5000000 | tf_op jit(solution)/shard_map/conv_both/pallas_call | solution.py:34
  15.9 6.7 %all-to-all-start = ((f32[32,6,128]{2,1,0:T(8,128)}), f32[32,6,128]{2,1,0:T(8,128)S(1)}, u32[]{:S(2)}, u32[]{:S(2)}) async-start(f32[32,6,128]{2,1,0:T(8,128)} %get-tuple-element.35), calls=%async_computation | async-start | bytes 262144 | tf_op jit(solution)/shard_map/all_to_all | solution.py:461
  22.6 0.0 copy-done.2
  22.6 0.0 copy-done.3
  22.7 10.3 %all-to-all-done.recv_ref = f32[32,6,128]{2,1,0:T(8,128)S(1)} async-done(((f32[32,6,128]{2,1,0:T(8,128)}), f32[32,6,128]{2,1,0:T(8,128)S(1)}, u32[]{:S(2)}, u32[]{:S(2)}) %all-to-all-start) | async-done | bytes 98336 | tf_op jit(solution)/shard_map/all_to_all | solution.py:461
  33.0 0.0 copy-done.1
  33.0 2.2 %head_and_sums.1 = (f32[2,192,128]{2,1,0:T(8,128)S(1)}, bf16[5,192,128]{2,1,0:T(8,128)(2,1)S(1)}, bf16[5,192,128]{2,1,0:T(8,128)(2,1)}, bf16[5,192,128]{2,1,0:T(...) custom-call(s32[5]{0:T(128)S(1)} %stack.39.flag_ref, ...), custom_call_target="tpu_custom_call" | custom-call | flops 41287680 | bytes 4000000 | tf_op jit(solution)/shard_map/head_and_sums/pallas_call | solution.py:34
  35.1 0.6 collective-permute-start.2
  35.8 2.0 %collective-permute-start.3 = (bf16[5,192,128]{2,1,0:T(8,128)(2,1)S(1)}, bf16[5,192,128]{2,1,0:T(8,128)(2,1)S(1)}, u32[]{:S(2)}, u32[]{:S(2)}) collective-permute-start(bf16[5,192,128]{2,1,0:T(8,128)(2,1)S(1)} %get-tuple-element.43), channel_id=1, source_target_pairs={{0,16},{8,24},{16,0},{24,8},{1,17},{9,25},{17,1},{25,9},{2,18},{10... | collective-permute-start | bytes 737288 | tf_op jit(solution)/shard_map/ppermute | solution.py:395
  37.8 1.4 %collective-permute-start.4 = (bf16[5,192,128]{2,1,0:T(8,128)(2,1)S(1)}, bf16[5,192,128]{2,1,0:T(8,128)(2,1)S(1)}, u32[]{:S(2)}, u32[]{:S(2)}) collective-permute-start(bf16[5,192,128]{2,1,0:T(8,128)(2,1)S(1)} %get-tuple-element.44), channel_id=1, source_target_pairs={{0,24},{8,0},{16,8},{24,16},{1,25},{9,1},{17,9},{25,17},{2,26},{10... | collective-permute-start | bytes 737288 | tf_op jit(solution)/shard_map/ppermute | solution.py:395
  39.1 4.6 %all-to-all-start.1 = ((f32[32,4,128]{2,1,0:T(4,128)}), f32[32,4,128]{2,1,0:T(4,128)S(1)}, u32[]{:S(2)}, u32[]{:S(2)}) async-start(f32[32,4,128]{2,1,0:T(4,128)} %get-tuple-element.36), calls=%async_computation.1 | async-start | bytes 131072 | tf_op jit(solution)/shard_map/all_to_all | solution.py:489
  43.7 0.5 forward_out.1
  44.3 1.9 %collective-permute-start.5 = (bf16[2,192,128]{2,1,0:T(8,128)(2,1)S(1)}, bf16[2,192,128]{2,1,0:T(8,128)(2,1)S(1)}, u32[]{:S(2)}, u32[]{:S(2)}) collective-permute-start(bf16[2,192,128]{2,1,0:T(8,128)(2,1)S(1)} %get-tuple-element.47), channel_id=1, source_target_pairs={{0,1},{1,2},{2,3},{3,4},{4,5},{5,6},{6,7},{7,8},{8,9},{9,10},{10,1... | collective-permute-start | bytes 294920 | tf_op jit(solution)/shard_map/ppermute | solution.py:395
  46.1 3.6 %collective-permute-start.6 = (bf16[2,192,128]{2,1,0:T(8,128)(2,1)S(1)}, bf16[2,192,128]{2,1,0:T(8,128)(2,1)S(1)}, u32[]{:S(2)}, u32[]{:S(2)}) collective-permute-start(bf16[2,192,128]{2,1,0:T(8,128)(2,1)S(1)} %get-tuple-element.48), channel_id=1, source_target_pairs={{0,31},{1,0},{2,1},{3,2},{4,3},{5,4},{6,5},{7,6},{8,7},{9,8},{10,9... | collective-permute-start | bytes 294920 | tf_op jit(solution)/shard_map/ppermute | solution.py:395
  49.7 4.1 %all-to-all-done.1.recv_ref = f32[32,4,128]{2,1,0:T(4,128)S(1)} async-done(((f32[32,4,128]{2,1,0:T(4,128)}), f32[32,4,128]{2,1,0:T(4,128)S(1)}, u32[]{:S(2)}, u32[]{:S(2)}) %all-to-all-start.1) | async-done | bytes 65568 | tf_op jit(solution)/shard_map/all_to_all | solution.py:489
  53.8 0.0 collective-permute-done.2.a_ref
  53.8 0.0 collective-permute-done.3.b_ref
  53.8 0.0 collective-permute-done.4.c_ref
  53.8 2.2 %kernel_grads.1 = (bf16[8,248,128]{2,1,0:T(8,128)(2,1)}, f32[1,192]{1,0:T(1,128)}, f32[1,192]{1,0:T(1,128)}) custom-call(f32[32,4,128]{2,1,0:T(4,128)S(1)} %all-to-all-done.1.recv_ref, bf16[5,192,128]{2,1,0:T(8,128)(2,1)S(1)} %get-tuple-element.37.share_ref.own_ref, bf16[5,192,128]{2,1,0:T(8,128)(2,1)S(1)} %collective-permute-done.2.a_ref, ...), custom_call_target="tpu_custom_call" | custom-call | bytes 1000 | tf_op jit(solution)/shard_map/kernel_grads/pallas_call | solution.py:34
  56.0 0.0 collective-permute-done.5.low_ref
  56.0 0.0 collective-permute-done.6.high_ref
  56.0 3.5 %all-to-all-start.2 = ((bf16[8,248,128]{2,1,0:T(8,128)(2,1)}), bf16[8,248,128]{2,1,0:T(8,128)(2,1)S(1)}, u32[]{:S(2)}, u32[]{:S(2)}) async-start(bf16[8,248,128]{2,1,0:T(8,128)(2,1)} %get-tuple-element.59), calls=%async_computation.2 | async-start | bytes 1015808 | tf_op jit(solution)/shard_map/all_to_all | solution.py:525
  59.5 3.5 %input_grads.1 = (bf16[384,128]{1,0:T(8,128)(2,1)S(1)}, bf16[384,128]{1,0:T(8,128)(2,1)S(1)}) custom-call(s32[5]{0:T(128)S(1)} %stack.39.flag_ref, bf16[192,5184]{1,0:T(8,128)(2,1)} %bitcast.33, f32[32,4,128]{2,1,0:T(4,128)S(1)} %all-to-all-done.1.recv_ref, bf16[5,192,128]{2,1,0:T(8,128)(2,1)S(1)} %get-tuple-element.37.share_ref.own_ref, ...), custom_call_target="tpu_custom_call" | custom-call | flops 509607936 | bytes 4000000 | tf_op jit(solution)/shard_map/input_grads/pallas_call | solution.py:34
  63.0 0.0 collective-permute-start.7
  63.0 1.7 %collective-permute-start.8 = (bf16[384,128]{1,0:T(8,128)(2,1)S(1)}, bf16[384,128]{1,0:T(8,128)(2,1)S(1)}, u32[]{:S(2)}, u32[]{:S(2)}) collective-permute-start(bf16[384,128]{1,0:T(8,128)(2,1)S(1)} %get-tuple-element.54), channel_id=1, source_target_pairs={{0,224},{32,0},{64,32},{96,64},{128,96},{160,128},{192,160},{224,1... | collective-permute-start | bytes 294920 | tf_op jit(solution)/shard_map/ppermute | solution.py:395
  64.8 0.0 collective-permute-start.9
  64.8 2.3 %collective-permute-done.7.one_ref = bf16[384,128]{1,0:T(8,128)(2,1)S(1)} collective-permute-done((bf16[384,128]{1,0:T(8,128)(2,1)S(1)}, bf16[384,128]{1,0:T(8,128)(2,1)S(1)}, u32[]{:S(2)}, u32[]{:S(2)}) %collective-permute-start.7) | collective-permute-done | bytes 98336 | tf_op jit(solution)/shard_map/ppermute | solution.py:395
  67.1 0.0 collective-permute-done.8.two_ref
  67.1 4.0 %collective-permute-done.9.three_ref = bf16[384,128]{1,0:T(8,128)(2,1)S(1)} collective-permute-done((bf16[384,128]{1,0:T(8,128)(2,1)S(1)}, bf16[384,128]{1,0:T(8,128)(2,1)S(1)}, u32[]{:S(2)}, u32[]{:S(2)}) %collective-permute-start.9) | collective-permute-done | bytes 98336 | tf_op jit(solution)/shard_map/ppermute | solution.py:548
  71.1 0.7 hand_over.1
  71.8 1.5 %all-to-all-done.2.recv_ref = bf16[8,248,128]{2,1,0:T(8,128)(2,1)S(1)} async-done(((bf16[8,248,128]{2,1,0:T(8,128)(2,1)}), bf16[8,248,128]{2,1,0:T(8,128)(2,1)S(1)}, u32[]{:S(2)}, u32[]{:S(2)}) %all-to-all-start.2) | async-done | bytes 507936 | tf_op jit(solution)/shard_map/all_to_all | solution.py:525
  73.2 0.8 %kernel.1 = f32[6,1,5184]{2,1,0:T(1,128)} custom-call(bf16[8,248,128]{2,1,0:T(8,128)(2,1)S(1)} %all-to-all-done.2.recv_ref), custom_call_target="tpu_custom_call" | custom-call | bytes 1000000 | tf_op jit(solution)/shard_map/kernel/pallas_call | solution.py:34
  (3 shorter events, 0.1 us)
Async XLA Ops:
  1.8 11.4 %collective-permute-start = (bf16[384,128]{1,0:T(8,128)(2,1)S(1)}, bf16[384,128]{1,0:T(8,128)(2,1)S(1)}, u32[]{:S(2)}, u32[]{:S(2)}) collective-permute-start(bf16[384,128]{1,0:T(8,128)(2,1)S(1)} %get-tuple-element.63), channel_id=1, source_target_pairs={{0,1},{1,2},{2,3},{3,4},{4,5},{5,6},{6,7},{7,8},{8,9},{9,10},{10,1... | collective-permute-start | bytes 294920 | tf_op jit(solution)/shard_map/ppermute | solution.py:395
  3.8 9.4 %collective-permute-start.1 = (bf16[384,128]{1,0:T(8,128)(2,1)S(1)}, bf16[384,128]{1,0:T(8,128)(2,1)S(1)}, u32[]{:S(2)}, u32[]{:S(2)}) collective-permute-start(bf16[384,128]{1,0:T(8,128)(2,1)S(1)} %get-tuple-element.62), channel_id=1, source_target_pairs={{0,31},{1,0},{2,1},{3,2},{4,3},{5,4},{6,5},{7,6},{8,7},{9,8},{10,9... | collective-permute-start | bytes 294920 | tf_op jit(solution)/shard_map/ppermute | solution.py:395
  10.3 2.5 %copy-start = (bf16[192,105]{1,0:T(8,128)(2,1)S(1)}, bf16[192,105]{1,0:T(8,128)(2,1)}, u32[]{:S(2)}) copy-start(bf16[192,105]{1,0:T(8,128)(2,1)} %head_ref.1) | copy-start | bytes 120964
  10.3 2.7 %slice-start = ((f32[1,192]{1,0:T(1,128)}), f32[1,64]{1,0:T(1,128)S(1)}, s32[]{:S(2)}) async-start(f32[1,192]{1,0:T(1,128)} %param.19), calls=%async_computation.3 | async-start | bytes 1024 | tf_op jit(solution)/shard_map/slice | solution.py:388
  10.3 2.7 %slice-start.1 = ((f32[1,192]{1,0:T(1,128)}), f32[1,128]{1,0:T(1,128)S(1)}, s32[]{:S(2)}) async-start(f32[1,192]{1,0:T(1,128)} %param.19), calls=%async_computation.4 | async-start | bytes 1024 | tf_op jit(solution)/shard_map/slice | solution.py:389
  10.3 2.7 %slice-start.2 = ((f32[1,192]{1,0:T(1,128)}), f32[1,64]{1,0:T(1,128)S(1)}, s32[]{:S(2)}) async-start(f32[1,192]{1,0:T(1,128)} %param.18), calls=%async_computation.5 | async-start | bytes 1024 | tf_op jit(solution)/shard_map/slice | solution.py:388
  10.3 2.7 %slice-start.3 = ((f32[1,192]{1,0:T(1,128)}), f32[1,128]{1,0:T(1,128)S(1)}, s32[]{:S(2)}) async-start(f32[1,192]{1,0:T(1,128)} %param.18), calls=%async_computation.6 | async-start | bytes 1024 | tf_op jit(solution)/shard_map/slice | solution.py:389
  13.2 9.5 %copy-start.2 = (bf16[1,192,2,128]{3,2,1,0:T(2,128)(2,1)S(1)}, bf16[1,192,2,128]{3,2,1,0:T(2,128)(2,1)}, u32[]{:S(2)}) copy-start(bf16[1,192,2,128]{3,2,1,0:T(2,128)(2,1)} %param.16) | copy-start | bytes 294916
  13.2 9.5 %copy-start.3 = (bf16[1,192,2,128]{3,2,1,0:T(2,128)(2,1)S(1)}, bf16[1,192,2,128]{3,2,1,0:T(2,128)(2,1)}, u32[]{:S(2)}) copy-start(bf16[1,192,2,128]{3,2,1,0:T(2,128)(2,1)} %param.15) | copy-start | bytes 294916
  13.2 19.8 %copy-start.1 = (s32[2,128]{1,0:T(2,128)S(1)}, s32[2,128]{1,0:T(2,128)}, u32[]{:S(2)}) copy-start(s32[2,128]{1,0:T(2,128)} %label_ref.1) | copy-start | bytes 3076
  15.9 17.1 %all-to-all-start = ((f32[32,6,128]{2,1,0:T(8,128)}), f32[32,6,128]{2,1,0:T(8,128)S(1)}, u32[]{:S(2)}, u32[]{:S(2)}) async-start(f32[32,6,128]{2,1,0:T(8,128)} %get-tuple-element.35), calls=%async_computation | async-start | bytes 262144 | tf_op jit(solution)/shard_map/all_to_all | solution.py:461
  35.1 18.7 %collective-permute-start.2 = (bf16[5,192,128]{2,1,0:T(8,128)(2,1)}, bf16[5,192,128]{2,1,0:T(8,128)(2,1)S(1)}, u32[]{:S(2)}, u32[]{:S(2)}) collective-permute-start(bf16[5,192,128]{2,1,0:T(8,128)(2,1)} %get-tuple-element.42), channel_id=1, source_target_pairs={{0,8},{8,16},{16,24},{24,0},{1,9},{9,17},{17,25},{25,1},{2,10},{10... | collective-permute-start | bytes 737288 | tf_op jit(solution)/shard_map/ppermute | solution.py:395
  35.8 18.1 %collective-permute-start.3 = (bf16[5,192,128]{2,1,0:T(8,128)(2,1)S(1)}, bf16[5,192,128]{2,1,0:T(8,128)(2,1)S(1)}, u32[]{:S(2)}, u32[]{:S(2)}) collective-permute-start(bf16[5,192,128]{2,1,0:T(8,128)(2,1)S(1)} %get-tuple-element.43), channel_id=1, source_target_pairs={{0,16},{8,24},{16,0},{24,8},{1,17},{9,25},{17,1},{25,9},{2,18},{10... | collective-permute-start | bytes 737288 | tf_op jit(solution)/shard_map/ppermute | solution.py:395
  37.8 16.1 %collective-permute-start.4 = (bf16[5,192,128]{2,1,0:T(8,128)(2,1)S(1)}, bf16[5,192,128]{2,1,0:T(8,128)(2,1)S(1)}, u32[]{:S(2)}, u32[]{:S(2)}) collective-permute-start(bf16[5,192,128]{2,1,0:T(8,128)(2,1)S(1)} %get-tuple-element.44), channel_id=1, source_target_pairs={{0,24},{8,0},{16,8},{24,16},{1,25},{9,1},{17,9},{25,17},{2,26},{10... | collective-permute-start | bytes 737288 | tf_op jit(solution)/shard_map/ppermute | solution.py:395
  39.1 14.7 %all-to-all-start.1 = ((f32[32,4,128]{2,1,0:T(4,128)}), f32[32,4,128]{2,1,0:T(4,128)S(1)}, u32[]{:S(2)}, u32[]{:S(2)}) async-start(f32[32,4,128]{2,1,0:T(4,128)} %get-tuple-element.36), calls=%async_computation.1 | async-start | bytes 131072 | tf_op jit(solution)/shard_map/all_to_all | solution.py:489
  44.3 11.8 %collective-permute-start.5 = (bf16[2,192,128]{2,1,0:T(8,128)(2,1)S(1)}, bf16[2,192,128]{2,1,0:T(8,128)(2,1)S(1)}, u32[]{:S(2)}, u32[]{:S(2)}) collective-permute-start(bf16[2,192,128]{2,1,0:T(8,128)(2,1)S(1)} %get-tuple-element.47), channel_id=1, source_target_pairs={{0,1},{1,2},{2,3},{3,4},{4,5},{5,6},{6,7},{7,8},{8,9},{9,10},{10,1... | collective-permute-start | bytes 294920 | tf_op jit(solution)/shard_map/ppermute | solution.py:395
  46.1 9.9 %collective-permute-start.6 = (bf16[2,192,128]{2,1,0:T(8,128)(2,1)S(1)}, bf16[2,192,128]{2,1,0:T(8,128)(2,1)S(1)}, u32[]{:S(2)}, u32[]{:S(2)}) collective-permute-start(bf16[2,192,128]{2,1,0:T(8,128)(2,1)S(1)} %get-tuple-element.48), channel_id=1, source_target_pairs={{0,31},{1,0},{2,1},{3,2},{4,3},{5,4},{6,5},{7,6},{8,7},{9,8},{10,9... | collective-permute-start | bytes 294920 | tf_op jit(solution)/shard_map/ppermute | solution.py:395
  56.0 17.2 %all-to-all-start.2 = ((bf16[8,248,128]{2,1,0:T(8,128)(2,1)}), bf16[8,248,128]{2,1,0:T(8,128)(2,1)S(1)}, u32[]{:S(2)}, u32[]{:S(2)}) async-start(bf16[8,248,128]{2,1,0:T(8,128)(2,1)} %get-tuple-element.59), calls=%async_computation.2 | async-start | bytes 1015808 | tf_op jit(solution)/shard_map/all_to_all | solution.py:525
  63.0 4.1 %collective-permute-start.7 = (bf16[384,128]{1,0:T(8,128)(2,1)S(1)}, bf16[384,128]{1,0:T(8,128)(2,1)S(1)}, u32[]{:S(2)}, u32[]{:S(2)}) collective-permute-start(bf16[384,128]{1,0:T(8,128)(2,1)S(1)} %get-tuple-element.53.fwd_out_ref), channel_id=1, source_target_pairs={{0,32},{32,64},{64,96},{96,128},{128,160},{160,192},{192,224},{224... | collective-permute-start | bytes 294920 | tf_op jit(solution)/shard_map/ppermute | solution.py:395
  63.0 4.0 %collective-permute-start.8 = (bf16[384,128]{1,0:T(8,128)(2,1)S(1)}, bf16[384,128]{1,0:T(8,128)(2,1)S(1)}, u32[]{:S(2)}, u32[]{:S(2)}) collective-permute-start(bf16[384,128]{1,0:T(8,128)(2,1)S(1)} %get-tuple-element.54), channel_id=1, source_target_pairs={{0,224},{32,0},{64,32},{96,64},{128,96},{160,128},{192,160},{224,1... | collective-permute-start | bytes 294920 | tf_op jit(solution)/shard_map/ppermute | solution.py:395
  64.8 6.3 %collective-permute-start.9 = (bf16[384,128]{1,0:T(8,128)(2,1)S(1)}, bf16[384,128]{1,0:T(8,128)(2,1)S(1)}, u32[]{:S(2)}, u32[]{:S(2)}) collective-permute-start(bf16[384,128]{1,0:T(8,128)(2,1)S(1)} %get-tuple-element.55), channel_id=1, source_target_pairs={{0,224},{32,192},{64,160},{96,128},{128,96},{160,64},{192,32},{224... | collective-permute-start | bytes 294920 | tf_op jit(solution)/shard_map/ppermute | solution.py:548

commit v7 on v6

--- a/solution.py
+++ b/solution.py
@@ -142,20 +142,30 @@
                         ] = view
 
 
-def conv_both(own_ref, low_ref, high_ref, wt_ref, z_ref, send_ref, x_ref):
-    masks = tap_masks()
-    for which in range(2):
-        rows = slice(192 * which, 192 * which + 192)
-        planes = [low_ref[rows], own_ref[0, rows], own_ref[1, rows], high_ref[rows]]
-        fill_taps(planes, 2, x_ref, masks, 192, 2 * which)
+def convolution(which, own_ref, low_ref, high_ref, wt_ref, z_ref, x_ref):
+    rows = slice(192 * which, 192 * which + 192)
+    planes = [low_ref[...], own_ref[0, rows], own_ref[1, rows], high_ref[...]]
+    fill_taps(planes, 2, x_ref, tap_masks(), 192, 0)
     z = jnp.dot(wt_ref[...], x_ref[...], preferred_element_type=F32)
-    outs = [z[:, j * AREA : (j + 1) * AREA] for j in range(4)]
-    for j in range(4):
-        z_ref[j] = outs[j]
-    tile = packed_tile(
-        local_stats(outs[:2], 2.0 * AREA) + local_stats(outs[2:], 2.0 * AREA)
-    )
+    outs = [z[:, :AREA], z[:, AREA:]]
+    z_ref[0] = outs[0]
+    z_ref[1] = outs[1]
+    return local_stats(outs, 2.0 * AREA)
+
+
+def conv_bwd(own_ref, low_ref, high_ref, wt_ref, z_ref, send_ref, x_ref):
+    tile = packed_tile(convolution(0, own_ref, low_ref, high_ref, wt_ref, z_ref, x_ref))
     send_ref[...] = jnp.broadcast_to(tile[None, : send_ref.shape[1]], send_ref.shape)
+
+
+def conv_fwd(own_ref, low_ref, high_ref, wt_ref, z_ref, tile_ref, x_ref):
+    mean, squares = convolution(1, own_ref, low_ref, high_ref, wt_ref, z_ref, x_ref)
+    tile_ref[...] = packed_tile([jnp.zeros_like(mean), jnp.zeros_like(mean), mean, squares])
+
+
+def rims(share_ref, rim_low_ref, rim_high_ref):
+    rim_high_ref[...] = share_ref[:2]
+    rim_low_ref[...] = share_ref[2:4]
 
 
 def head_and_sums(
@@ -171,6 +181,7 @@
     affine_ref,
     head_ref,
     head_turned_ref,
+    fwd_tile_ref,
     up_ref,
     share_ref,
     share_a_ref,
@@ -226,22 +237,18 @@
                 ref[2 * j + k] = part
         sum_grad = sum_grad + jnp.sum(grad_act, axis=1, keepdims=True)
         sum_cross = sum_cross + jnp.sum(grad_act * normed, axis=1, keepdims=True)
-    tile = packed_tile([sum_grad, sum_cross])
+    tile = packed_tile([sum_grad, sum_cross]) + fwd_tile_ref[...]
     send_ref[...] = jnp.broadcast_to(tile[None, : send_ref.shape[1]], send_ref.shape)
 
 
-def forward_out(
-    recv_ref, z_ref, own_ref, affine_ref, share_ref, out_ref, rim_low_ref, rim_high_ref, mix_ref
-):
-    rim_high_ref[...] = share_ref[:2]
-    rim_low_ref[...] = share_ref[2:4]
+def forward_out(recv_ref, z_ref, own_ref, affine_ref, out_ref, mix_ref):
     peers = recv_ref.shape[0]
     cells = 2.0 * AREA
     mean, squares = spread_sums(recv_ref[...], 1, cells, peers)
     inv_std = lax.rsqrt(squares / (cells * peers) + epsilon)
     gain, shift = columns(affine_ref[...], 0)
     for j in range(2):
-        scaled = (z_ref[2 + j] - mean) * inv_std * gain + shift
+        scaled = (z_ref[j] - mean) * inv_std * gain + shift
         activated = jnp.where(scaled > 0, scaled, leak_slope * scaled)
         mix_ref[pl.ds(j, 192, stride=2), :] = own_ref[j, 192:].astype(F32) + activated
     out_ref[...] = mix_ref[...].astype(BF16)
@@ -434,9 +441,12 @@
         return by_plane(jnp.where(is_decoder, added, block))
 
     own = jnp.concatenate([joined(bwd_input, bwd_skip), joined(fwd_input, fwd_skip)], axis=1)
-    nothing = jnp.zeros_like(own[0])
-    low = moved(jnp.where(slab_id < slabs - 1, own[1], nothing), SLABS, 1)
-    high = moved(jnp.where(slab_id > 0, own[0], nothing), SLABS, -1)
+    nothing = jnp.zeros((192, AREA), BF16)
+    upper, lower = slab_id < slabs - 1, slab_id > 0
+    low = moved(jnp.where(upper, own[1, :192], nothing), SLABS, 1)
+    high = moved(jnp.where(lower, own[0, :192], nothing), SLABS, -1)
+    fwd_low = moved(jnp.where(upper, own[1, 192:], nothing), SLABS, 1)
+    fwd_high = moved(jnp.where(lower, own[0, 192:], nothing), SLABS, -1)
     (turned,) = call(
         turn_weights,
         [((192, 5184), BF16)],
@@ -448,14 +458,25 @@
         limit=52,
     )
     z, stats_send = call(
-        conv_both,
-        [((4, 192, AREA), F32), ((slabs, 6, AREA), F32)],
-        [((5184, 512), BF16)],
-        2 * 5184 * 192 * 512,
+        conv_bwd,
+        [((2, 192, AREA), F32), ((slabs, 3, AREA), F32)],
+        [((5184, 256), BF16)],
+        2 * 5184 * 192 * 256,
         5000000,
         own,
         low,
         high,
+        turned,
+    )
+    fwd_z, fwd_tile = call(
+        conv_fwd,
+        [((2, 192, AREA), F32), ((8, AREA), F32)],
+        [((5184, 256), BF16)],
+        2 * 5184 * 192 * 256,
+        5000000,
+        own,
+        fwd_low,
+        fwd_high,
         turned,
     )
     stats = lax.all_to_all(stats_send, SLABS, 0, 0, tiled=True)
@@ -467,7 +488,7 @@
             ((2, 192, AREA), F32),
             *[((5, 192, AREA), BF16)] * 4,
             ((192, AREA), F32),
-            ((slabs, 4, AREA), F32),
+            ((slabs, 6, AREA), F32),
         ],
         HEAD_SCRATCH,
         4 * 192 * 105 * 512,
@@ -484,26 +505,26 @@
         affine,
         head_weight,
         head_weight.T,
+        fwd_tile,
         smem=1,
     )
     sums = lax.all_to_all(sums_send, SLABS, 0, 0, tiled=True)
     share = shares[0]
     shares = [share] + [moved(shares[d], "y", d) for d in (1, 2, 3)]
-    fwd_out, rim_low, rim_high = call(
+    rim_low, rim_high = call(rims, [((2, 192, AREA), BF16)] * 2, [], 0, 400000, share)
+    (fwd_out,) = call(
         forward_out,
-        [((384, AREA), BF16), ((2, 192, AREA), BF16), ((2, 192, AREA), BF16)],
+        [((384, AREA), BF16)],
         [((384, AREA), F32)],
         0,
         1000000,
-        stats,
-        z,
+        sums,
+        fwd_z,
         own,
         affine,
-        share,
     )
     rim_low = moved(rim_low, SLABS, 1)
     rim_high = moved(rim_high, SLABS, -1)
-    sums, fwd_out = lax.optimization_barrier((sums, fwd_out))
     parts, shift_grad, gain_grad = call(
         kernel_grads,
         [((8, 248, AREA), BF16), ((1, 192), F32), ((1, 192), F32)],

time: 74.5 us -> 77.7 us (1.043)
  starting transfers between devices: 34.4 us -> 36 us
  local copies, waits for them, and re-layouts: 0.27 us -> 1.21 us
  other arithmetic: 1.23 us -> 2.06 us
    ppermute x9 -> x11, starting transfers between devices: 19.6 us -> 23.5 us  [moved(): return lax.ppermute(block, axis, route)]
    all_to_all x1, starting transfers between devices: 6.7 us -> 4.22 us  [per_device(): stats = lax.all_to_all(stats_send, SLABS, 0, 0, tiled=True)]
    all_to_all x1, waiting for transfers between devices: 10.3 us -> 8.51 us  [per_device(): stats = lax.all_to_all(stats_send, SLABS, 0, 0, tiled=True)]
    all_to_all x1, waiting for transfers between devices: 1.46 us -> 3.13 us  [per_device(): summed = lax.all_to_all(parts, 'z', 0, 0, tiled=True)]
    transpose x1, local copies, waits for them, and re-layouts: 0.03 us -> 0.97 us  [by_plane(): return jnp.swapaxes(block[0], 0, 1)]
    transpose x1 -> x2, other arithmetic: 1.09 us -> 1.94 us  [by_plane(): return jnp.swapaxes(block[0], 0, 1)]
    ppermute x9 -> x11, waiting for transfers between devices: 2.31 us -> 1.57 us  [moved(): return lax.ppermute(block, axis, route)]
    pallas_call x8 -> x10, Pallas kernels: 15.1 us -> 15.5 us  [call(): pl.pallas_call(body, out_shape=shapes, in_specs=specs, out_specs=[VMEM] *...]
  transfers between devices with their start and end apart: 13 -> 15, of which waited for: 5 -> 5; matrix products, arithmetic and copies ran while one was open for 0% -> 3% of each run, Pallas kernels for 13% -> 16%
where the time goes in v7:
time: 77.7 us; the launch traced here: 77.2 us
  starting transfers between devices  36 us (46%)
  waiting for transfers between devices  21.6 us (28%)
  Pallas kernels  15.5 us (20%)
  other arithmetic  2.06 us (3%)
  local copies, waits for them, and re-layouts  1.21 us (2%)
  between operations  0.87 us (1%)
    ppermute x11, starting transfers between devices, moved(): return lax.ppermute(block, axis, route)  23.5 us
    pallas_call x10, Pallas kernels, call(): pl.pallas_call(body, out_shape=shapes, in_specs=specs, out_specs=[VMEM] *...  15.5 us
    all_to_all x1, waiting for transfers between devices, per_device(): stats = lax.all_to_all(stats_send, SLABS, 0, 0, tiled=True)  8.51 us
    all_to_all x1, waiting for transfers between devices, per_device(): sums = lax.all_to_all(sums_send, SLABS, 0, 0, tiled=True)  4.75 us
    all_to_all x1, starting transfers between devices, per_device(): sums = lax.all_to_all(sums_send, SLABS, 0, 0, tiled=True)  4.26 us
    all_to_all x1, starting transfers between devices, per_device(): stats = lax.all_to_all(stats_send, SLABS, 0, 0, tiled=True)  4.22 us
    ppermute x1, waiting for transfers between devices, per_device(): lax.ppermute(outgoing, 'segment', [(i, segments - 1 - i) for i in range(s...  3.63 us
    all_to_all x1, starting transfers between devices, per_device(): summed = lax.all_to_all(parts, 'z', 0, 0, tiled=True)  3.49 us
  transfers between devices with their start and end apart: 15, of which 5 were waited for; matrix products, arithmetic and copies ran while one was open for 3% of the time, Pallas kernels for 16%

profile of v7, /device:TPU:6, one launch (start us, length us, event | category | flops | bytes accessed | tf_op | source)
XLA Modules:
  0.0 77.2 jit_solution(10393494268623241557)
XLA Ops:
  0.6 1.0 %fusion.3 = bf16[2,192,128]{2,1,0:T(8,128)(2,1)S(1)} fusion(bf16[1,192,2,128]{3,2,1,0:T(2,128)(2,1)} %param.14, bf16[1,192,2,128]{3,2,1,0:T(2,128)(2,1)} %param.13, pred[]{:T(512)S(6)} %ge.3), kind=kLoop, calls=%fused_computation.6 | loop fusion | flops 245760 | bytes 294913 | tf_op jit(solution)/shard_map/transpose | solution.py:437
  1.6 2.0 %collective-permute-start = (bf16[192,128]{1,0:T(8,128)(2,1)S(1)}, bf16[192,128]{1,0:T(8,128)(2,1)S(1)}, u32[]{:S(2)}, u32[]{:S(2)}) collective-permute-start(bf16[192,128]{1,0:T(8,128)(2,1)S(1)} %get-tuple-element.63), channel_id=1, source_target_pairs={{0,1},{1,2},{2,3},{3,4},{4,5},{5,6},{6,7},{7,8},{8,9},{9,10},{10,1... | collective-permute-start | bytes 147464 | tf_op jit(solution)/shard_map/ppermute | solution.py:402
  3.6 6.5 %collective-permute-start.1 = (bf16[192,128]{1,0:T(8,128)(2,1)S(1)}, bf16[192,128]{1,0:T(8,128)(2,1)S(1)}, u32[]{:S(2)}, u32[]{:S(2)}) collective-permute-start(bf16[192,128]{1,0:T(8,128)(2,1)S(1)} %get-tuple-element.62), channel_id=1, source_target_pairs={{0,31},{1,0},{2,1},{3,2},{4,3},{5,4},{6,5},{7,6},{8,7},{9,8},{10,9... | collective-permute-start | bytes 147464 | tf_op jit(solution)/shard_map/ppermute | solution.py:402
  10.1 1.0 %fusion.2 = bf16[2,192,128]{2,1,0:T(8,128)(2,1)S(1)} fusion(bf16[1,192,2,128]{3,2,1,0:T(2,128)(2,1)} %param.12, bf16[1,192,2,128]{3,2,1,0:T(2,128)(2,1)} %param.11, pred[]{:T(512)S(6)} %ge.3), kind=kLoop, calls=%fused_computation.5 | loop fusion | flops 245760 | bytes 294913 | tf_op jit(solution)/shard_map/transpose | solution.py:437
  11.1 0.1 collective-permute-start.2
  11.2 5.3 %collective-permute-start.3 = (bf16[192,128]{1,0:T(8,128)(2,1)S(1)}, bf16[192,128]{1,0:T(8,128)(2,1)S(1)}, u32[]{:S(2)}, u32[]{:S(2)}) collective-permute-start(bf16[192,128]{1,0:T(8,128)(2,1)S(1)} %get-tuple-element.60), channel_id=1, source_target_pairs={{0,31},{1,0},{2,1},{3,2},{4,3},{5,4},{6,5},{7,6},{8,7},{9,8},{10,9... | collective-permute-start | bytes 147464 | tf_op jit(solution)/shard_map/ppermute | solution.py:402
  16.5 1.0 %copy_bitcast_fusion = (bf16[2,192,128]{2,1,0:T(8,128)(2,1)S(1)}, bf16[2,192,128]{2,1,0:T(8,128)(2,1)S(1)}) fusion(bf16[1,192,2,128]{3,2,1,0:T(2,128)(2,1)} %param.16, bf16[1,192,2,128]{3,2,1,0:T(2,128)(2,1)} %param.15), kind=kLoop, calls=%fused_computation.7 | loop fusion | bytes 393216 | tf_op jit(solution)/shard_map/transpose | solution.py:437
  17.5 2.4 %turn_weights.1.wt_ref = bf16[192,5184]{1,0:T(8,128)(2,1)S(1)} custom-call(bf16[192,5184]{1,0:T(8,128)(2,1)} %bitcast.36), custom_call_target="tpu_custom_call" | custom-call | bytes 3981312 | tf_op jit(solution)/shard_map/turn_weights/pallas_call | solution.py:34
  20.0 0.0 slice-start
  20.0 0.0 slice-start.1
  20.0 0.0 slice-start.2
  20.0 0.0 slice-start.3
  20.0 0.0 copy-start
  20.0 0.0 copy-start.1
  20.1 0.0 collective-permute-done.low_ref
  20.1 0.0 collective-permute-done.1.high_ref
  20.1 1.9 %conv_bwd.1 = (f32[2,192,128]{2,1,0:T(8,128)S(1)}, f32[32,3,128]{2,1,0:T(4,128)}) custom-call(bf16[2,384,128]{2,1,0:T(8,128)(2,1)S(1)} %pad_maximum_fusion.own_ref, bf16[192,128]{1,0:T(8,128)(2,1)S(1)} %collective-permute-done.low_ref, bf16[192,128]{1,0:T(8,128)(2,1)S(1)} %collective-permute-done.1.high_ref, bf16[192,5184]{1,0:T(8,128)(2,1)S(1)} %turn_weights.1.wt_ref), custom_call_target="tpu_custom_call" | custom-call | flops 509607936 | bytes 5000000 | tf_op jit(solution)/shard_map/conv_bwd/pallas_call | solution.py:34
  22.0 4.2 %all-to-all-start = ((f32[32,3,128]{2,1,0:T(4,128)}), f32[32,3,128]{2,1,0:T(4,128)S(1)}, u32[]{:S(2)}, u32[]{:S(2)}) async-start(f32[32,3,128]{2,1,0:T(4,128)} %get-tuple-element.34), calls=%async_computation | async-start | bytes 131072 | tf_op jit(solution)/shard_map/all_to_all | solution.py:482
  26.2 0.0 slice-done
  26.2 0.0 slice-done.1
  26.2 0.0 slice-done.2
  26.2 0.0 slice-done.3
  26.2 0.1 maximum_maximum_fusion.affine_ref
  26.3 0.0 copy-done
  26.3 0.1 copy.25
  26.4 0.1 stack.39.flag_ref
  26.5 0.0 collective-permute-done.2.low_ref
  26.5 0.0 collective-permute-done.3.high_ref
  26.5 1.2 %conv_fwd.1 = (f32[2,192,128]{2,1,0:T(8,128)S(1)}, f32[8,128]{1,0:T(8,128)S(1)}) custom-call(bf16[2,384,128]{2,1,0:T(8,128)(2,1)S(1)} %pad_maximum_fusion.own_ref, bf16[192,128]{1,0:T(8,128)(2,1)S(1)} %collective-permute-done.2.low_ref, bf16[192,128]{1,0:T(8,128)(2,1)S(1)} %collective-permute-done.3.high_ref, bf16[192,5184]{1,0:T(8,128)(2,1)S(1)} %turn_weights.1.wt_ref), custom_call_target="tpu_custom_call" | custom-call | flops 509607936 | bytes 5000000 | tf_op jit(solution)/shard_map/conv_fwd/pallas_call | solution.py:34
  27.7 8.5 %all-to-all-done.recv_ref = f32[32,3,128]{2,1,0:T(4,128)S(1)} async-done(((f32[32,3,128]{2,1,0:T(4,128)}), f32[32,3,128]{2,1,0:T(4,128)S(1)}, u32[]{:S(2)}, u32[]{:S(2)}) %all-to-all-start) | async-done | bytes 49184 | tf_op jit(solution)/shard_map/all_to_all | solution.py:482
  36.3 0.0 copy-done.1
  36.3 2.2 %head_and_sums.1 = (f32[2,192,128]{2,1,0:T(8,128)S(1)}, bf16[5,192,128]{2,1,0:T(8,128)(2,1)S(1)}, bf16[5,192,128]{2,1,0:T(8,128)(2,1)S(1)}, bf16[5,192,128]{2,1,...) custom-call(s32[5]{0:T(128)S(1)} %stack.39.flag_ref, ...), custom_call_target="tpu_custom_call" | custom-call | flops 41287680 | bytes 4000000 | tf_op jit(solution)/shard_map/head_and_sums/pallas_call | solution.py:34
  38.4 0.6 collective-permute-start.4
  39.1 2.0 %collective-permute-start.5 = (bf16[5,192,128]{2,1,0:T(8,128)(2,1)S(1)}, bf16[5,192,128]{2,1,0:T(8,128)(2,1)S(1)}, u32[]{:S(2)}, u32[]{:S(2)}) collective-permute-start(bf16[5,192,128]{2,1,0:T(8,128)(2,1)S(1)} %get-tuple-element.41), channel_id=1, source_target_pairs={{0,16},{8,24},{16,0},{24,8},{1,17},{9,25},{17,1},{25,9},{2,18},{10... | collective-permute-start | bytes 737288 | tf_op jit(solution)/shard_map/ppermute | solution.py:402
  41.0 1.3 %collective-permute-start.6 = (bf16[5,192,128]{2,1,0:T(8,128)(2,1)S(1)}, bf16[5,192,128]{2,1,0:T(8,128)(2,1)S(1)}, u32[]{:S(2)}, u32[]{:S(2)}) collective-permute-start(bf16[5,192,128]{2,1,0:T(8,128)(2,1)S(1)} %get-tuple-element.42), channel_id=1, source_target_pairs={{0,24},{8,0},{16,8},{24,16},{1,25},{9,1},{17,9},{25,17},{2,26},{10... | collective-permute-start | bytes 737288 | tf_op jit(solution)/shard_map/ppermute | solution.py:402
  42.4 4.3 %all-to-all-start.1 = ((f32[32,6,128]{2,1,0:T(8,128)}), f32[32,6,128]{2,1,0:T(8,128)S(1)}, u32[]{:S(2)}, u32[]{:S(2)}) async-start(f32[32,6,128]{2,1,0:T(8,128)} %get-tuple-element.36), calls=%async_computation.1 | async-start | bytes 262144 | tf_op jit(solution)/shard_map/all_to_all | solution.py:511
  46.6 1.9 %collective-permute-start.7 = (bf16[2,192,128]{2,1,0:T(8,128)(2,1)S(1)}, bf16[2,192,128]{2,1,0:T(8,128)(2,1)S(1)}, u32[]{:S(2)}, u32[]{:S(2)}) collective-permute-start(bf16[2,192,128]{2,1,0:T(8,128)(2,1)S(1)} %get-tuple-element.45), channel_id=1, source_target_pairs={{0,1},{1,2},{2,3},{3,4},{4,5},{5,6},{6,7},{7,8},{8,9},{9,10},{10,1... | collective-permute-start | bytes 294920 | tf_op jit(solution)/shard_map/ppermute | solution.py:402
  48.5 3.7 %collective-permute-start.8 = (bf16[2,192,128]{2,1,0:T(8,128)(2,1)S(1)}, bf16[2,192,128]{2,1,0:T(8,128)(2,1)S(1)}, u32[]{:S(2)}, u32[]{:S(2)}) collective-permute-start(bf16[2,192,128]{2,1,0:T(8,128)(2,1)S(1)} %get-tuple-element.46), channel_id=1, source_target_pairs={{0,31},{1,0},{2,1},{3,2},{4,3},{5,4},{6,5},{7,6},{8,7},{9,8},{10,9... | collective-permute-start | bytes 294920 | tf_op jit(solution)/shard_map/ppermute | solution.py:402
  52.2 4.7 %all-to-all-done.1.recv_ref = f32[32,6,128]{2,1,0:T(8,128)S(1)} async-done(((f32[32,6,128]{2,1,0:T(8,128)}), f32[32,6,128]{2,1,0:T(8,128)S(1)}, u32[]{:S(2)}, u32[]{:S(2)}) %all-to-all-start.1) | async-done | bytes 98336 | tf_op jit(solution)/shard_map/all_to_all | solution.py:511
  56.9 0.0 collective-permute-done.4.a_ref
  57.0 0.0 collective-permute-done.5.b_ref
  57.0 0.0 collective-permute-done.6.c_ref
  57.0 2.2 %kernel_grads.1 = (bf16[8,248,128]{2,1,0:T(8,128)(2,1)}, f32[1,192]{1,0:T(1,128)}, f32[1,192]{1,0:T(1,128)}) custom-call(f32[32,6,128]{2,1,0:T(8,128)S(1)} %all-to-all-done.1.recv_ref, bf16[5,192,128]{2,1,0:T(8,128)(2,1)S(1)} %get-tuple-element.38.own_ref.share_ref, bf16[5,192,128]{2,1,0:T(8,128)(2,1)S(1)} %collective-permute-done.4.a_ref, ...), custom_call_target="tpu_custom_call" | custom-call | bytes 1000 | tf_op jit(solution)/shard_map/kernel_grads/pallas_call | solution.py:34
  59.2 0.0 collective-permute-done.7.low_ref
  59.2 0.0 collective-permute-done.8.high_ref
  59.2 3.5 %all-to-all-start.2 = ((bf16[8,248,128]{2,1,0:T(8,128)(2,1)}), bf16[8,248,128]{2,1,0:T(8,128)(2,1)S(1)}, u32[]{:S(2)}, u32[]{:S(2)}) async-start(bf16[8,248,128]{2,1,0:T(8,128)(2,1)} %get-tuple-element.57), calls=%async_computation.2 | async-start | bytes 1015808 | tf_op jit(solution)/shard_map/all_to_all | solution.py:546
  62.7 0.5 forward_out.1.fwd_out_ref
  63.2 3.5 %input_grads.1 = (bf16[384,128]{1,0:T(8,128)(2,1)S(1)}, bf16[384,128]{1,0:T(8,128)(2,1)S(1)}) custom-call(s32[5]{0:T(128)S(1)} %stack.39.flag_ref, bf16[192,5184]{1,0:T(8,128)(2,1)} %bitcast.37, f32[32,6,128]{2,1,0:T(8,128)S(1)} %all-to-all-done.1.recv_ref, bf16[5,192,128]{2,1,0:T(8,128)(2,1)S(1)} %get-tuple-element.38.own_ref.share_ref, ...), custom_call_target="tpu_custom_call" | custom-call | flops 509607936 | bytes 4000000 | tf_op jit(solution)/shard_map/input_grads/pallas_call | solution.py:34
  66.7 0.0 collective-permute-start.10
  66.7 0.6 collective-permute-start.11
  67.3 0.1 collective-permute-start.9
  67.4 1.5 %collective-permute-done.10.two_ref = bf16[384,128]{1,0:T(8,128)(2,1)S(1)} collective-permute-done((bf16[384,128]{1,0:T(8,128)(2,1)S(1)}, bf16[384,128]{1,0:T(8,128)(2,1)S(1)}, u32[]{:S(2)}, u32[]{:S(2)}) %collective-permute-start.10) | collective-permute-done | bytes 98336 | tf_op jit(solution)/shard_map/ppermute | solution.py:402
  68.9 3.6 %collective-permute-done.11.three_ref = bf16[384,128]{1,0:T(8,128)(2,1)S(1)} collective-permute-done((bf16[384,128]{1,0:T(8,128)(2,1)S(1)}, bf16[384,128]{1,0:T(8,128)(2,1)S(1)}, u32[]{:S(2)}, u32[]{:S(2)}) %collective-permute-start.11) | collective-permute-done | bytes 98336 | tf_op jit(solution)/shard_map/ppermute | solution.py:569
  72.5 0.0 collective-permute-done.9.one_ref
  72.5 0.7 hand_over.1
  73.3 3.1 %all-to-all-done.2.recv_ref = bf16[8,248,128]{2,1,0:T(8,128)(2,1)S(1)} async-done(((bf16[8,248,128]{2,1,0:T(8,128)(2,1)}), bf16[8,248,128]{2,1,0:T(8,128)(2,1)S(1)}, u32[]{:S(2)}, u32[]{:S(2)}) %all-to-all-start.2) | async-done | bytes 507936 | tf_op jit(solution)/shard_map/all_to_all | solution.py:546
  76.4 0.8 %kernel.1 = f32[6,1,5184]{2,1,0:T(1,128)} custom-call(bf16[8,248,128]{2,1,0:T(8,128)(2,1)S(1)} %all-to-all-done.2.recv_ref), custom_call_target="tpu_custom_call" | custom-call | bytes 1000000 | tf_op jit(solution)/shard_map/kernel/pallas_call | solution.py:34
  (4 shorter events, 0.1 us)
Async XLA Ops:
  1.6 18.4 %collective-permute-start = (bf16[192,128]{1,0:T(8,128)(2,1)S(1)}, bf16[192,128]{1,0:T(8,128)(2,1)S(1)}, u32[]{:S(2)}, u32[]{:S(2)}) collective-permute-start(bf16[192,128]{1,0:T(8,128)(2,1)S(1)} %get-tuple-element.63), channel_id=1, source_target_pairs={{0,1},{1,2},{2,3},{3,4},{4,5},{5,6},{6,7},{7,8},{8,9},{9,10},{10,1... | collective-permute-start | bytes 147464 | tf_op jit(solution)/shard_map/ppermute | solution.py:402
  3.6 16.4 %collective-permute-start.1 = (bf16[192,128]{1,0:T(8,128)(2,1)S(1)}, bf16[192,128]{1,0:T(8,128)(2,1)S(1)}, u32[]{:S(2)}, u32[]{:S(2)}) collective-permute-start(bf16[192,128]{1,0:T(8,128)(2,1)S(1)} %get-tuple-element.62), channel_id=1, source_target_pairs={{0,31},{1,0},{2,1},{3,2},{4,3},{5,4},{6,5},{7,6},{8,7},{9,8},{10,9... | collective-permute-start | bytes 147464 | tf_op jit(solution)/shard_map/ppermute | solution.py:402
  11.1 15.4 %collective-permute-start.2 = (bf16[192,128]{1,0:T(8,128)(2,1)S(1)}, bf16[192,128]{1,0:T(8,128)(2,1)S(1)}, u32[]{:S(2)}, u32[]{:S(2)}) collective-permute-start(bf16[192,128]{1,0:T(8,128)(2,1)S(1)} %get-tuple-element.61), channel_id=1, source_target_pairs={{0,1},{1,2},{2,3},{3,4},{4,5},{5,6},{6,7},{7,8},{8,9},{9,10},{10,1... | collective-permute-start | bytes 147464 | tf_op jit(solution)/shard_map/ppermute | solution.py:402
  11.2 15.3 %collective-permute-start.3 = (bf16[192,128]{1,0:T(8,128)(2,1)S(1)}, bf16[192,128]{1,0:T(8,128)(2,1)S(1)}, u32[]{:S(2)}, u32[]{:S(2)}) collective-permute-start(bf16[192,128]{1,0:T(8,128)(2,1)S(1)} %get-tuple-element.60), channel_id=1, source_target_pairs={{0,31},{1,0},{2,1},{3,2},{4,3},{5,4},{6,5},{7,6},{8,7},{9,8},{10,9... | collective-permute-start | bytes 147464 | tf_op jit(solution)/shard_map/ppermute | solution.py:402
  20.0 6.2 %slice-start = ((f32[1,192]{1,0:T(1,128)}), f32[1,128]{1,0:T(1,128)S(1)}, s32[]{:S(2)}) async-start(f32[1,192]{1,0:T(1,128)} %param.18), calls=%async_computation.3 | async-start | bytes 1024 | tf_op jit(solution)/shard_map/slice | solution.py:396
  20.0 6.2 %slice-start.1 = ((f32[1,192]{1,0:T(1,128)}), f32[1,64]{1,0:T(1,128)S(1)}, s32[]{:S(2)}) async-start(f32[1,192]{1,0:T(1,128)} %param.18), calls=%async_computation.4 | async-start | bytes 1024 | tf_op jit(solution)/shard_map/slice | solution.py:395
  20.0 6.2 %slice-start.2 = ((f32[1,192]{1,0:T(1,128)}), f32[1,128]{1,0:T(1,128)S(1)}, s32[]{:S(2)}) async-start(f32[1,192]{1,0:T(1,128)} %param.19), calls=%async_computation.5 | async-start | bytes 1024 | tf_op jit(solution)/shard_map/slice | solution.py:396
  20.0 6.2 %slice-start.3 = ((f32[1,192]{1,0:T(1,128)}), f32[1,64]{1,0:T(1,128)S(1)}, s32[]{:S(2)}) async-start(f32[1,192]{1,0:T(1,128)} %param.19), calls=%async_computation.6 | async-start | bytes 1024 | tf_op jit(solution)/shard_map/slice | solution.py:395
  20.0 6.3 %copy-start = (bf16[192,105]{1,0:T(8,128)(2,1)S(1)}, bf16[192,105]{1,0:T(8,128)(2,1)}, u32[]{:S(2)}) copy-start(bf16[192,105]{1,0:T(8,128)(2,1)} %head_ref.1) | copy-start | bytes 120964
  20.0 16.2 %copy-start.1 = (s32[2,128]{1,0:T(2,128)S(1)}, s32[2,128]{1,0:T(2,128)}, u32[]{:S(2)}) copy-start(s32[2,128]{1,0:T(2,128)} %label_ref.1) | copy-start | bytes 3076
  22.0 14.3 %all-to-all-start = ((f32[32,3,128]{2,1,0:T(4,128)}), f32[32,3,128]{2,1,0:T(4,128)S(1)}, u32[]{:S(2)}, u32[]{:S(2)}) async-start(f32[32,3,128]{2,1,0:T(4,128)} %get-tuple-element.34), calls=%async_computation | async-start | bytes 131072 | tf_op jit(solution)/shard_map/all_to_all | solution.py:482
  38.4 18.5 %collective-permute-start.4 = (bf16[5,192,128]{2,1,0:T(8,128)(2,1)S(1)}, bf16[5,192,128]{2,1,0:T(8,128)(2,1)S(1)}, u32[]{:S(2)}, u32[]{:S(2)}) collective-permute-start(bf16[5,192,128]{2,1,0:T(8,128)(2,1)S(1)} %get-tuple-element.40), channel_id=1, source_target_pairs={{0,8},{8,16},{16,24},{24,0},{1,9},{9,17},{17,25},{25,1},{2,10},{10... | collective-permute-start | bytes 737288 | tf_op jit(solution)/shard_map/ppermute | solution.py:402
  39.1 17.9 %collective-permute-start.5 = (bf16[5,192,128]{2,1,0:T(8,128)(2,1)S(1)}, bf16[5,192,128]{2,1,0:T(8,128)(2,1)S(1)}, u32[]{:S(2)}, u32[]{:S(2)}) collective-permute-start(bf16[5,192,128]{2,1,0:T(8,128)(2,1)S(1)} %get-tuple-element.41), channel_id=1, source_target_pairs={{0,16},{8,24},{16,0},{24,8},{1,17},{9,25},{17,1},{25,9},{2,18},{10... | collective-permute-start | bytes 737288 | tf_op jit(solution)/shard_map/ppermute | solution.py:402
  41.0 15.9 %collective-permute-start.6 = (bf16[5,192,128]{2,1,0:T(8,128)(2,1)S(1)}, bf16[5,192,128]{2,1,0:T(8,128)(2,1)S(1)}, u32[]{:S(2)}, u32[]{:S(2)}) collective-permute-start(bf16[5,192,128]{2,1,0:T(8,128)(2,1)S(1)} %get-tuple-element.42), channel_id=1, source_target_pairs={{0,24},{8,0},{16,8},{24,16},{1,25},{9,1},{17,9},{25,17},{2,26},{10... | collective-permute-start | bytes 737288 | tf_op jit(solution)/shard_map/ppermute | solution.py:402
  42.4 14.6 %all-to-all-start.1 = ((f32[32,6,128]{2,1,0:T(8,128)}), f32[32,6,128]{2,1,0:T(8,128)S(1)}, u32[]{:S(2)}, u32[]{:S(2)}) async-start(f32[32,6,128]{2,1,0:T(8,128)} %get-tuple-element.36), calls=%async_computation.1 | async-start | bytes 262144 | tf_op jit(solution)/shard_map/all_to_all | solution.py:511
  46.6 12.5 %collective-permute-start.7 = (bf16[2,192,128]{2,1,0:T(8,128)(2,1)S(1)}, bf16[2,192,128]{2,1,0:T(8,128)(2,1)S(1)}, u32[]{:S(2)}, u32[]{:S(2)}) collective-permute-start(bf16[2,192,128]{2,1,0:T(8,128)(2,1)S(1)} %get-tuple-element.45), channel_id=1, source_target_pairs={{0,1},{1,2},{2,3},{3,4},{4,5},{5,6},{6,7},{7,8},{8,9},{9,10},{10,1... | collective-permute-start | bytes 294920 | tf_op jit(solution)/shard_map/ppermute | solution.py:402
  48.5 10.7 %collective-permute-start.8 = (bf16[2,192,128]{2,1,0:T(8,128)(2,1)S(1)}, bf16[2,192,128]{2,1,0:T(8,128)(2,1)S(1)}, u32[]{:S(2)}, u32[]{:S(2)}) collective-permute-start(bf16[2,192,128]{2,1,0:T(8,128)(2,1)S(1)} %get-tuple-element.46), channel_id=1, source_target_pairs={{0,31},{1,0},{2,1},{3,2},{4,3},{5,4},{6,5},{7,6},{8,7},{9,8},{10,9... | collective-permute-start | bytes 294920 | tf_op jit(solution)/shard_map/ppermute | solution.py:402
  59.2 17.2 %all-to-all-start.2 = ((bf16[8,248,128]{2,1,0:T(8,128)(2,1)}), bf16[8,248,128]{2,1,0:T(8,128)(2,1)S(1)}, u32[]{:S(2)}, u32[]{:S(2)}) async-start(bf16[8,248,128]{2,1,0:T(8,128)(2,1)} %get-tuple-element.57), calls=%async_computation.2 | async-start | bytes 1015808 | tf_op jit(solution)/shard_map/all_to_all | solution.py:546
  66.7 2.2 %collective-permute-start.10 = (bf16[384,128]{1,0:T(8,128)(2,1)S(1)}, bf16[384,128]{1,0:T(8,128)(2,1)S(1)}, u32[]{:S(2)}, u32[]{:S(2)}) collective-permute-start(bf16[384,128]{1,0:T(8,128)(2,1)S(1)} %get-tuple-element.52), channel_id=1, source_target_pairs={{0,224},{32,0},{64,32},{96,64},{128,96},{160,128},{192,160},{224,1... | collective-permute-start | bytes 294920 | tf_op jit(solution)/shard_map/ppermute | solution.py:402
  66.7 5.8 %collective-permute-start.11 = (bf16[384,128]{1,0:T(8,128)(2,1)S(1)}, bf16[384,128]{1,0:T(8,128)(2,1)S(1)}, u32[]{:S(2)}, u32[]{:S(2)}) collective-permute-start(bf16[384,128]{1,0:T(8,128)(2,1)S(1)} %get-tuple-element.53), channel_id=1, source_target_pairs={{0,224},{32,192},{64,160},{96,128},{128,96},{160,64},{192,32},{224... | collective-permute-start | bytes 294920 | tf_op jit(solution)/shard_map/ppermute | solution.py:569
  67.3 5.3 %collective-permute-start.9 = (bf16[384,128]{1,0:T(8,128)(2,1)S(1)}, bf16[384,128]{1,0:T(8,128)(2,1)S(1)}, u32[]{:S(2)}, u32[]{:S(2)}) collective-permute-start(bf16[384,128]{1,0:T(8,128)(2,1)S(1)} %forward_out.1.fwd_out_ref), channel_id=1, source_target_pairs={{0,32},{32,64},{64,96},{96,128},{128,160},{160,192},{192,224},{224... | collective-permute-start | bytes 294920 | tf_op jit(solution)/shard_map/ppermute | solution.py:402

commit v8 on v7

--- a/solution.py
+++ b/solution.py
@@ -161,6 +161,11 @@
 def conv_fwd(own_ref, low_ref, high_ref, wt_ref, z_ref, tile_ref, x_ref):
     mean, squares = convolution(1, own_ref, low_ref, high_ref, wt_ref, z_ref, x_ref)
     tile_ref[...] = packed_tile([jnp.zeros_like(mean), jnp.zeros_like(mean), mean, squares])
+
+
+def fwd_edges(flag_ref, own_ref, z_ref, low_ref, high_ref):
+    low_ref[...] = jnp.where(flag_ref[3] == 1, own_ref[1, 192:], jnp.zeros((192, AREA), BF16))
+    high_ref[...] = jnp.where(flag_ref[2] == 1, own_ref[0, 192:], jnp.zeros((192, AREA), BF16))
 
 
 def rims(share_ref, rim_low_ref, rim_high_ref):
@@ -445,8 +450,6 @@
     upper, lower = slab_id < slabs - 1, slab_id > 0
     low = moved(jnp.where(upper, own[1, :192], nothing), SLABS, 1)
     high = moved(jnp.where(lower, own[0, :192], nothing), SLABS, -1)
-    fwd_low = moved(jnp.where(upper, own[1, 192:], nothing), SLABS, 1)
-    fwd_high = moved(jnp.where(lower, own[0, 192:], nothing), SLABS, -1)
     (turned,) = call(
         turn_weights,
         [((192, 5184), BF16)],
@@ -459,7 +462,7 @@
     )
     z, stats_send = call(
         conv_bwd,
-        [((2, 192, AREA), F32), ((slabs, 3, AREA), F32)],
+        [((2, 192, AREA), F32), ((slabs, 6, AREA), F32)],
         [((5184, 256), BF16)],
         2 * 5184 * 192 * 256,
         5000000,
@@ -468,6 +471,11 @@
         high,
         turned,
     )
+    fwd_low, fwd_high = call(
+        fwd_edges, [((192, AREA), BF16)] * 2, [], 0, 400000, flags, own, z, smem=1
+    )
+    fwd_low = moved(fwd_low, SLABS, 1)
+    fwd_high = moved(fwd_high, SLABS, -1)
     fwd_z, fwd_tile = call(
         conv_fwd,
         [((2, 192, AREA), F32), ((8, AREA), F32)],

time: 77.7 us -> 76.2 us (0.981)
  waiting for transfers between devices: 21.6 us -> 16.1 us
  starting transfers between devices: 36 us -> 40.4 us
  local copies, waits for them, and re-layouts: 1.21 us -> 0.28 us
    all_to_all x1, waiting for transfers between devices: 8.51 us -> 0.4 us  [per_device(): stats = lax.all_to_all(stats_send, SLABS, 0, 0, tiled=True)]
    ppermute x11, waiting for transfers between devices: 1.57 us -> 4.2 us  [moved(): return lax.ppermute(block, axis, route)]
    all_to_all x1, starting transfers between devices: 4.22 us -> 6.46 us  [per_device(): stats = lax.all_to_all(stats_send, SLABS, 0, 0, tiled=True)]
    all_to_all x1, starting transfers between devices: 4.26 us -> 6.35 us  [per_device(): sums = lax.all_to_all(sums_send, SLABS, 0, 0, tiled=True)]
    transpose x1, local copies, waits for them, and re-layouts: 0.97 us -> 0.03 us  [by_plane(): return jnp.swapaxes(block[0], 0, 1)]
    pallas_call x10 -> x11, Pallas kernels: 15.5 us -> 16.1 us  [call(): pl.pallas_call(body, out_shape=shapes, in_specs=specs, out_specs=[VMEM] *...]
  transfers between devices with their start and end apart: 15 -> 15, of which waited for: 5 -> 6; matrix products, arithmetic and copies ran while one was open for 3% -> 2% of each run, Pallas kernels for 16% -> 15%
where the time goes in v8:
time: 76.2 us; the launch traced here: 75.8 us
  starting transfers between devices  40.4 us (53%)
  Pallas kernels  16.1 us (21%)
  waiting for transfers between devices  16.1 us (21%)
  other arithmetic  2.05 us (3%)
  between operations  0.88 us (1%)
    ppermute x11, starting transfers between devices, moved(): return lax.ppermute(block, axis, route)  23.5 us
    pallas_call x11, Pallas kernels, call(): pl.pallas_call(body, out_shape=shapes, in_specs=specs, out_specs=[VMEM] *...  16.1 us
    all_to_all x1, starting transfers between devices, per_device(): stats = lax.all_to_all(stats_send, SLABS, 0, 0, tiled=True)  6.46 us
    all_to_all x1, starting transfers between devices, per_device(): sums = lax.all_to_all(sums_send, SLABS, 0, 0, tiled=True)  6.35 us
    all_to_all x1, waiting for transfers between devices, per_device(): sums = lax.all_to_all(sums_send, SLABS, 0, 0, tiled=True)  4.75 us
    ppermute x11, waiting for transfers between devices, moved(): return lax.ppermute(block, axis, route)  4.2 us
    ppermute x1, waiting for transfers between devices, per_device(): lax.ppermute(outgoing, 'segment', [(i, segments - 1 - i) for i in range(s...  3.63 us
    all_to_all x1, starting transfers between devices, per_device(): summed = lax.all_to_all(parts, 'z', 0, 0, tiled=True)  3.49 us
  transfers between devices with their start and end apart: 15, of which 6 were waited for; matrix products, arithmetic and copies ran while one was open for 2% of the time, Pallas kernels for 15%

profile of v8, /device:TPU:6, one launch (start us, length us, event | category | flops | bytes accessed | tf_op | source)
XLA Modules:
  0.0 75.8 jit_solution(17931636764549840711)
XLA Ops:
  0.6 1.0 %fusion.3 = bf16[2,192,128]{2,1,0:T(8,128)(2,1)S(1)} fusion(bf16[1,192,2,128]{3,2,1,0:T(2,128)(2,1)} %param.14, bf16[1,192,2,128]{3,2,1,0:T(2,128)(2,1)} %param.13, pred[]{:T(512)S(6)} %ge.3), kind=kLoop, calls=%fused_computation.6 | loop fusion | flops 245760 | bytes 294913 | tf_op jit(solution)/shard_map/transpose | solution.py:442
  1.6 2.0 %collective-permute-start = (bf16[192,128]{1,0:T(8,128)(2,1)S(1)}, bf16[192,128]{1,0:T(8,128)(2,1)S(1)}, u32[]{:S(2)}, u32[]{:S(2)}) collective-permute-start(bf16[192,128]{1,0:T(8,128)(2,1)S(1)} %get-tuple-element.65), channel_id=1, source_target_pairs={{0,1},{1,2},{2,3},{3,4},{4,5},{5,6},{6,7},{7,8},{8,9},{9,10},{10,1... | collective-permute-start | bytes 147464 | tf_op jit(solution)/shard_map/ppermute | solution.py:407
  3.6 6.5 %collective-permute-start.1 = (bf16[192,128]{1,0:T(8,128)(2,1)S(1)}, bf16[192,128]{1,0:T(8,128)(2,1)S(1)}, u32[]{:S(2)}, u32[]{:S(2)}) collective-permute-start(bf16[192,128]{1,0:T(8,128)(2,1)S(1)} %get-tuple-element.64), channel_id=1, source_target_pairs={{0,31},{1,0},{2,1},{3,2},{4,3},{5,4},{6,5},{7,6},{8,7},{9,8},{10,9... | collective-permute-start | bytes 147464 | tf_op jit(solution)/shard_map/ppermute | solution.py:407
  10.1 1.0 %fusion.2 = bf16[2,192,128]{2,1,0:T(8,128)(2,1)S(1)} fusion(bf16[1,192,2,128]{3,2,1,0:T(2,128)(2,1)} %param.12, bf16[1,192,2,128]{3,2,1,0:T(2,128)(2,1)} %param.11, pred[]{:T(512)S(6)} %ge.3), kind=kLoop, calls=%fused_computation.5 | loop fusion | flops 245760 | bytes 294913 | tf_op jit(solution)/shard_map/transpose | solution.py:442
  11.1 2.4 %turn_weights.1.wt_ref = bf16[192,5184]{1,0:T(8,128)(2,1)S(1)} custom-call(bf16[192,5184]{1,0:T(8,128)(2,1)} %bitcast.32), custom_call_target="tpu_custom_call" | custom-call | bytes 3981312 | tf_op jit(solution)/shard_map/turn_weights/pallas_call | solution.py:34
  13.6 0.0 copy-start.2
  13.6 0.0 copy-start.3
  13.6 0.0 slice-start
  13.6 0.0 slice-start.1
  13.6 0.0 slice-start.2
  13.6 0.0 slice-start.3
  13.6 0.0 copy-start
  13.7 0.0 collective-permute-done.low_ref
  13.7 0.0 collective-permute-done.1.high_ref
  13.7 1.9 %conv_bwd.1 = (f32[2,192,128]{2,1,0:T(8,128)S(1)}, f32[32,6,128]{2,1,0:T(8,128)}) custom-call(bf16[2,384,128]{2,1,0:T(8,128)(2,1)S(1)} %pad_maximum_fusion.own_ref, bf16[192,128]{1,0:T(8,128)(2,1)S(1)} %collective-permute-done.low_ref, bf16[192,128]{1,0:T(8,128)(2,1)S(1)} %collective-permute-done.1.high_ref, bf16[192,5184]{1,0:T(8,128)(2,1)S(1)} %turn_weights.1.wt_ref), custom_call_target="tpu_custom_call" | custom-call | flops 509607936 | bytes 5000000 | tf_op jit(solution)/shard_map/conv_bwd/pallas_call | solution.py:34
  15.6 0.0 copy-start.1
  15.6 6.5 %all-to-all-start = ((f32[32,6,128]{2,1,0:T(8,128)}), f32[32,6,128]{2,1,0:T(8,128)S(1)}, u32[]{:S(2)}, u32[]{:S(2)}) async-start(f32[32,6,128]{2,1,0:T(8,128)} %get-tuple-element.36), calls=%async_computation | async-start | bytes 262144 | tf_op jit(solution)/shard_map/all_to_all | solution.py:490
  22.0 0.0 copy-done.2
  22.0 0.0 copy-done.3
  22.1 0.1 stack.39.flag_ref
  22.2 0.6 fwd_edges.1
  22.8 1.9 %collective-permute-start.2 = (bf16[192,128]{1,0:T(8,128)(2,1)S(1)}, bf16[192,128]{1,0:T(8,128)(2,1)S(1)}, u32[]{:S(2)}, u32[]{:S(2)}) collective-permute-start(bf16[192,128]{1,0:T(8,128)(2,1)S(1)} %get-tuple-element.37), channel_id=1, source_target_pairs={{0,1},{1,2},{2,3},{3,4},{4,5},{5,6},{6,7},{7,8},{8,9},{9,10},{10,1... | collective-permute-start | bytes 147464 | tf_op jit(solution)/shard_map/ppermute | solution.py:407
  24.6 3.6 %collective-permute-start.3 = (bf16[192,128]{1,0:T(8,128)(2,1)S(1)}, bf16[192,128]{1,0:T(8,128)(2,1)S(1)}, u32[]{:S(2)}, u32[]{:S(2)}) collective-permute-start(bf16[192,128]{1,0:T(8,128)(2,1)S(1)} %get-tuple-element.38), channel_id=1, source_target_pairs={{0,31},{1,0},{2,1},{3,2},{4,3},{5,4},{6,5},{7,6},{8,7},{9,8},{10,9... | collective-permute-start | bytes 147464 | tf_op jit(solution)/shard_map/ppermute | solution.py:407
  28.2 0.0 slice-done
  28.2 0.0 slice-done.1
  28.2 0.0 slice-done.2
  28.2 0.0 slice-done.3
  28.2 0.1 maximum_maximum_fusion.affine_ref
  28.3 0.0 copy-done
  28.3 0.1 copy.25
  28.4 2.6 %collective-permute-done.2.low_ref = bf16[192,128]{1,0:T(8,128)(2,1)S(1)} collective-permute-done((bf16[192,128]{1,0:T(8,128)(2,1)S(1)}, bf16[192,128]{1,0:T(8,128)(2,1)S(1)}, u32[]{:S(2)}, u32[]{:S(2)}) %collective-permute-start.2) | collective-permute-done | bytes 49184 | tf_op jit(solution)/shard_map/ppermute | solution.py:407
  31.0 0.0 collective-permute-done.3.high_ref
  31.0 1.2 %conv_fwd.1 = (f32[2,192,128]{2,1,0:T(8,128)S(1)}, f32[8,128]{1,0:T(8,128)S(1)}) custom-call(bf16[2,384,128]{2,1,0:T(8,128)(2,1)S(1)} %pad_maximum_fusion.own_ref, bf16[192,128]{1,0:T(8,128)(2,1)S(1)} %collective-permute-done.2.low_ref, bf16[192,128]{1,0:T(8,128)(2,1)S(1)} %collective-permute-done.3.high_ref, bf16[192,5184]{1,0:T(8,128)(2,1)S(1)} %turn_weights.1.wt_ref), custom_call_target="tpu_custom_call" | custom-call | flops 509607936 | bytes 5000000 | tf_op jit(solution)/shard_map/conv_fwd/pallas_call | solution.py:34
  32.3 0.4 all-to-all-done.recv_ref
  32.7 0.0 copy-done.1
  32.7 2.2 %head_and_sums.1 = (f32[2,192,128]{2,1,0:T(8,128)S(1)}, bf16[5,192,128]{2,1,0:T(8,128)(2,1)S(1)}, bf16[5,192,128]{2,1,0:T(8,128)(2,1)}, bf16[5,192,128]{2,1,0:T(...) custom-call(s32[5]{0:T(128)S(1)} %stack.39.flag_ref, ...), custom_call_target="tpu_custom_call" | custom-call | flops 41287680 | bytes 4000000 | tf_op jit(solution)/shard_map/head_and_sums/pallas_call | solution.py:34
  34.9 0.6 collective-permute-start.4
  35.5 2.0 %collective-permute-start.5 = (bf16[5,192,128]{2,1,0:T(8,128)(2,1)S(1)}, bf16[5,192,128]{2,1,0:T(8,128)(2,1)S(1)}, u32[]{:S(2)}, u32[]{:S(2)}) collective-permute-start(bf16[5,192,128]{2,1,0:T(8,128)(2,1)S(1)} %get-tuple-element.45), channel_id=1, source_target_pairs={{0,16},{8,24},{16,0},{24,8},{1,17},{9,25},{17,1},{25,9},{2,18},{10... | collective-permute-start | bytes 737288 | tf_op jit(solution)/shard_map/ppermute | solution.py:407
  37.5 1.3 %collective-permute-start.6 = (bf16[5,192,128]{2,1,0:T(8,128)(2,1)S(1)}, bf16[5,192,128]{2,1,0:T(8,128)(2,1)S(1)}, u32[]{:S(2)}, u32[]{:S(2)}) collective-permute-start(bf16[5,192,128]{2,1,0:T(8,128)(2,1)S(1)} %get-tuple-element.46), channel_id=1, source_target_pairs={{0,24},{8,0},{16,8},{24,16},{1,25},{9,1},{17,9},{25,17},{2,26},{10... | collective-permute-start | bytes 737288 | tf_op jit(solution)/shard_map/ppermute | solution.py:407
  38.8 6.4 %all-to-all-start.1 = ((f32[32,6,128]{2,1,0:T(8,128)}), f32[32,6,128]{2,1,0:T(8,128)S(1)}, u32[]{:S(2)}, u32[]{:S(2)}) async-start(f32[32,6,128]{2,1,0:T(8,128)} %get-tuple-element.40), calls=%async_computation.1 | async-start | bytes 262144 | tf_op jit(solution)/shard_map/all_to_all | solution.py:519
  45.2 1.9 %collective-permute-start.7 = (bf16[2,192,128]{2,1,0:T(8,128)(2,1)S(1)}, bf16[2,192,128]{2,1,0:T(8,128)(2,1)S(1)}, u32[]{:S(2)}, u32[]{:S(2)}) collective-permute-start(bf16[2,192,128]{2,1,0:T(8,128)(2,1)S(1)} %get-tuple-element.49), channel_id=1, source_target_pairs={{0,1},{1,2},{2,3},{3,4},{4,5},{5,6},{6,7},{7,8},{8,9},{9,10},{10,1... | collective-permute-start | bytes 294920 | tf_op jit(solution)/shard_map/ppermute | solution.py:407
  47.1 3.7 %collective-permute-start.8 = (bf16[2,192,128]{2,1,0:T(8,128)(2,1)S(1)}, bf16[2,192,128]{2,1,0:T(8,128)(2,1)S(1)}, u32[]{:S(2)}, u32[]{:S(2)}) collective-permute-start(bf16[2,192,128]{2,1,0:T(8,128)(2,1)S(1)} %get-tuple-element.50), channel_id=1, source_target_pairs={{0,31},{1,0},{2,1},{3,2},{4,3},{5,4},{6,5},{7,6},{8,7},{9,8},{10,9... | collective-permute-start | bytes 294920 | tf_op jit(solution)/shard_map/ppermute | solution.py:407
  50.8 4.7 %all-to-all-done.1.recv_ref = f32[32,6,128]{2,1,0:T(8,128)S(1)} async-done(((f32[32,6,128]{2,1,0:T(8,128)}), f32[32,6,128]{2,1,0:T(8,128)S(1)}, u32[]{:S(2)}, u32[]{:S(2)}) %all-to-all-start.1) | async-done | bytes 98336 | tf_op jit(solution)/shard_map/all_to_all | solution.py:519
  55.5 0.0 collective-permute-done.4.a_ref
  55.5 0.0 collective-permute-done.5.b_ref
  55.5 0.0 collective-permute-done.6.c_ref
  55.5 2.2 %kernel_grads.1 = (bf16[8,248,128]{2,1,0:T(8,128)(2,1)}, f32[1,192]{1,0:T(1,128)}, f32[1,192]{1,0:T(1,128)}) custom-call(f32[32,6,128]{2,1,0:T(8,128)S(1)} %all-to-all-done.1.recv_ref, bf16[5,192,128]{2,1,0:T(8,128)(2,1)S(1)} %get-tuple-element.42.own_ref.share_ref, bf16[5,192,128]{2,1,0:T(8,128)(2,1)S(1)} %collective-permute-done.4.a_ref, ...), custom_call_target="tpu_custom_call" | custom-call | bytes 1000 | tf_op jit(solution)/shard_map/kernel_grads/pallas_call | solution.py:34
  57.7 0.0 collective-permute-done.7.low_ref
  57.7 0.0 collective-permute-done.8.high_ref
  57.7 3.5 %all-to-all-start.2 = ((bf16[8,248,128]{2,1,0:T(8,128)(2,1)}), bf16[8,248,128]{2,1,0:T(8,128)(2,1)S(1)}, u32[]{:S(2)}, u32[]{:S(2)}) async-start(bf16[8,248,128]{2,1,0:T(8,128)(2,1)} %get-tuple-element.61), calls=%async_computation.2 | async-start | bytes 1015808 | tf_op jit(solution)/shard_map/all_to_all | solution.py:554
  61.3 0.5 forward_out.1.fwd_out_ref
  61.8 3.5 %input_grads.1 = (bf16[384,128]{1,0:T(8,128)(2,1)S(1)}, bf16[384,128]{1,0:T(8,128)(2,1)S(1)}) custom-call(s32[5]{0:T(128)S(1)} %stack.39.flag_ref, bf16[192,5184]{1,0:T(8,128)(2,1)} %bitcast.33, f32[32,6,128]{2,1,0:T(8,128)S(1)} %all-to-all-done.1.recv_ref, bf16[5,192,128]{2,1,0:T(8,128)(2,1)S(1)} %get-tuple-element.42.own_ref.share_ref, ...), custom_call_target="tpu_custom_call" | custom-call | flops 509607936 | bytes 4000000 | tf_op jit(solution)/shard_map/input_grads/pallas_call | solution.py:34
  65.2 0.0 collective-permute-start.10
  65.3 0.6 collective-permute-start.11
  65.8 0.1 collective-permute-start.9
  65.9 1.6 %collective-permute-done.10.two_ref = bf16[384,128]{1,0:T(8,128)(2,1)S(1)} collective-permute-done((bf16[384,128]{1,0:T(8,128)(2,1)S(1)}, bf16[384,128]{1,0:T(8,128)(2,1)S(1)}, u32[]{:S(2)}, u32[]{:S(2)}) %collective-permute-start.10) | collective-permute-done | bytes 98336 | tf_op jit(solution)/shard_map/ppermute | solution.py:407
  67.5 3.6 %collective-permute-done.11.three_ref = bf16[384,128]{1,0:T(8,128)(2,1)S(1)} collective-permute-done((bf16[384,128]{1,0:T(8,128)(2,1)S(1)}, bf16[384,128]{1,0:T(8,128)(2,1)S(1)}, u32[]{:S(2)}, u32[]{:S(2)}) %collective-permute-start.11) | collective-permute-done | bytes 98336 | tf_op jit(solution)/shard_map/ppermute | solution.py:577
  71.1 0.0 collective-permute-done.9.one_ref
  71.1 0.7 hand_over.1
  71.8 3.1 %all-to-all-done.2.recv_ref = bf16[8,248,128]{2,1,0:T(8,128)(2,1)S(1)} async-done(((bf16[8,248,128]{2,1,0:T(8,128)(2,1)}), bf16[8,248,128]{2,1,0:T(8,128)(2,1)S(1)}, u32[]{:S(2)}, u32[]{:S(2)}) %all-to-all-start.2) | async-done | bytes 507936 | tf_op jit(solution)/shard_map/all_to_all | solution.py:554
  75.0 0.8 %kernel.1 = f32[6,1,5184]{2,1,0:T(1,128)} custom-call(bf16[8,248,128]{2,1,0:T(8,128)(2,1)S(1)} %all-to-all-done.2.recv_ref), custom_call_target="tpu_custom_call" | custom-call | bytes 1000000 | tf_op jit(solution)/shard_map/kernel/pallas_call | solution.py:34
  (4 shorter events, 0.1 us)
Async XLA Ops:
  1.6 12.0 %collective-permute-start = (bf16[192,128]{1,0:T(8,128)(2,1)S(1)}, bf16[192,128]{1,0:T(8,128)(2,1)S(1)}, u32[]{:S(2)}, u32[]{:S(2)}) collective-permute-start(bf16[192,128]{1,0:T(8,128)(2,1)S(1)} %get-tuple-element.65), channel_id=1, source_target_pairs={{0,1},{1,2},{2,3},{3,4},{4,5},{5,6},{6,7},{7,8},{8,9},{9,10},{10,1... | collective-permute-start | bytes 147464 | tf_op jit(solution)/shard_map/ppermute | solution.py:407
  3.6 10.0 %collective-permute-start.1 = (bf16[192,128]{1,0:T(8,128)(2,1)S(1)}, bf16[192,128]{1,0:T(8,128)(2,1)S(1)}, u32[]{:S(2)}, u32[]{:S(2)}) collective-permute-start(bf16[192,128]{1,0:T(8,128)(2,1)S(1)} %get-tuple-element.64), channel_id=1, source_target_pairs={{0,31},{1,0},{2,1},{3,2},{4,3},{5,4},{6,5},{7,6},{8,7},{9,8},{10,9... | collective-permute-start | bytes 147464 | tf_op jit(solution)/shard_map/ppermute | solution.py:407
  13.6 8.5 %copy-start.2 = (bf16[1,192,2,128]{3,2,1,0:T(2,128)(2,1)S(1)}, bf16[1,192,2,128]{3,2,1,0:T(2,128)(2,1)}, u32[]{:S(2)}) copy-start(bf16[1,192,2,128]{3,2,1,0:T(2,128)(2,1)} %param.16) | copy-start | bytes 294916
  13.6 8.5 %copy-start.3 = (bf16[1,192,2,128]{3,2,1,0:T(2,128)(2,1)S(1)}, bf16[1,192,2,128]{3,2,1,0:T(2,128)(2,1)}, u32[]{:S(2)}) copy-start(bf16[1,192,2,128]{3,2,1,0:T(2,128)(2,1)} %param.15) | copy-start | bytes 294916
  13.6 14.6 %slice-start = ((f32[1,192]{1,0:T(1,128)}), f32[1,128]{1,0:T(1,128)S(1)}, s32[]{:S(2)}) async-start(f32[1,192]{1,0:T(1,128)} %param.18), calls=%async_computation.3 | async-start | bytes 1024 | tf_op jit(solution)/shard_map/slice | solution.py:401
  13.6 14.6 %slice-start.1 = ((f32[1,192]{1,0:T(1,128)}), f32[1,64]{1,0:T(1,128)S(1)}, s32[]{:S(2)}) async-start(f32[1,192]{1,0:T(1,128)} %param.18), calls=%async_computation.4 | async-start | bytes 1024 | tf_op jit(solution)/shard_map/slice | solution.py:400
  13.6 14.6 %slice-start.2 = ((f32[1,192]{1,0:T(1,128)}), f32[1,128]{1,0:T(1,128)S(1)}, s32[]{:S(2)}) async-start(f32[1,192]{1,0:T(1,128)} %param.19), calls=%async_computation.5 | async-start | bytes 1024 | tf_op jit(solution)/shard_map/slice | solution.py:401
  13.6 14.6 %slice-start.3 = ((f32[1,192]{1,0:T(1,128)}), f32[1,64]{1,0:T(1,128)S(1)}, s32[]{:S(2)}) async-start(f32[1,192]{1,0:T(1,128)} %param.19), calls=%async_computation.6 | async-start | bytes 1024 | tf_op jit(solution)/shard_map/slice | solution.py:400
  13.6 14.6 %copy-start = (bf16[192,105]{1,0:T(8,128)(2,1)S(1)}, bf16[192,105]{1,0:T(8,128)(2,1)}, u32[]{:S(2)}) copy-start(bf16[192,105]{1,0:T(8,128)(2,1)} %head_ref.1) | copy-start | bytes 120964
  15.6 17.1 %copy-start.1 = (s32[2,128]{1,0:T(2,128)S(1)}, s32[2,128]{1,0:T(2,128)}, u32[]{:S(2)}) copy-start(s32[2,128]{1,0:T(2,128)} %label_ref.1) | copy-start | bytes 3076
  15.6 17.1 %all-to-all-start = ((f32[32,6,128]{2,1,0:T(8,128)}), f32[32,6,128]{2,1,0:T(8,128)S(1)}, u32[]{:S(2)}, u32[]{:S(2)}) async-start(f32[32,6,128]{2,1,0:T(8,128)} %get-tuple-element.36), calls=%async_computation | async-start | bytes 262144 | tf_op jit(solution)/shard_map/all_to_all | solution.py:490
  22.8 8.3 %collective-permute-start.2 = (bf16[192,128]{1,0:T(8,128)(2,1)S(1)}, bf16[192,128]{1,0:T(8,128)(2,1)S(1)}, u32[]{:S(2)}, u32[]{:S(2)}) collective-permute-start(bf16[192,128]{1,0:T(8,128)(2,1)S(1)} %get-tuple-element.37), channel_id=1, source_target_pairs={{0,1},{1,2},{2,3},{3,4},{4,5},{5,6},{6,7},{7,8},{8,9},{9,10},{10,1... | collective-permute-start | bytes 147464 | tf_op jit(solution)/shard_map/ppermute | solution.py:407
  24.6 6.4 %collective-permute-start.3 = (bf16[192,128]{1,0:T(8,128)(2,1)S(1)}, bf16[192,128]{1,0:T(8,128)(2,1)S(1)}, u32[]{:S(2)}, u32[]{:S(2)}) collective-permute-start(bf16[192,128]{1,0:T(8,128)(2,1)S(1)} %get-tuple-element.38), channel_id=1, source_target_pairs={{0,31},{1,0},{2,1},{3,2},{4,3},{5,4},{6,5},{7,6},{8,7},{9,8},{10,9... | collective-permute-start | bytes 147464 | tf_op jit(solution)/shard_map/ppermute | solution.py:407
  34.9 20.7 %collective-permute-start.4 = (bf16[5,192,128]{2,1,0:T(8,128)(2,1)}, bf16[5,192,128]{2,1,0:T(8,128)(2,1)S(1)}, u32[]{:S(2)}, u32[]{:S(2)}) collective-permute-start(bf16[5,192,128]{2,1,0:T(8,128)(2,1)} %get-tuple-element.44), channel_id=1, source_target_pairs={{0,8},{8,16},{16,24},{24,0},{1,9},{9,17},{17,25},{25,1},{2,10},{10... | collective-permute-start | bytes 737288 | tf_op jit(solution)/shard_map/ppermute | solution.py:407
  35.5 20.0 %collective-permute-start.5 = (bf16[5,192,128]{2,1,0:T(8,128)(2,1)S(1)}, bf16[5,192,128]{2,1,0:T(8,128)(2,1)S(1)}, u32[]{:S(2)}, u32[]{:S(2)}) collective-permute-start(bf16[5,192,128]{2,1,0:T(8,128)(2,1)S(1)} %get-tuple-element.45), channel_id=1, source_target_pairs={{0,16},{8,24},{16,0},{24,8},{1,17},{9,25},{17,1},{25,9},{2,18},{10... | collective-permute-start | bytes 737288 | tf_op jit(solution)/shard_map/ppermute | solution.py:407
  37.5 18.0 %collective-permute-start.6 = (bf16[5,192,128]{2,1,0:T(8,128)(2,1)S(1)}, bf16[5,192,128]{2,1,0:T(8,128)(2,1)S(1)}, u32[]{:S(2)}, u32[]{:S(2)}) collective-permute-start(bf16[5,192,128]{2,1,0:T(8,128)(2,1)S(1)} %get-tuple-element.46), channel_id=1, source_target_pairs={{0,24},{8,0},{16,8},{24,16},{1,25},{9,1},{17,9},{25,17},{2,26},{10... | collective-permute-start | bytes 737288 | tf_op jit(solution)/shard_map/ppermute | solution.py:407
  38.8 16.7 %all-to-all-start.1 = ((f32[32,6,128]{2,1,0:T(8,128)}), f32[32,6,128]{2,1,0:T(8,128)S(1)}, u32[]{:S(2)}, u32[]{:S(2)}) async-start(f32[32,6,128]{2,1,0:T(8,128)} %get-tuple-element.40), calls=%async_computation.1 | async-start | bytes 262144 | tf_op jit(solution)/shard_map/all_to_all | solution.py:519
  45.2 12.5 %collective-permute-start.7 = (bf16[2,192,128]{2,1,0:T(8,128)(2,1)S(1)}, bf16[2,192,128]{2,1,0:T(8,128)(2,1)S(1)}, u32[]{:S(2)}, u32[]{:S(2)}) collective-permute-start(bf16[2,192,128]{2,1,0:T(8,128)(2,1)S(1)} %get-tuple-element.49), channel_id=1, source_target_pairs={{0,1},{1,2},{2,3},{3,4},{4,5},{5,6},{6,7},{7,8},{8,9},{9,10},{10,1... | collective-permute-start | bytes 294920 | tf_op jit(solution)/shard_map/ppermute | solution.py:407
  47.1 10.7 %collective-permute-start.8 = (bf16[2,192,128]{2,1,0:T(8,128)(2,1)S(1)}, bf16[2,192,128]{2,1,0:T(8,128)(2,1)S(1)}, u32[]{:S(2)}, u32[]{:S(2)}) collective-permute-start(bf16[2,192,128]{2,1,0:T(8,128)(2,1)S(1)} %get-tuple-element.50), channel_id=1, source_target_pairs={{0,31},{1,0},{2,1},{3,2},{4,3},{5,4},{6,5},{7,6},{8,7},{9,8},{10,9... | collective-permute-start | bytes 294920 | tf_op jit(solution)/shard_map/ppermute | solution.py:407
  57.7 17.2 %all-to-all-start.2 = ((bf16[8,248,128]{2,1,0:T(8,128)(2,1)}), bf16[8,248,128]{2,1,0:T(8,128)(2,1)S(1)}, u32[]{:S(2)}, u32[]{:S(2)}) async-start(bf16[8,248,128]{2,1,0:T(8,128)(2,1)} %get-tuple-element.61), calls=%async_computation.2 | async-start | bytes 1015808 | tf_op jit(solution)/shard_map/all_to_all | solution.py:554
  65.2 2.2 %collective-permute-start.10 = (bf16[384,128]{1,0:T(8,128)(2,1)S(1)}, bf16[384,128]{1,0:T(8,128)(2,1)S(1)}, u32[]{:S(2)}, u32[]{:S(2)}) collective-permute-start(bf16[384,128]{1,0:T(8,128)(2,1)S(1)} %get-tuple-element.56), channel_id=1, source_target_pairs={{0,224},{32,0},{64,32},{96,64},{128,96},{160,128},{192,160},{224,1... | collective-permute-start | bytes 294920 | tf_op jit(solution)/shard_map/ppermute | solution.py:407
  65.3 5.8 %collective-permute-start.11 = (bf16[384,128]{1,0:T(8,128)(2,1)S(1)}, bf16[384,128]{1,0:T(8,128)(2,1)S(1)}, u32[]{:S(2)}, u32[]{:S(2)}) collective-permute-start(bf16[384,128]{1,0:T(8,128)(2,1)S(1)} %get-tuple-element.57), channel_id=1, source_target_pairs={{0,224},{32,192},{64,160},{96,128},{128,96},{160,64},{192,32},{224... | collective-permute-start | bytes 294920 | tf_op jit(solution)/shard_map/ppermute | solution.py:577
  65.8 5.3 %collective-permute-start.9 = (bf16[384,128]{1,0:T(8,128)(2,1)S(1)}, bf16[384,128]{1,0:T(8,128)(2,1)S(1)}, u32[]{:S(2)}, u32[]{:S(2)}) collective-permute-start(bf16[384,128]{1,0:T(8,128)(2,1)S(1)} %forward_out.1.fwd_out_ref), channel_id=1, source_target_pairs={{0,32},{32,64},{64,96},{96,128},{128,160},{160,192},{192,224},{224... | collective-permute-start | bytes 294920 | tf_op jit(solution)/shard_map/ppermute | solution.py:407

commit v9 on v6

--- a/solution.py
+++ b/solution.py
@@ -542,7 +542,6 @@
         hbm=1,
         limit=52,
     )
-    fwd_out, grad_joined, outgoing = lax.optimization_barrier((fwd_out, grad_joined, outgoing))
     prev_block = moved(grad_joined, "segment", -1)
     next_block = moved(fwd_out, "segment", 1)
     mirrored = lax.ppermute(outgoing, "segment", [(i, segments - 1 - i) for i in range(segments)])

time: 74.5 us -> 74.5 us (level)
  no operation moved by 1% of the time
where the time goes in v9:
time: 74.5 us; the launch traced here: 74.1 us
  starting transfers between devices  34.5 us (46%)
  waiting for transfers between devices  22.2 us (30%)
  Pallas kernels  15.1 us (20%)
  other arithmetic  1.23 us (2%)
  between operations  0.84 us (1%)
    ppermute x9, starting transfers between devices, moved(): return lax.ppermute(block, axis, route)  19.6 us
    pallas_call x8, Pallas kernels, call(): pl.pallas_call(body, out_shape=shapes, in_specs=specs, out_specs=[VMEM] *...  15.1 us
    all_to_all x1, waiting for transfers between devices, per_device(): stats = lax.all_to_all(stats_send, SLABS, 0, 0, tiled=True)  10.3 us
    all_to_all x1, starting transfers between devices, per_device(): stats = lax.all_to_all(stats_send, SLABS, 0, 0, tiled=True)  6.7 us
    all_to_all x1, starting transfers between devices, per_device(): sums = lax.all_to_all(sums_send, SLABS, 0, 0, tiled=True)  4.6 us
    all_to_all x1, waiting for transfers between devices, per_device(): sums = lax.all_to_all(sums_send, SLABS, 0, 0, tiled=True)  4.13 us
    ppermute x1, waiting for transfers between devices, per_device(): lax.ppermute(outgoing, 'segment', [(i, segments - 1 - i) for i in range(s...  4.08 us
    all_to_all x1, starting transfers between devices, per_device(): summed = lax.all_to_all(parts, 'z', 0, 0, tiled=True)  3.49 us
  transfers between devices with their start and end apart: 13, of which 5 were waited for; matrix products, arithmetic and copies ran while one was open for 0% of the time, Pallas kernels for 13%

profile of v9, /device:TPU:6, one launch (start us, length us, event | category | flops | bytes accessed | tf_op | source)
XLA Modules:
  0.0 74.1 jit_solution(8860615323898362923)
XLA Ops:
  0.6 1.1 %fusion.2 = (bf16[2,192,128]{2,1,0:T(8,128)(2,1)S(1)}, bf16[2,192,128]{2,1,0:T(8,128)(2,1)S(1)}) fusion(bf16[1,192,2,128]{3,2,1,0:T(2,128)(2,1)} %param.12, bf16[1,192,2,128]{3,2,1,0:T(2,128)(2,1)} %param.11, pred[]{:T(512)S(6)} %ge.3, bf16[1,192,2,128]{3,2,1,0:T(2,128)(2,1)} %param.14, bf16[1,192,2,128]{3,2,1,0:T(2,128)(2,1)} %param.13), kind=kLoop, calls=%fused_computation.9 | loop fusion | flops 491520 | bytes 589825 | tf_op jit(solution)/shard_map/transpose | solution.py:430
  1.8 2.0 %collective-permute-start = (bf16[384,128]{1,0:T(8,128)(2,1)S(1)}, bf16[384,128]{1,0:T(8,128)(2,1)S(1)}, u32[]{:S(2)}, u32[]{:S(2)}) collective-permute-start(bf16[384,128]{1,0:T(8,128)(2,1)S(1)} %get-tuple-element.57), channel_id=1, source_target_pairs={{0,1},{1,2},{2,3},{3,4},{4,5},{5,6},{6,7},{7,8},{8,9},{9,10},{10,1... | collective-permute-start | bytes 294920 | tf_op jit(solution)/shard_map/ppermute | solution.py:395
  3.8 6.5 %collective-permute-start.1 = (bf16[384,128]{1,0:T(8,128)(2,1)S(1)}, bf16[384,128]{1,0:T(8,128)(2,1)S(1)}, u32[]{:S(2)}, u32[]{:S(2)}) collective-permute-start(bf16[384,128]{1,0:T(8,128)(2,1)S(1)} %get-tuple-element.56), channel_id=1, source_target_pairs={{0,31},{1,0},{2,1},{3,2},{4,3},{5,4},{6,5},{7,6},{8,7},{9,8},{10,9... | collective-permute-start | bytes 294920 | tf_op jit(solution)/shard_map/ppermute | solution.py:395
  10.3 0.0 copy-start
  10.3 0.0 slice-start
  10.3 0.0 slice-start.1
  10.3 0.0 slice-start.2
  10.3 0.0 slice-start.3
  10.4 2.5 %turn_weights.1.wt_ref = bf16[192,5184]{1,0:T(8,128)(2,1)S(1)} custom-call(bf16[192,5184]{1,0:T(8,128)(2,1)} %bitcast.32), custom_call_target="tpu_custom_call" | custom-call | bytes 3981312 | tf_op jit(solution)/shard_map/turn_weights/pallas_call | solution.py:34
  12.8 0.0 copy-done
  12.8 0.1 copy.25
  13.0 0.1 stack.39.flag_ref
  13.0 0.0 slice-done
  13.1 0.0 slice-done.1
  13.1 0.0 slice-done.2
  13.1 0.0 slice-done.3
  13.1 0.1 maximum_maximum_fusion.affine_ref
  13.2 0.0 copy-start.2
  13.2 0.0 copy-start.3
  13.2 0.0 copy-start.1
  13.2 0.0 collective-permute-done.low_ref
  13.2 0.0 collective-permute-done.1.high_ref
  13.2 2.7 %conv_both.1 = (f32[4,192,128]{2,1,0:T(8,128)S(1)}, f32[32,6,128]{2,1,0:T(8,128)}) custom-call(bf16[2,384,128]{2,1,0:T(8,128)(2,1)S(1)} %pad_maximum_fusion.own_ref, bf16[384,128]{1,0:T(8,128)(2,1)S(1)} %collective-permute-done.low_ref, bf16[384,128]{1,0:T(8,128)(2,1)S(1)} %collective-permute-done.1.high_ref, bf16[192,5184]{1,0:T(8,128)(2,1)S(1)} %turn_weights.1.wt_ref), custom_call_target="tpu_custom_call" | custom-call | flops 1019215872 | bytes 5000000 | tf_op jit(solution)/shard_map/conv_both/pallas_call | solution.py:34
  15.9 6.7 %all-to-all-start = ((f32[32,6,128]{2,1,0:T(8,128)}), f32[32,6,128]{2,1,0:T(8,128)S(1)}, u32[]{:S(2)}, u32[]{:S(2)}) async-start(f32[32,6,128]{2,1,0:T(8,128)} %get-tuple-element.32), calls=%async_computation | async-start | bytes 262144 | tf_op jit(solution)/shard_map/all_to_all | solution.py:461
  22.6 0.0 copy-done.2
  22.6 0.0 copy-done.3
  22.7 10.3 %all-to-all-done.recv_ref = f32[32,6,128]{2,1,0:T(8,128)S(1)} async-done(((f32[32,6,128]{2,1,0:T(8,128)}), f32[32,6,128]{2,1,0:T(8,128)S(1)}, u32[]{:S(2)}, u32[]{:S(2)}) %all-to-all-start) | async-done | bytes 98336 | tf_op jit(solution)/shard_map/all_to_all | solution.py:461
  33.0 0.0 copy-done.1
  33.0 2.2 %head_and_sums.1 = (f32[2,192,128]{2,1,0:T(8,128)S(1)}, bf16[5,192,128]{2,1,0:T(8,128)(2,1)S(1)}, bf16[5,192,128]{2,1,0:T(8,128)(2,1)}, bf16[5,192,128]{2,1,0:T(...) custom-call(s32[5]{0:T(128)S(1)} %stack.39.flag_ref, ...), custom_call_target="tpu_custom_call" | custom-call | flops 41287680 | bytes 4000000 | tf_op jit(solution)/shard_map/head_and_sums/pallas_call | solution.py:34
  35.1 0.6 collective-permute-start.3
  35.8 2.0 %collective-permute-start.4 = (bf16[5,192,128]{2,1,0:T(8,128)(2,1)S(1)}, bf16[5,192,128]{2,1,0:T(8,128)(2,1)S(1)}, u32[]{:S(2)}, u32[]{:S(2)}) collective-permute-start(bf16[5,192,128]{2,1,0:T(8,128)(2,1)S(1)} %get-tuple-element.40), channel_id=1, source_target_pairs={{0,16},{8,24},{16,0},{24,8},{1,17},{9,25},{17,1},{25,9},{2,18},{10... | collective-permute-start | bytes 737288 | tf_op jit(solution)/shard_map/ppermute | solution.py:395
  37.8 1.4 %collective-permute-start.5 = (bf16[5,192,128]{2,1,0:T(8,128)(2,1)S(1)}, bf16[5,192,128]{2,1,0:T(8,128)(2,1)S(1)}, u32[]{:S(2)}, u32[]{:S(2)}) collective-permute-start(bf16[5,192,128]{2,1,0:T(8,128)(2,1)S(1)} %get-tuple-element.41), channel_id=1, source_target_pairs={{0,24},{8,0},{16,8},{24,16},{1,25},{9,1},{17,9},{25,17},{2,26},{10... | collective-permute-start | bytes 737288 | tf_op jit(solution)/shard_map/ppermute | solution.py:395
  39.1 4.6 %all-to-all-start.1 = ((f32[32,4,128]{2,1,0:T(4,128)}), f32[32,4,128]{2,1,0:T(4,128)S(1)}, u32[]{:S(2)}, u32[]{:S(2)}) async-start(f32[32,4,128]{2,1,0:T(4,128)} %get-tuple-element.33), calls=%async_computation.1 | async-start | bytes 131072 | tf_op jit(solution)/shard_map/all_to_all | solution.py:489
  43.7 0.5 forward_out.1
  44.3 1.9 %collective-permute-start.6 = (bf16[2,192,128]{2,1,0:T(8,128)(2,1)S(1)}, bf16[2,192,128]{2,1,0:T(8,128)(2,1)S(1)}, u32[]{:S(2)}, u32[]{:S(2)}) collective-permute-start(bf16[2,192,128]{2,1,0:T(8,128)(2,1)S(1)} %get-tuple-element.44), channel_id=1, source_target_pairs={{0,1},{1,2},{2,3},{3,4},{4,5},{5,6},{6,7},{7,8},{8,9},{9,10},{10,1... | collective-permute-start | bytes 294920 | tf_op jit(solution)/shard_map/ppermute | solution.py:395
  46.1 3.6 %collective-permute-start.7 = (bf16[2,192,128]{2,1,0:T(8,128)(2,1)S(1)}, bf16[2,192,128]{2,1,0:T(8,128)(2,1)S(1)}, u32[]{:S(2)}, u32[]{:S(2)}) collective-permute-start(bf16[2,192,128]{2,1,0:T(8,128)(2,1)S(1)} %get-tuple-element.45), channel_id=1, source_target_pairs={{0,31},{1,0},{2,1},{3,2},{4,3},{5,4},{6,5},{7,6},{8,7},{9,8},{10,9... | collective-permute-start | bytes 294920 | tf_op jit(solution)/shard_map/ppermute | solution.py:395
  49.7 4.1 %all-to-all-done.1.recv_ref = f32[32,4,128]{2,1,0:T(4,128)S(1)} async-done(((f32[32,4,128]{2,1,0:T(4,128)}), f32[32,4,128]{2,1,0:T(4,128)S(1)}, u32[]{:S(2)}, u32[]{:S(2)}) %all-to-all-start.1) | async-done | bytes 65568 | tf_op jit(solution)/shard_map/all_to_all | solution.py:489
  53.8 0.0 collective-permute-done.3.a_ref
  53.8 0.0 collective-permute-done.4.b_ref
  53.8 0.0 collective-permute-done.5.c_ref
  53.8 2.2 %kernel_grads.1 = (bf16[8,248,128]{2,1,0:T(8,128)(2,1)}, f32[1,192]{1,0:T(1,128)}, f32[1,192]{1,0:T(1,128)}) custom-call(f32[32,4,128]{2,1,0:T(4,128)S(1)} %all-to-all-done.1.recv_ref, bf16[5,192,128]{2,1,0:T(8,128)(2,1)S(1)} %get-tuple-element.34.share_ref.own_ref, bf16[5,192,128]{2,1,0:T(8,128)(2,1)S(1)} %collective-permute-done.3.a_ref, ...), custom_call_target="tpu_custom_call" | custom-call | bytes 1000 | tf_op jit(solution)/shard_map/kernel_grads/pallas_call | solution.py:34
  56.0 0.0 collective-permute-done.6.low_ref
  56.0 0.0 collective-permute-done.7.high_ref
  56.0 3.5 %all-to-all-start.2 = ((bf16[8,248,128]{2,1,0:T(8,128)(2,1)}), bf16[8,248,128]{2,1,0:T(8,128)(2,1)S(1)}, u32[]{:S(2)}, u32[]{:S(2)}) async-start(bf16[8,248,128]{2,1,0:T(8,128)(2,1)} %get-tuple-element.53), calls=%async_computation.2 | async-start | bytes 1015808 | tf_op jit(solution)/shard_map/all_to_all | solution.py:525
  59.5 0.0 collective-permute-start.2
  59.6 3.5 %input_grads.1 = (bf16[384,128]{1,0:T(8,128)(2,1)S(1)}, bf16[384,128]{1,0:T(8,128)(2,1)S(1)}) custom-call(s32[5]{0:T(128)S(1)} %stack.39.flag_ref, bf16[192,5184]{1,0:T(8,128)(2,1)} %bitcast.33, f32[32,4,128]{2,1,0:T(4,128)S(1)} %all-to-all-done.1.recv_ref, bf16[5,192,128]{2,1,0:T(8,128)(2,1)S(1)} %get-tuple-element.34.share_ref.own_ref, ...), custom_call_target="tpu_custom_call" | custom-call | flops 509607936 | bytes 4000000 | tf_op jit(solution)/shard_map/input_grads/pallas_call | solution.py:34
  63.0 1.7 %collective-permute-start.8 = (bf16[384,128]{1,0:T(8,128)(2,1)S(1)}, bf16[384,128]{1,0:T(8,128)(2,1)S(1)}, u32[]{:S(2)}, u32[]{:S(2)}) collective-permute-start(bf16[384,128]{1,0:T(8,128)(2,1)S(1)} %get-tuple-element.48), channel_id=1, source_target_pairs={{0,224},{32,0},{64,32},{96,64},{128,96},{160,128},{192,160},{224,1... | collective-permute-start | bytes 294920 | tf_op jit(solution)/shard_map/ppermute | solution.py:395
  64.8 0.0 collective-permute-start.9
  64.8 0.0 collective-permute-done.2.one_ref
  64.8 2.2 %collective-permute-done.8.two_ref = bf16[384,128]{1,0:T(8,128)(2,1)S(1)} collective-permute-done((bf16[384,128]{1,0:T(8,128)(2,1)S(1)}, bf16[384,128]{1,0:T(8,128)(2,1)S(1)}, u32[]{:S(2)}, u32[]{:S(2)}) %collective-permute-start.8) | collective-permute-done | bytes 98336 | tf_op jit(solution)/shard_map/ppermute | solution.py:395
  67.0 4.1 %collective-permute-done.9.three_ref = bf16[384,128]{1,0:T(8,128)(2,1)S(1)} collective-permute-done((bf16[384,128]{1,0:T(8,128)(2,1)S(1)}, bf16[384,128]{1,0:T(8,128)(2,1)S(1)}, u32[]{:S(2)}, u32[]{:S(2)}) %collective-permute-start.9) | collective-permute-done | bytes 98336 | tf_op jit(solution)/shard_map/ppermute | solution.py:547
  71.1 0.7 hand_over.1
  71.8 1.5 %all-to-all-done.2.recv_ref = bf16[8,248,128]{2,1,0:T(8,128)(2,1)S(1)} async-done(((bf16[8,248,128]{2,1,0:T(8,128)(2,1)}), bf16[8,248,128]{2,1,0:T(8,128)(2,1)S(1)}, u32[]{:S(2)}, u32[]{:S(2)}) %all-to-all-start.2) | async-done | bytes 507936 | tf_op jit(solution)/shard_map/all_to_all | solution.py:525
  73.2 0.8 %kernel.1 = f32[6,1,5184]{2,1,0:T(1,128)} custom-call(bf16[8,248,128]{2,1,0:T(8,128)(2,1)S(1)} %all-to-all-done.2.recv_ref), custom_call_target="tpu_custom_call" | custom-call | bytes 1000000 | tf_op jit(solution)/shard_map/kernel/pallas_call | solution.py:34
  (3 shorter events, 0.1 us)
Async XLA Ops:
  1.8 11.4 %collective-permute-start = (bf16[384,128]{1,0:T(8,128)(2,1)S(1)}, bf16[384,128]{1,0:T(8,128)(2,1)S(1)}, u32[]{:S(2)}, u32[]{:S(2)}) collective-permute-start(bf16[384,128]{1,0:T(8,128)(2,1)S(1)} %get-tuple-element.57), channel_id=1, source_target_pairs={{0,1},{1,2},{2,3},{3,4},{4,5},{5,6},{6,7},{7,8},{8,9},{9,10},{10,1... | collective-permute-start | bytes 294920 | tf_op jit(solution)/shard_map/ppermute | solution.py:395
  3.8 9.4 %collective-permute-start.1 = (bf16[384,128]{1,0:T(8,128)(2,1)S(1)}, bf16[384,128]{1,0:T(8,128)(2,1)S(1)}, u32[]{:S(2)}, u32[]{:S(2)}) collective-permute-start(bf16[384,128]{1,0:T(8,128)(2,1)S(1)} %get-tuple-element.56), channel_id=1, source_target_pairs={{0,31},{1,0},{2,1},{3,2},{4,3},{5,4},{6,5},{7,6},{8,7},{9,8},{10,9... | collective-permute-start | bytes 294920 | tf_op jit(solution)/shard_map/ppermute | solution.py:395
  10.3 2.5 %copy-start = (bf16[192,105]{1,0:T(8,128)(2,1)S(1)}, bf16[192,105]{1,0:T(8,128)(2,1)}, u32[]{:S(2)}) copy-start(bf16[192,105]{1,0:T(8,128)(2,1)} %head_ref.1) | copy-start | bytes 120964
  10.3 2.7 %slice-start = ((f32[1,192]{1,0:T(1,128)}), f32[1,64]{1,0:T(1,128)S(1)}, s32[]{:S(2)}) async-start(f32[1,192]{1,0:T(1,128)} %param.19), calls=%async_computation.3 | async-start | bytes 1024 | tf_op jit(solution)/shard_map/slice | solution.py:388
  10.3 2.7 %slice-start.1 = ((f32[1,192]{1,0:T(1,128)}), f32[1,128]{1,0:T(1,128)S(1)}, s32[]{:S(2)}) async-start(f32[1,192]{1,0:T(1,128)} %param.19), calls=%async_computation.4 | async-start | bytes 1024 | tf_op jit(solution)/shard_map/slice | solution.py:389
  10.3 2.7 %slice-start.2 = ((f32[1,192]{1,0:T(1,128)}), f32[1,64]{1,0:T(1,128)S(1)}, s32[]{:S(2)}) async-start(f32[1,192]{1,0:T(1,128)} %param.18), calls=%async_computation.5 | async-start | bytes 1024 | tf_op jit(solution)/shard_map/slice | solution.py:388
  10.3 2.7 %slice-start.3 = ((f32[1,192]{1,0:T(1,128)}), f32[1,128]{1,0:T(1,128)S(1)}, s32[]{:S(2)}) async-start(f32[1,192]{1,0:T(1,128)} %param.18), calls=%async_computation.6 | async-start | bytes 1024 | tf_op jit(solution)/shard_map/slice | solution.py:389
  13.2 9.5 %copy-start.2 = (bf16[1,192,2,128]{3,2,1,0:T(2,128)(2,1)S(1)}, bf16[1,192,2,128]{3,2,1,0:T(2,128)(2,1)}, u32[]{:S(2)}) copy-start(bf16[1,192,2,128]{3,2,1,0:T(2,128)(2,1)} %param.16) | copy-start | bytes 294916
  13.2 9.5 %copy-start.3 = (bf16[1,192,2,128]{3,2,1,0:T(2,128)(2,1)S(1)}, bf16[1,192,2,128]{3,2,1,0:T(2,128)(2,1)}, u32[]{:S(2)}) copy-start(bf16[1,192,2,128]{3,2,1,0:T(2,128)(2,1)} %param.15) | copy-start | bytes 294916
  13.2 19.8 %copy-start.1 = (s32[2,128]{1,0:T(2,128)S(1)}, s32[2,128]{1,0:T(2,128)}, u32[]{:S(2)}) copy-start(s32[2,128]{1,0:T(2,128)} %label_ref.1) | copy-start | bytes 3076
  15.9 17.1 %all-to-all-start = ((f32[32,6,128]{2,1,0:T(8,128)}), f32[32,6,128]{2,1,0:T(8,128)S(1)}, u32[]{:S(2)}, u32[]{:S(2)}) async-start(f32[32,6,128]{2,1,0:T(8,128)} %get-tuple-element.32), calls=%async_computation | async-start | bytes 262144 | tf_op jit(solution)/shard_map/all_to_all | solution.py:461
  35.1 18.7 %collective-permute-start.3 = (bf16[5,192,128]{2,1,0:T(8,128)(2,1)}, bf16[5,192,128]{2,1,0:T(8,128)(2,1)S(1)}, u32[]{:S(2)}, u32[]{:S(2)}) collective-permute-start(bf16[5,192,128]{2,1,0:T(8,128)(2,1)} %get-tuple-element.39), channel_id=1, source_target_pairs={{0,8},{8,16},{16,24},{24,0},{1,9},{9,17},{17,25},{25,1},{2,10},{10... | collective-permute-start | bytes 737288 | tf_op jit(solution)/shard_map/ppermute | solution.py:395
  35.8 18.1 %collective-permute-start.4 = (bf16[5,192,128]{2,1,0:T(8,128)(2,1)S(1)}, bf16[5,192,128]{2,1,0:T(8,128)(2,1)S(1)}, u32[]{:S(2)}, u32[]{:S(2)}) collective-permute-start(bf16[5,192,128]{2,1,0:T(8,128)(2,1)S(1)} %get-tuple-element.40), channel_id=1, source_target_pairs={{0,16},{8,24},{16,0},{24,8},{1,17},{9,25},{17,1},{25,9},{2,18},{10... | collective-permute-start | bytes 737288 | tf_op jit(solution)/shard_map/ppermute | solution.py:395
  37.8 16.1 %collective-permute-start.5 = (bf16[5,192,128]{2,1,0:T(8,128)(2,1)S(1)}, bf16[5,192,128]{2,1,0:T(8,128)(2,1)S(1)}, u32[]{:S(2)}, u32[]{:S(2)}) collective-permute-start(bf16[5,192,128]{2,1,0:T(8,128)(2,1)S(1)} %get-tuple-element.41), channel_id=1, source_target_pairs={{0,24},{8,0},{16,8},{24,16},{1,25},{9,1},{17,9},{25,17},{2,26},{10... | collective-permute-start | bytes 737288 | tf_op jit(solution)/shard_map/ppermute | solution.py:395
  39.1 14.7 %all-to-all-start.1 = ((f32[32,4,128]{2,1,0:T(4,128)}), f32[32,4,128]{2,1,0:T(4,128)S(1)}, u32[]{:S(2)}, u32[]{:S(2)}) async-start(f32[32,4,128]{2,1,0:T(4,128)} %get-tuple-element.33), calls=%async_computation.1 | async-start | bytes 131072 | tf_op jit(solution)/shard_map/all_to_all | solution.py:489
  44.3 11.8 %collective-permute-start.6 = (bf16[2,192,128]{2,1,0:T(8,128)(2,1)S(1)}, bf16[2,192,128]{2,1,0:T(8,128)(2,1)S(1)}, u32[]{:S(2)}, u32[]{:S(2)}) collective-permute-start(bf16[2,192,128]{2,1,0:T(8,128)(2,1)S(1)} %get-tuple-element.44), channel_id=1, source_target_pairs={{0,1},{1,2},{2,3},{3,4},{4,5},{5,6},{6,7},{7,8},{8,9},{9,10},{10,1... | collective-permute-start | bytes 294920 | tf_op jit(solution)/shard_map/ppermute | solution.py:395
  46.1 9.9 %collective-permute-start.7 = (bf16[2,192,128]{2,1,0:T(8,128)(2,1)S(1)}, bf16[2,192,128]{2,1,0:T(8,128)(2,1)S(1)}, u32[]{:S(2)}, u32[]{:S(2)}) collective-permute-start(bf16[2,192,128]{2,1,0:T(8,128)(2,1)S(1)} %get-tuple-element.45), channel_id=1, source_target_pairs={{0,31},{1,0},{2,1},{3,2},{4,3},{5,4},{6,5},{7,6},{8,7},{9,8},{10,9... | collective-permute-start | bytes 294920 | tf_op jit(solution)/shard_map/ppermute | solution.py:395
  56.0 17.2 %all-to-all-start.2 = ((bf16[8,248,128]{2,1,0:T(8,128)(2,1)}), bf16[8,248,128]{2,1,0:T(8,128)(2,1)S(1)}, u32[]{:S(2)}, u32[]{:S(2)}) async-start(bf16[8,248,128]{2,1,0:T(8,128)(2,1)} %get-tuple-element.53), calls=%async_computation.2 | async-start | bytes 1015808 | tf_op jit(solution)/shard_map/all_to_all | solution.py:525
  59.5 5.3 %collective-permute-start.2 = (bf16[384,128]{1,0:T(8,128)(2,1)S(1)}, bf16[384,128]{1,0:T(8,128)(2,1)S(1)}, u32[]{:S(2)}, u32[]{:S(2)}) collective-permute-start(bf16[384,128]{1,0:T(8,128)(2,1)S(1)} %get-tuple-element.36.fwd_out_ref), channel_id=1, source_target_pairs={{0,32},{32,64},{64,96},{96,128},{128,160},{160,192},{192,224},{224... | collective-permute-start | bytes 294920 | tf_op jit(solution)/shard_map/ppermute | solution.py:395
  63.0 4.0 %collective-permute-start.8 = (bf16[384,128]{1,0:T(8,128)(2,1)S(1)}, bf16[384,128]{1,0:T(8,128)(2,1)S(1)}, u32[]{:S(2)}, u32[]{:S(2)}) collective-permute-start(bf16[384,128]{1,0:T(8,128)(2,1)S(1)} %get-tuple-element.48), channel_id=1, source_target_pairs={{0,224},{32,0},{64,32},{96,64},{128,96},{160,128},{192,160},{224,1... | collective-permute-start | bytes 294920 | tf_op jit(solution)/shard_map/ppermute | solution.py:395
  64.8 6.3 %collective-permute-start.9 = (bf16[384,128]{1,0:T(8,128)(2,1)S(1)}, bf16[384,128]{1,0:T(8,128)(2,1)S(1)}, u32[]{:S(2)}, u32[]{:S(2)}) collective-permute-start(bf16[384,128]{1,0:T(8,128)(2,1)S(1)} %get-tuple-element.49), channel_id=1, source_target_pairs={{0,224},{32,192},{64,160},{96,128},{128,96},{160,64},{192,32},{224... | collective-permute-start | bytes 294920 | tf_op jit(solution)/shard_map/ppermute | solution.py:547
